TPU v7x, 32 devices: a whole 2x2x4 slice. The times are simulated.
32 devices in a mesh: parts: 1, replica: 32 (over z, y, x, core).
Axes of the slice: x: 2, y: 2, z: 4, core: 2. Of those that a mesh axis runs over, the one named last changes fastest.
Arguments:
- attention_output: bfloat16 [152, 8192], P('parts', 'replica'), may hold values from -6 to 6
- output_weight: bfloat16 [8192, 8192], P('replica'), may hold values from -0.0625 to 0.0625
- down_weight: bfloat16 [128, 8192, 64], P(('parts', 'replica')), may hold values from -0.0625 to 0.0625
- up_weight: bfloat16 [128, 8192, 64], P(('parts', 'replica')), may hold values from -0.75 to 0.75
- store_adapter_ids: int32 [128], P('parts'), may hold values from 0 to 127, as said below
- segment_adapter: int32 [8], P('parts'), may hold values from 0 to 127, as said below
- segment_rows: int32 [8], P('parts'), may hold values from 1 to 32, 128 in all
Outputs:
- mixed: bfloat16 [152, 8192], P('parts', 'replica')
Inputs may be any that keep to these rules, and one draw needn't show every extreme that they name: `store_adapter_ids`: a permutation; device r of the replica axis holds store slots r * 4 to r * 4 + 3. `segment_adapter`: 8 different adapters; at most 2 of them lie in one device's store slots, and some device's store holds exactly 2 of them. `segment_rows`: the counts sum to 128.
All inputs are finite; a program needn't handle non-finite values.
Results may differ from a plain program's by a relative error of at most 0.0046.
Values may be sent and summed in bfloat16 or wider, within the bound.
No kernel may reach another device: no remote copies, remote signals or barrier semaphores. Data moves between devices by JAX's collectives and lax.ppermute only.
A program may use at most 128 MiB of HBM per device.

v0:
```python
import jax
import jax.numpy as jnp
from jax import lax
from jax.sharding import PartitionSpec as P

BLOCK = 4


ADAPTER_SCALE = 2.0


def segment_member(segment_rows, total_rows, block_rows):
    padded = (segment_rows + block_rows - 1) // block_rows * block_rows
    starts = jnp.cumsum(padded) - padded
    row_ids = jnp.arange(total_rows, dtype=jnp.int32)
    inside = (row_ids[:, None] >= starts[None, :]) & (
        row_ids[:, None] < (starts + segment_rows)[None, :]
    )
    return inside.astype(jnp.float32)


def slot_lookup(store_adapter_ids, segment_adapter):
    positions = jnp.arange(store_adapter_ids.shape[0], dtype=jnp.int32)
    equal = store_adapter_ids[None, :] == segment_adapter[:, None]
    return jnp.sum(jnp.where(equal, positions[None, :], 0), axis=1)


def per_device(
    attention_output,
    output_weight,
    down_weight,
    up_weight,
    store_adapter_ids,
    segment_adapter,
    segment_rows,
):
    device_list = lax.axis_size("replica")
    total_rows, feature_columns = attention_output.shape
    holding_count, hidden_width, adapter_rank_size = down_weight.shape
    seg_count = segment_rows.shape[0]
    member = segment_member(segment_rows, total_rows, BLOCK)
    active_rows = jnp.sum(member, axis=1)
    slot_for_adapter = slot_lookup(store_adapter_ids, segment_adapter)
    partial_value = jnp.dot(attention_output, output_weight, preferred_element_type=jnp.float32)
    down_pieces = down_weight.reshape(
        holding_count, device_list, feature_columns, adapter_rank_size
    )
    up_pieces = up_weight.reshape(holding_count, device_list, feature_columns, adapter_rank_size)
    tile_pairs = jnp.concatenate([down_pieces, up_pieces], axis=3)
    arrived = lax.all_to_all(tile_pairs, "replica", split_axis=1, concat_axis=0, tiled=True)
    arrived = arrived.reshape(-1, feature_columns, 2 * adapter_rank_size)
    seg_tiles = arrived[slot_for_adapter]
    a_part = seg_tiles[:, :, :adapter_rank_size]
    b_part = seg_tiles[:, :, adapter_rank_size:]
    a_matrix = jnp.transpose(a_part, (1, 0, 2)).reshape(
        feature_columns, seg_count * adapter_rank_size
    )
    shrink_all = jnp.dot(attention_output, a_matrix, preferred_element_type=jnp.float32)
    shrink_all = shrink_all.reshape(total_rows, seg_count, adapter_rank_size)
    shrink_part = jnp.einsum("ps,psr->pr", member, shrink_all)
    base_column_block = lax.psum_scatter(partial_value, "replica", scatter_dimension=1, tiled=True)
    shrink = lax.psum(shrink_part, "replica")
    shrink_half = shrink.astype(jnp.bfloat16)
    spread = (member[:, :, None] * shrink_half.astype(jnp.float32)[:, None, :]).astype(jnp.bfloat16)
    spread = spread.reshape(total_rows, seg_count * adapter_rank_size)
    b_matrix = jnp.transpose(b_part, (0, 2, 1)).reshape(
        seg_count * adapter_rank_size, feature_columns
    )
    adapter_column_block = jnp.dot(spread, b_matrix, preferred_element_type=jnp.float32)
    mixed = active_rows[:, None] * (base_column_block + ADAPTER_SCALE * adapter_column_block)
    return mixed.astype(jnp.bfloat16)


def solution(mesh):
    in_specs = (
        P("parts", "replica"),
        P("replica", None),
        P(("parts", "replica"), None, None),
        P(("parts", "replica"), None, None),
        P("parts"),
        P("parts"),
        P("parts"),
    )
    out_specs = P("parts", "replica")
    return jax.shard_map(
        per_device, mesh=mesh, in_specs=in_specs, out_specs=out_specs, check_vma=False
    )
```

profile of v0, /device:TPU:0, one launch (start us, length us, event | category | flops | bytes accessed | tf_op | source)
XLA Modules:
  0.0 319.8 jit_solution(13850081227028889451)
XLA Ops:
  6.5 5.7 %copy.27 = bf16[32,8,32,256]{3,2,1,0:T(8,128)(2,1)} copy(bf16[32,8,32,256]{3,1,2,0:T(8,128)(2,1)} %bitcast.51) | data formatting | bytes 8388608
  12.2 3.4 %copy.28 = bf16[32,8,32,256]{3,2,1,0:T(8,128)(2,1)} copy(bf16[32,8,32,256]{3,1,2,0:T(8,128)(2,1)S(1)} %bitcast.52) | data formatting | bytes 8388608
  15.6 7.4 %pad_maximum_fusion = bf16[4,32,256,128]{2,1,3,0:T(8,128)(2,1)} fusion(bf16[4,32,256,64]{2,1,3,0:T(8,128)(2,1)} %bitcast.49, bf16[4,32,256,64]{2,1,3,0:T(8,128)(2,1)} %bitcast.48), kind=kLoop, calls=%fused_computation.1 | loop fusion | flops 4194304 | bytes 16777216 | tf_op jit(solution)/shard_map/concatenate | solution.py:49
  23.0 11.4 %copy.16 = bf16[4,32,256,128]{2,3,0,1:T(8,128)(2,1)} copy(bf16[4,32,256,128]{2,1,3,0:T(8,128)(2,1)} %pad_maximum_fusion) | data formatting | bytes 16777216 | tf_op jit(solution)/shard_map/concatenate | solution.py:49
  34.4 7.4 %all-to-all-start = ((bf16[4,32,256,128]{2,3,0,1:T(8,128)(2,1)}), bf16[4,32,256,128]{2,3,0,1:T(8,128)(2,1)}, u32[]{:S(2)}, u32[]{:S(2)}) async-start(bf16[4,32,256,128]{2,3,0,1:T(8,128)(2,1)} %copy.16), calls=%async_computation.1 | async-start | bytes 16777216 | tf_op jit(solution)/shard_map/all_to_all | solution.py:50
  41.8 0.0 reduce-scatter.2.cloned.1.call-start
  41.9 5.2 %fusion.13 = f32[152,8192]{1,0:T(8,128)} fusion(bf16[152,256]{1,0:T(8,128)(2,1)S(1)} %copy-done, bf16[256,8192]{1,0:T(8,128)(2,1)} %param.8), kind=kOutput, calls=%fused_computation.31 | convolution fusion | flops 637534208 | bytes 9252864 | tf_op jit(solution)/shard_map/dot_general | solution.py:44
  47.2 0.2 reduce-window.9
  47.4 0.1 fusion.8
  47.4 0.1 copy.26
  47.6 0.2 select_reduce_fusion
  47.8 0.1 fusion.9
  47.8 206.5 %all-to-all-done = bf16[4,32,256,128]{2,3,0,1:T(8,128)(2,1)} async-done(((bf16[4,32,256,128]{2,3,0,1:T(8,128)(2,1)}), bf16[4,32,256,128]{2,3,0,1:T(8,128)(2,1)}, u32[]{:S(2)}, u32[]{:S(2)}) %all-to-all-start) | async-done | bytes 8388640 | tf_op jit(solution)/shard_map/all_to_all | solution.py:50
  254.4 11.9 %copy.17 = bf16[4,32,256,128]{3,2,0,1:T(8,128)(2,1)} copy(bf16[4,32,256,128]{2,3,0,1:T(8,128)(2,1)} %all-to-all-done) | data formatting | bytes 16777216 | tf_op jit(solution)/shard_map/all_to_all | solution.py:50
  266.2 4.0 %gather_fusion = bf16[8,256,128]{2,1,0:T(8,128)(2,1)S(1)} fusion(bf16[128,256,128]{2,1,0:T(8,128)(2,1)} %bitcast.50, s32[1024]{0:T(1024)S(1)} %pad_clamp_fusion), kind=kCustom, calls=%fused_computation | custom fusion | bytes 1048608 | tf_op jit(solution)/shard_map/gather | solution.py:52
  270.3 0.2 slice_bitcast_fusion
  270.5 0.2 copy.18
  270.7 0.2 convolution_bitcast_fusion
  271.0 0.1 reshape.103
  271.1 0.3 multiply_reduce_fusion
  271.4 0.1 copy.23
  271.5 39.5 %psum.7 = bf16[152,64]{0,1:T(8,128)(2,1)S(1)} all-reduce(f32[152,64]{0,1:T(8,128)S(1)} %copy.23), channel_id=1, replica_groups=mesh['parts'=1,'replica'=32] {'replica'}, use_global_device_ids=true, to_apply=%region_4.5 | all-reduce | flops 9728 | bytes 58368 | tf_op jit(solution)/shard_map/psum | solution.py:62
  311.0 0.2 copy.24
  311.2 1.8 fusion.3
  (17 shorter events, 0.1 us)
Async XLA Ops:
  6.5 35.3 %copy-start = (bf16[152,256]{1,0:T(8,128)(2,1)S(1)}, bf16[152,256]{1,0:T(8,128)(2,1)}, u32[]{:S(2)}) copy-start(bf16[152,256]{1,0:T(8,128)(2,1)} %param.7) | copy-start | bytes 233476
  6.5 5.7 %copy-start.1 = (bf16[4,8192,64]{1,2,0:T(8,128)(2,1)S(1)}, bf16[4,8192,64]{1,2,0:T(8,128)(2,1)}, u32[]{:S(2)}) copy-start(bf16[4,8192,64]{1,2,0:T(8,128)(2,1)} %param.10) | copy-start | bytes 12582916
  34.4 220.0 %all-to-all-start = ((bf16[4,32,256,128]{2,3,0,1:T(8,128)(2,1)}), bf16[4,32,256,128]{2,3,0,1:T(8,128)(2,1)}, u32[]{:S(2)}, u32[]{:S(2)}) async-start(bf16[4,32,256,128]{2,3,0,1:T(8,128)(2,1)} %copy.16), calls=%async_computation.1 | async-start | bytes 16777216 | tf_op jit(solution)/shard_map/all_to_all | solution.py:50
  41.8 5.3 %copy-start.2 = (s32[8]{0:T(128)S(1)}, s32[8]{0:T(128)}, u32[]{:S(2)}) copy-start(s32[8]{0:T(128)} %param.13) | copy-start | bytes 100
  41.8 5.7 %copy-start.3 = (s32[128]{0:T(128)S(1)}, s32[128]{0:T(128)}, u32[]{:S(2)}) copy-start(s32[128]{0:T(128)} %param.11) | copy-start | bytes 1540
  41.8 5.7 %copy-start.4 = (s32[8]{0:T(128)S(1)}, s32[8]{0:T(128)}, u32[]{:S(2)}) copy-start(s32[8]{0:T(128)} %param.12) | copy-start | bytes 100
  41.8 269.4 %reduce-scatter.2.cloned.1.call-start = ((), (), s32[]{:S(2)}) async-start(), calls=%async_computation.2 | async-start | bytes 5136384 | tf_op jit(solution)/shard_map/reduce_scatter | solution.py:61
Sparse Core Ops, SparseCore 0:
  47.2 194.3 reduce-scatter.1
where the time goes:
time: 321 us; the launch traced here: 320 us
  waiting for transfers between devices  207 us (64%)
  blocking collectives  39.5 us (12%)
  local copies, waits for them, and re-layouts  37.3 us (12%)
  between operations  13.6 us (4%)
  other arithmetic  8.24 us (3%)
  starting transfers between devices  7.47 us (2%)
  matrix products  7.24 us (2%)
    all_to_all x1, waiting for transfers between devices, per_device(): lax.all_to_all(tile_pairs, 'replica', split_axis=1, concat_axis=0, tiled=...  207 us
    psum x1, blocking collectives, per_device(): shrink = lax.psum(shrink_part, 'replica')  39.5 us
    all_to_all x1, local copies, waits for them, and re-layouts, per_device(): lax.all_to_all(tile_pairs, 'replica', split_axis=1, concat_axis=0, tiled=...  11.9 us
    concatenate x1, local copies, waits for them, and re-layouts, per_device(): tile_pairs = jnp.concatenate([down_pieces, up_pieces], axis=3)  11.4 us
    unnamed x14, local copies, waits for them, and re-layouts  9.38 us
    all_to_all x1, starting transfers between devices, per_device(): lax.all_to_all(tile_pairs, 'replica', split_axis=1, concat_axis=0, tiled=...  7.43 us
    concatenate x1, other arithmetic, per_device(): tile_pairs = jnp.concatenate([down_pieces, up_pieces], axis=3)  7.41 us
  transfers between devices with their start and end apart: 2, of which 1 were waited for; matrix products, arithmetic and copies ran while one was open for 7% of the time, Pallas kernels for 0%

commit v1 on v0

--- a/solution.py
+++ b/solution.py
@@ -1,12 +1,20 @@
 import jax
 import jax.numpy as jnp
 from jax import lax
+from jax.experimental import pallas as pl
+from jax.experimental.pallas import tpu as pltpu
 from jax.sharding import PartitionSpec as P
 
 BLOCK = 4
 
 
 ADAPTER_SCALE = 2.0
+
+CHUNKS = 1
+
+PICKED = 2
+
+VMEM_LIMIT = 40 * 1024 * 1024
 
 
 def segment_member(segment_rows, total_rows, block_rows):
@@ -25,7 +33,7 @@
     return jnp.sum(jnp.where(equal, positions[None, :], 0), axis=1)
 
 
-def per_device(
+def tile_side(
     attention_output,
     output_weight,
     down_weight,
@@ -71,6 +79,296 @@
     return mixed.astype(jnp.bfloat16)
 
 
+def stage_masks(device_count):
+    masks = []
+    mask = device_count // 2
+    while mask >= 2:
+        masks.append(mask)
+        mask //= 2
+    other = list(masks)
+    if len(other) >= 2:
+        other[-1], other[-2] = other[-2], other[-1]
+    return masks, other
+
+
+def position_masks(masks):
+    found = [0]
+    for mask in masks:
+        found = found + [value ^ mask for value in found]
+    return found
+
+
+def exchange(value, mask_even, mask_odd):
+    count = lax.axis_size("replica")
+    pairs = [(i, i ^ (mask_odd if i & 1 else mask_even)) for i in range(count)]
+    return lax.ppermute(value, "replica", pairs)
+
+
+def block_at(device, position, tables):
+    even, odd = tables[0][position], tables[1][position]
+    if even == odd:
+        return jnp.bitwise_xor(device, even)
+    return jnp.bitwise_xor(device, jnp.where(jnp.bitwise_and(device, 1) == 0, even, odd))
+
+
+def padded_row(live_row, rows_ref):
+    place = live_row
+    end = jnp.int32(0)
+    for s in range(rows_ref.shape[0]):
+        count = rows_ref[s]
+        gap = (BLOCK - count % BLOCK) % BLOCK
+        end = end + count
+        place = place + jnp.where(live_row >= end, gap, 0)
+    return place
+
+
+def compact_kernel(rows_ref, x_ref, *out_refs):
+    step = out_refs[0].shape[0]
+    live_rows = step * len(out_refs)
+    shape = (live_rows, x_ref.shape[0])
+    live_row = lax.broadcasted_iota(jnp.int32, shape, 0)
+    layout_row = lax.broadcasted_iota(jnp.int32, shape, 1)
+    pick = jnp.where(padded_row(live_row, rows_ref) == layout_row, 1.0, 0.0).astype(jnp.bfloat16)
+    rows = jnp.dot(pick, x_ref[...], preferred_element_type=jnp.float32).astype(jnp.bfloat16)
+    for i, out_ref in enumerate(out_refs):
+        out_ref[...] = rows[i * step : (i + 1) * step]
+
+
+def spread_rows_kernel(count, rows_ref, *refs):
+    keep_refs, got_refs, out_ref = refs[:count], refs[count : 2 * count], refs[2 * count]
+    live = [
+        (k[0] + g[0].astype(jnp.float32)).astype(jnp.bfloat16) for k, g in zip(keep_refs, got_refs)
+    ]
+    mixed = live[0] if count == 1 else jnp.concatenate(live, axis=0)
+    shape = (out_ref.shape[0], mixed.shape[0])
+    live_row = lax.broadcasted_iota(jnp.int32, shape, 1)
+    layout_row = lax.broadcasted_iota(jnp.int32, shape, 0)
+    pick = jnp.where(padded_row(live_row, rows_ref) == layout_row, 1.0, 0.0).astype(jnp.bfloat16)
+    out_ref[...] = jnp.dot(pick, mixed, preferred_element_type=jnp.float32).astype(jnp.bfloat16)
+
+
+def base_kernel(tables, chunks, info_ref, *refs):
+    x_refs, w_ref, send_ref, keep_ref = refs[:chunks], refs[chunks], refs[chunks + 1], refs[chunks + 2]
+    me = info_ref[0]
+    peer = jnp.bitwise_xor(me, 1)
+    x = jnp.concatenate([x_ref[...] for x_ref in x_refs], axis=0) if chunks > 1 else x_refs[0][...]
+    width = x.shape[1]
+    for p in range(len(tables[0])):
+        for device, out_ref in ((peer, send_ref), (me, keep_ref)):
+            at = pl.multiple_of(block_at(device, p, tables) * width, width)
+            part = jnp.dot(x, w_ref[:, pl.ds(at, width)], preferred_element_type=jnp.float32)
+            out_ref[p] = part.astype(out_ref.dtype)
+
+
+def tiles_kernel(tables, info_ref, down_ref, up_ref, down_send, up_send, down_keep, up_keep):
+    me = info_ref[0]
+    peer = jnp.bitwise_xor(me, 1)
+    width = down_keep.shape[2]
+    for p in range(len(tables[0])):
+        for device, down_out, up_out in ((peer, down_send, up_send), (me, down_keep, up_keep)):
+            at = pl.multiple_of(block_at(device, p, tables) * width, width)
+            down_out[p] = down_ref[0, :, pl.ds(at, width)]
+            up_out[p] = up_ref[0, :, pl.ds(at, width)]
+
+
+def row_codes(first_row, shape, info_ref, rows_ref):
+    live_row = lax.broadcasted_iota(jnp.int32, shape, 0) + first_row
+    code = jnp.zeros(shape, jnp.int32)
+    start = jnp.int32(0)
+    for s in range(rows_ref.shape[0]):
+        end = start + rows_ref[s]
+        code = jnp.where((live_row >= start) & (live_row < end), info_ref[1 + PICKED + s], code)
+        start = end
+    return code
+
+
+def shrink_kernel(first_row, info_ref, rows_ref, x_ref, own_ref, peer_ref, out_ref):
+    positions, rows, _ = x_ref.shape
+    rank = out_ref.shape[1]
+    contract = (((1,), (1,)), ((), ()))
+    own = jnp.zeros((rows, own_ref.shape[1]), jnp.float32)
+    peer = jnp.zeros((rows, own_ref.shape[1]), jnp.float32)
+    for p in range(positions):
+        x = x_ref[p]
+        own = own + lax.dot_general(x, own_ref[p], contract, preferred_element_type=jnp.float32)
+        peer = peer + lax.dot_general(x, peer_ref[p], contract, preferred_element_type=jnp.float32)
+    code = row_codes(first_row, (rows, rank), info_ref, rows_ref)
+    total = jnp.zeros((rows, rank), jnp.float32)
+    for place, part in enumerate((own, peer)):
+        for j in range(PICKED):
+            value = part[:, j * rank : (j + 1) * rank]
+            total = total + jnp.where(code == 1 + place * PICKED + j, value, 0.0)
+    out_ref[...] = total
+
+
+def expand_kernel(
+    first_row, info_ref, rows_ref, mine_ref, got_ref, keep_ref, base_ref, own_ref, peer_ref, out_ref
+):
+    rows, rank = mine_ref.shape
+    half = (mine_ref[...] + got_ref[...]).astype(jnp.bfloat16)
+    code = row_codes(first_row, (rows, rank), info_ref, rows_ref)
+    picked = [
+        jnp.where(code == 1 + j, half.astype(jnp.float32), 0.0).astype(jnp.bfloat16)
+        for j in range(2 * PICKED)
+    ]
+    own = jnp.concatenate(picked[:PICKED], axis=1)
+    peer = jnp.concatenate(picked[PICKED:], axis=1)
+    for p in range(out_ref.shape[0]):
+        term = jnp.dot(own, own_ref[p], preferred_element_type=jnp.float32)
+        term = term + jnp.dot(peer, peer_ref[p], preferred_element_type=jnp.float32)
+        base = keep_ref[p] + base_ref[p].astype(jnp.float32)
+        out_ref[p] = (base + ADAPTER_SCALE * term).astype(out_ref.dtype)
+
+
+def smem():
+    return pl.BlockSpec(memory_space=pltpu.SMEM)
+
+
+def vmem():
+    return pl.BlockSpec(memory_space=pltpu.VMEM)
+
+
+def params(**more):
+    return pltpu.CompilerParams(vmem_limit_bytes=VMEM_LIMIT, **more)
+
+
+def owner_side(
+    attention_output,
+    output_weight,
+    down_weight,
+    up_weight,
+    store_adapter_ids,
+    segment_adapter,
+    segment_rows,
+):
+    bf16, f32 = jnp.bfloat16, jnp.float32
+    device_count = lax.axis_size("replica")
+    me = lax.axis_index("replica")
+    total_rows, width = attention_output.shape
+    held, _, rank = down_weight.shape
+    seg_count = segment_rows.shape[0]
+    live_rows = total_rows - seg_count * (BLOCK - 1)
+    step = live_rows // CHUNKS
+    even_masks, odd_masks = stage_masks(device_count)
+    tables = (position_masks(even_masks), position_masks(odd_masks))
+    positions = len(tables[0])
+
+    slot = slot_lookup(store_adapter_ids, segment_adapter)
+    owner, local = slot // held, slot % held
+
+    def picks(device):
+        here = owner == device
+        low = jnp.minimum(jnp.min(jnp.where(here, local, held)), held - 1)
+        high = jnp.max(jnp.where(here, local, 0))
+        return here, low, high
+
+    own_here, own_low, own_high = picks(me)
+    peer_here, peer_low, _ = picks(me ^ 1)
+    place = jnp.where(own_here, jnp.where(local == own_low, 1, 2), 0)
+    place = jnp.where(peer_here, PICKED + jnp.where(local == peer_low, 1, 2), place)
+    info = jnp.concatenate([jnp.stack([me, own_low, own_high]), place]).astype(jnp.int32)
+
+    live = pl.pallas_call(
+        compact_kernel,
+        out_shape=[jax.ShapeDtypeStruct((step, width), bf16)] * CHUNKS,
+        in_specs=[smem(), vmem()],
+        out_specs=[vmem()] * CHUNKS,
+        compiler_params=params(),
+        name="compact_rows",
+    )(segment_rows, attention_output)
+
+    tile = jax.ShapeDtypeStruct((positions, PICKED * rank, width), bf16)
+    tile_in = pl.BlockSpec((1, rank, down_weight.shape[1]), lambda j, info: (info[1 + j], 0, 0))
+    tile_out = pl.BlockSpec((positions, rank, width), lambda j, info: (0, j, 0))
+    down_send, up_send, down_own, up_own = pl.pallas_call(
+        lambda *refs: tiles_kernel(tables, *refs),
+        out_shape=[tile] * 4,
+        grid_spec=pltpu.PrefetchScalarGridSpec(
+            num_scalar_prefetch=1,
+            grid=(PICKED,),
+            in_specs=[tile_in, tile_in],
+            out_specs=[tile_out] * 4,
+        ),
+        compiler_params=params(dimension_semantics=("arbitrary",)),
+        name="cut_tiles",
+    )(info, jnp.transpose(down_weight, (0, 2, 1)), jnp.transpose(up_weight, (0, 2, 1)))
+    down_peer = exchange(down_send, 1, 1)
+    up_peer = exchange(up_send, 1, 1)
+
+    base_send, base_keep = pl.pallas_call(
+        lambda *refs: base_kernel(tables, CHUNKS, *refs),
+        out_shape=[
+            jax.ShapeDtypeStruct((positions, live_rows, width), bf16),
+            jax.ShapeDtypeStruct((positions, live_rows, width), f32),
+        ],
+        in_specs=[smem()] + [vmem()] * (CHUNKS + 1),
+        out_specs=[vmem()] * 2,
+        compiler_params=params(),
+        name="base_partials",
+    )(info, *live, output_weight)
+    base_got = exchange(base_send, 1, 1)
+
+    gathered = [part[None] for part in live]
+    for mask_even, mask_odd in zip(even_masks, odd_masks):
+        got = [exchange(part, mask_even, mask_odd) for part in gathered]
+        gathered = [jnp.concatenate(pair, axis=0) for pair in zip(gathered, got)]
+
+    half = positions // 2
+    totals = []
+    for i in range(CHUNKS):
+        mine = pl.pallas_call(
+            lambda *refs, i=i: shrink_kernel(i * step, *refs),
+            out_shape=jax.ShapeDtypeStruct((step, rank), f32),
+            in_specs=[smem()] * 2 + [vmem()] * 3,
+            out_specs=vmem(),
+            compiler_params=params(),
+            name="shrink",
+        )(info, segment_rows, gathered[i], down_own, down_peer)
+        got = exchange(mine, 1, 1)
+
+        def expand(part, dtype, i=i, mine=mine, got=got):
+            whole = pl.BlockSpec((step, rank), lambda g: (0, 0))
+            rows_of = pl.BlockSpec((half, step, width), lambda g: (part, i, 0))
+            tiles_of = pl.BlockSpec((half, PICKED * rank, width), lambda g: (part, 0, 0))
+            return pl.pallas_call(
+                lambda *refs: expand_kernel(i * step, *refs),
+                grid=(1,),
+                out_shape=jax.ShapeDtypeStruct((half, step, width), dtype),
+                in_specs=[smem()] * 2 + [whole] * 2 + [rows_of] * 2 + [tiles_of] * 2,
+                out_specs=pl.BlockSpec((half, step, width), lambda g: (0, 0, 0)),
+                compiler_params=params(dimension_semantics=("arbitrary",)),
+                name="expand",
+            )(info, segment_rows, mine, got, base_keep, base_got, up_own, up_peer)
+
+        totals.append((expand(0, f32), expand(1, bf16)))
+
+    keep = [pair[0] for pair in totals]
+    send = [pair[1] for pair in totals]
+    got = None
+    for k, (mask_even, mask_odd) in enumerate(zip(reversed(even_masks), reversed(odd_masks))):
+        if k:
+            left = keep[0].shape[0] // 2
+            sums = [a + b.astype(f32) for a, b in zip(keep, got)]
+            keep = [value[:left] for value in sums]
+            send = [value[left:].astype(bf16) for value in sums]
+        got = [exchange(value, mask_even, mask_odd) for value in send]
+    return pl.pallas_call(
+        lambda *refs: spread_rows_kernel(CHUNKS, *refs),
+        out_shape=jax.ShapeDtypeStruct((total_rows, width), bf16),
+        in_specs=[smem()] + [vmem()] * (2 * CHUNKS),
+        out_specs=vmem(),
+        compiler_params=params(),
+        name="spread_rows",
+    )(segment_rows, *keep, *got)
+
+
+def per_device(*arrays):
+    width, features = arrays[0].shape[1], arrays[1].shape[1]
+    if width % 128 == 0 and lax.axis_size("replica") >= 4:
+        return owner_side(*arrays)
+    return tile_side(*arrays)
+
+
 def solution(mesh):
     in_specs = (
         P("parts", "replica"),

time: 321 us -> 67.3 us (0.21)
  waiting for transfers between devices: 207 us -> 34.7 us
  blocking collectives: 39.5 us -> 0 us
  local copies, waits for them, and re-layouts: 37.3 us -> 6.26 us
  between operations: 13.6 us -> 1.47 us
  Pallas kernels: 0 us -> 8.24 us
  matrix products: 7.24 us -> 0 us
  starting transfers between devices: 7.47 us -> 13.7 us
  other arithmetic: 8.24 us -> 2.59 us
    all_to_all x1 -> x0, waiting for transfers between devices: 207 us -> none  [per_device(): lax.all_to_all(tile_pairs, 'replica', split_axis=1, concat_axis=0, tiled=...]
    psum x1 -> x0, blocking collectives: 39.5 us -> none  [per_device(): shrink = lax.psum(shrink_part, 'replica')]
    ppermute x0 -> x12, waiting for transfers between devices: none -> 34.7 us  [exchange(): return lax.ppermute(value, 'replica', pairs)]
    ppermute x0 -> x12, starting transfers between devices: none -> 13.7 us  [exchange(): return lax.ppermute(value, 'replica', pairs)]
    all_to_all x1 -> x0, local copies, waits for them, and re-layouts: 11.9 us -> none  [per_device(): lax.all_to_all(tile_pairs, 'replica', split_axis=1, concat_axis=0, tiled=...]
    concatenate x1, local copies, waits for them, and re-layouts: 11.4 us -> 0.03 us  [owner_side(): gathered = [jnp.concatenate(pair, axis=0) for pair in zip(gathered, got)]]
    pallas_call x0 -> x7, Pallas kernels: none -> 8.24 us  [the longest x2 2.1 us: expand(): pl.pallas_call(lambda *refs: expand_kernel(i * step, *refs), grid=(1,), o...]
    all_to_all x1 -> x0, starting transfers between devices: 7.43 us -> none  [per_device(): lax.all_to_all(tile_pairs, 'replica', split_axis=1, concat_axis=0, tiled=...]
  transfers between devices with their start and end apart: 2 -> 12, of which waited for: 1 -> 8; matrix products, arithmetic and copies ran while one was open for 7% -> 4% of each run, Pallas kernels for 0% -> 8%
where the time goes in v1:
time: 67.3 us; the launch traced here: 67 us
  waiting for transfers between devices  34.7 us (52%)
  starting transfers between devices  13.7 us (20%)
  Pallas kernels  8.24 us (12%)
  local copies, waits for them, and re-layouts  6.26 us (9%)
  other arithmetic  2.59 us (4%)
  between operations  1.47 us (2%)
    ppermute x12, waiting for transfers between devices, exchange(): return lax.ppermute(value, 'replica', pairs)  34.7 us
    ppermute x12, starting transfers between devices, exchange(): return lax.ppermute(value, 'replica', pairs)  13.7 us
    unnamed x16, local copies, waits for them, and re-layouts  6.17 us
    pallas_call x2, Pallas kernels, expand(): pl.pallas_call(lambda *refs: expand_kernel(i * step, *refs), grid=(1,), o...  2.1 us
    pallas_call x1, Pallas kernels, owner_side(): pl.pallas_call(lambda *refs: tiles_kernel(tables, *refs), out_shape=[tile...  1.39 us
    pallas_call x1, Pallas kernels, owner_side(): pl.pallas_call(lambda *refs: spread_rows_kernel(CHUNKS, *refs), out_shape...  1.37 us
  transfers between devices with their start and end apart: 12, of which 8 were waited for; matrix products, arithmetic and copies ran while one was open for 4% of the time, Pallas kernels for 8%

profile of v1, /device:TPU:0, one launch (start us, length us, event | category | flops | bytes accessed | tf_op | source)
XLA Modules:
  0.0 67.0 jit_solution(1092487669488220477)
XLA Ops:
  0.0 0.9 %copy-done.3 = bf16[152,256]{1,0:T(8,128)(2,1)S(1)} copy-done((bf16[152,256]{1,0:T(8,128)(2,1)S(1)}, bf16[152,256]{1,0:T(8,128)(2,1)}, u32[]{:S(2)}) %copy-start.3) | copy-done | bytes 77848
  2.3 4.1 %collective-permute-start = (bf16[1,128,256]{2,1,0:T(8,128)(2,1)S(1)}, bf16[1,128,256]{2,1,0:T(8,128)(2,1)S(1)}, u32[]{:S(2)}, u32[]{:S(2)}) collective-permute-start(bf16[1,128,256]{2,1,0:T(8,128)(2,1)S(1)} %bitcast.9), channel_id=1, source_target_pairs={{0,16},{1,17},{2,18},{3,19},{4,20},{5,21},{6,22},{7,23},{8,24},{9,... | collective-permute-start | bytes 196616 | tf_op jit(solution)/shard_map/ppermute | solution.py:104
  6.4 0.9 %select_reduce_fusion = s32[8]{0:T(128)S(1)} fusion(s32[128]{0:T(128)} %param.11, s32[8]{0:T(128)} %param.12), kind=kLoop, calls=%fused_computation.14 | loop fusion | flops 3064 | bytes 576 | tf_op jit(solution)/shard_map/reduce_sum | solution.py:33
  9.3 0.8 %collective-permute-done = bf16[1,128,256]{2,1,0:T(8,128)(2,1)S(1)} collective-permute-done((bf16[1,128,256]{2,1,0:T(8,128)(2,1)S(1)}, bf16[1,128,256]{2,1,0:T(8,128)(2,1)S(1)}, u32[]{:S(2)}, u32[]{:S(2)}) %collective-permute-start) | collective-permute-done | bytes 65568 | tf_op jit(solution)/shard_map/ppermute | solution.py:104
  10.1 0.9 %collective-permute-start.1 = (bf16[2,128,256]{2,1,0:T(8,128)(2,1)S(1)}, bf16[2,128,256]{2,1,0:T(8,128)(2,1)S(1)}, u32[]{:S(2)}, u32[]{:S(2)}) collective-permute-start(bf16[2,128,256]{2,1,0:T(8,128)(2,1)S(1)} %pad_maximum_fusion.2), channel_id=1, source_target_pairs={{0,8},{1,9},{2,10},{3,11},{4,12},{5,13},{6,14},{7,15},{8,0},{9,1},... | collective-permute-start | bytes 393224 | tf_op jit(solution)/shard_map/ppermute | solution.py:104
  10.9 4.2 %collective-permute-done.1 = bf16[2,128,256]{2,1,0:T(8,128)(2,1)S(1)} collective-permute-done((bf16[2,128,256]{2,1,0:T(8,128)(2,1)S(1)}, bf16[2,128,256]{2,1,0:T(8,128)(2,1)S(1)}, u32[]{:S(2)}, u32[]{:S(2)}) %collective-permute-start.1) | collective-permute-done | bytes 131104 | tf_op jit(solution)/shard_map/ppermute | solution.py:104
  15.1 1.8 %collective-permute-start.2 = (bf16[4,128,256]{2,1,0:T(8,128)(2,1)S(1)}, bf16[4,128,256]{2,1,0:T(8,128)(2,1)S(1)}, u32[]{:S(2)}, u32[]{:S(2)}) collective-permute-start(bf16[4,128,256]{2,1,0:T(8,128)(2,1)S(1)} %pad_maximum_fusion.1), channel_id=1, source_target_pairs={{0,4},{1,3},{2,6},{3,1},{4,0},{5,7},{6,2},{7,5},{8,12},{9,11},{10,... | collective-permute-start | bytes 786440 | tf_op jit(solution)/shard_map/ppermute | solution.py:104
  17.6 2.2 %copy-done = bf16[4,8192,64]{1,2,0:T(8,128)(2,1)S(1)} copy-done((bf16[4,8192,64]{1,2,0:T(8,128)(2,1)S(1)}, bf16[4,8192,64]{1,2,0:T(8,128)(2,1)}, u32[]{:S(2)}) %copy-start) | copy-done | bytes 4194328
  19.8 2.2 %copy-done.1 = bf16[4,8192,64]{1,2,0:T(8,128)(2,1)S(1)} copy-done((bf16[4,8192,64]{1,2,0:T(8,128)(2,1)S(1)}, bf16[4,8192,64]{1,2,0:T(8,128)(2,1)}, u32[]{:S(2)}) %copy-start.1) | copy-done | bytes 4194328
  22.0 1.4 %cut_tiles.1 = (bf16[16,128,256]{2,1,0:T(8,128)(2,1)S(1)}, bf16[16,128,256]{2,1,0:T(8,128)(2,1)S(1)}, bf16[16,128,256]{2,1,0:T(8,128)(2,1)S(1)}, bf16[16,128,256]{2,1,0:T(8,128)(2,1)S(1)}) custom-call(s32[11]{0:T(128)S(1)} %pad_add_fusion.refs_0_, bf16[4,64,8192]{2,1,0:T(8,128)(2,1)S(1)} %bitcast.7, bf16[4,64,8192]{2,1,0:T(8,128)(2,1)S(1)} %bitcast.8), custom_call_target="tpu_custom_call" | custom-call | tf_op jit(solution)/shard_map/cut_tiles/pallas_call | solution.py:283
  24.2 1.3 %base_partials.1 = (bf16[16,128,256]{2,1,0:T(8,128)(2,1)S(1)}, f32[16,128,256]{2,1,0:T(8,128)S(1)}) custom-call(s32[11]{0:T(128)S(1)} %pad_add_fusion.refs_0_, bf16[128,256]{1,0:T(8,128)(2,1)S(1)} %compact_rows.1.refs_1_, bf16[256,8192]{1,0:T(8,128)(2,1)S(1)} %copy-done.2), custom_call_target="tpu_custom_call" | custom-call | tf_op jit(solution)/shard_map/base_partials/pallas_call | solution.py:298
  25.7 1.5 %collective-permute-start.3 = (bf16[8,128,256]{2,1,0:T(8,128)(2,1)S(1)}, bf16[8,128,256]{2,1,0:T(8,128)(2,1)S(1)}, u32[]{:S(2)}, u32[]{:S(2)}) collective-permute-start(bf16[8,128,256]{2,1,0:T(8,128)(2,1)S(1)} %pad_maximum_fusion), channel_id=1, source_target_pairs={{0,2},{1,5},{2,0},{3,7},{4,6},{5,1},{6,4},{7,3},{8,10},{9,13},{10,... | collective-permute-start | bytes 1572872 | tf_op jit(solution)/shard_map/ppermute | solution.py:104
  27.3 7.6 %collective-permute-done.3 = bf16[8,128,256]{2,1,0:T(8,128)(2,1)S(1)} collective-permute-done((bf16[8,128,256]{2,1,0:T(8,128)(2,1)S(1)}, bf16[8,128,256]{2,1,0:T(8,128)(2,1)S(1)}, u32[]{:S(2)}, u32[]{:S(2)}) %collective-permute-start.3) | collective-permute-done | bytes 524320 | tf_op jit(solution)/shard_map/ppermute | solution.py:104
  35.0 1.3 %shrink.1.refs_2_ = f32[128,64]{1,0:T(8,128)S(1)} custom-call(s32[11]{0:T(128)S(1)} %pad_add_fusion.refs_0_, s32[8]{0:T(128)S(1)} %copy-done.5, bf16[16,128,256]{2,1,0:T(8,128)(2,1)S(1)} %constant_dynamic-update-slice_fusion.refs_2_, bf16[16,128,256]{2,1,0:T(8,128)(2,1)S(1)} %get-tuple-element.11.refs_3_, ...), custom_call_target="tpu_custom_call" | custom-call | tf_op jit(solution)/shard_map/shrink/pallas_call | solution.py:319
  36.4 1.2 %collective-permute-done.5.refs_3_ = f32[128,64]{1,0:T(8,128)S(1)} collective-permute-done((f32[128,64]{1,0:T(8,128)S(1)}, f32[128,64]{1,0:T(8,128)S(1)}, u32[]{:S(2)}, u32[]{:S(2)}) %collective-permute-start.5) | collective-permute-done | bytes 32800 | tf_op jit(solution)/shard_map/ppermute | solution.py:104
  37.6 1.1 %expand.3 = bf16[8,128,256]{2,1,0:T(8,128)(2,1)S(1)} custom-call(s32[11]{0:T(128)S(1)} %pad_add_fusion.refs_0_, s32[8]{0:T(128)S(1)} %copy-done.5, f32[128,64]{1,0:T(8,128)S(1)} %shrink.1.refs_2_, f32[128,64]{1,0:T(8,128)S(1)} %collective-permute-done.5.refs_3_, f32[16,128,256]{2,1,0:T(8,128)S(1)} %get-tuple-element.13.refs_4_, ...), custom_call_target="tpu_custom_call" | custom-call | tf_op jit(solution)/shard_map/expand/pallas_call | solution.py:333
  38.7 1.5 %collective-permute-start.8 = (bf16[8,128,256]{2,1,0:T(8,128)(2,1)S(1)}, bf16[8,128,256]{2,1,0:T(8,128)(2,1)S(1)}, u32[]{:S(2)}, u32[]{:S(2)}) collective-permute-start(bf16[8,128,256]{2,1,0:T(8,128)(2,1)S(1)} %expand.3), channel_id=1, source_target_pairs={{0,2},{1,5},{2,0},{3,7},{4,6},{5,1},{6,4},{7,3},{8,10},{9,13},{10,... | collective-permute-start | bytes 1572872 | tf_op jit(solution)/shard_map/ppermute | solution.py:104
  40.2 1.0 %expand.2 = f32[8,128,256]{2,1,0:T(8,128)S(1)} custom-call(s32[11]{0:T(128)S(1)} %pad_add_fusion.refs_0_, s32[8]{0:T(128)S(1)} %copy-done.5, f32[128,64]{1,0:T(8,128)S(1)} %shrink.1.refs_2_, f32[128,64]{1,0:T(8,128)S(1)} %collective-permute-done.5.refs_3_, f32[16,128,256]{2,1,0:T(8,128)S(1)} %get-tuple-element.13.refs_4_, ...), custom_call_target="tpu_custom_call" | custom-call | tf_op jit(solution)/shard_map/expand/pallas_call | solution.py:333
  41.3 6.7 %collective-permute-done.8 = bf16[8,128,256]{2,1,0:T(8,128)(2,1)S(1)} collective-permute-done((bf16[8,128,256]{2,1,0:T(8,128)(2,1)S(1)}, bf16[8,128,256]{2,1,0:T(8,128)(2,1)S(1)}, u32[]{:S(2)}, u32[]{:S(2)}) %collective-permute-start.8) | collective-permute-done | bytes 524320 | tf_op jit(solution)/shard_map/ppermute | solution.py:104
  48.4 6.1 %collective-permute-done.9 = bf16[4,128,256]{2,1,0:T(8,128)(2,1)S(1)} collective-permute-done((bf16[4,128,256]{2,1,0:T(8,128)(2,1)S(1)}, bf16[4,128,256]{2,1,0:T(8,128)(2,1)S(1)}, u32[]{:S(2)}, u32[]{:S(2)}) %collective-permute-start.9) | collective-permute-done | bytes 262176 | tf_op jit(solution)/shard_map/ppermute | solution.py:104
  55.2 4.4 %collective-permute-done.10 = bf16[2,128,256]{2,1,0:T(8,128)(2,1)S(1)} collective-permute-done((bf16[2,128,256]{2,1,0:T(8,128)(2,1)S(1)}, bf16[2,128,256]{2,1,0:T(8,128)(2,1)S(1)}, u32[]{:S(2)}, u32[]{:S(2)}) %collective-permute-start.10) | collective-permute-done | bytes 131104 | tf_op jit(solution)/shard_map/ppermute | solution.py:104
  59.7 2.2 %collective-permute-start.11 = (bf16[1,128,256]{2,1,0:T(8,128)(2,1)S(1)}, bf16[1,128,256]{2,1,0:T(8,128)(2,1)S(1)}, u32[]{:S(2)}, u32[]{:S(2)}) collective-permute-start(bf16[1,128,256]{2,1,0:T(8,128)(2,1)S(1)} %slice.40), channel_id=1, source_target_pairs={{0,16},{1,17},{2,18},{3,19},{4,20},{5,21},{6,22},{7,23},{8,24},{9,... | collective-permute-start | bytes 196616 | tf_op jit(solution)/shard_map/ppermute | solution.py:104
  61.8 3.8 %collective-permute-done.11.refs_2_ = bf16[1,128,256]{2,1,0:T(8,128)(2,1)S(1)} collective-permute-done((bf16[1,128,256]{2,1,0:T(8,128)(2,1)S(1)}, bf16[1,128,256]{2,1,0:T(8,128)(2,1)S(1)}, u32[]{:S(2)}, u32[]{:S(2)}) %collective-permute-start.11) | collective-permute-done | bytes 65568 | tf_op jit(solution)/shard_map/ppermute | solution.py:104
  65.6 1.4 %spread_rows.1 = bf16[152,256]{1,0:T(8,128)(2,1)} custom-call(s32[8]{0:T(128)S(1)} %copy-done.5, f32[1,128,256]{2,1,0:T(8,128)S(1)} %slice.31.refs_1_, bf16[1,128,256]{2,1,0:T(8,128)(2,1)S(1)} %collective-permute-done.11.refs_2_), custom_call_target="tpu_custom_call" | custom-call | tf_op jit(solution)/shard_map/spread_rows/pallas_call | solution.py:355
  (38 shorter events, 5.2 us)
Async XLA Ops:
  0.0 0.9 %copy-start.3 = (bf16[152,256]{1,0:T(8,128)(2,1)S(1)}, bf16[152,256]{1,0:T(8,128)(2,1)}, u32[]{:S(2)}) copy-start(bf16[152,256]{1,0:T(8,128)(2,1)} %x_ref.1) | copy-start | bytes 233476
  0.9 0.7 copy-start.4
  2.3 7.7 %collective-permute-start = (bf16[1,128,256]{2,1,0:T(8,128)(2,1)S(1)}, bf16[1,128,256]{2,1,0:T(8,128)(2,1)S(1)}, u32[]{:S(2)}, u32[]{:S(2)}) collective-permute-start(bf16[1,128,256]{2,1,0:T(8,128)(2,1)S(1)} %bitcast.9), channel_id=1, source_target_pairs={{0,16},{1,17},{2,18},{3,19},{4,20},{5,21},{6,22},{7,23},{8,24},{9,... | collective-permute-start | bytes 196616 | tf_op jit(solution)/shard_map/ppermute | solution.py:104
  10.1 5.0 %collective-permute-start.1 = (bf16[2,128,256]{2,1,0:T(8,128)(2,1)S(1)}, bf16[2,128,256]{2,1,0:T(8,128)(2,1)S(1)}, u32[]{:S(2)}, u32[]{:S(2)}) collective-permute-start(bf16[2,128,256]{2,1,0:T(8,128)(2,1)S(1)} %pad_maximum_fusion.2), channel_id=1, source_target_pairs={{0,8},{1,9},{2,10},{3,11},{4,12},{5,13},{6,14},{7,15},{8,0},{9,1},... | collective-permute-start | bytes 393224 | tf_op jit(solution)/shard_map/ppermute | solution.py:104
  15.1 10.5 %collective-permute-start.2 = (bf16[4,128,256]{2,1,0:T(8,128)(2,1)S(1)}, bf16[4,128,256]{2,1,0:T(8,128)(2,1)S(1)}, u32[]{:S(2)}, u32[]{:S(2)}) collective-permute-start(bf16[4,128,256]{2,1,0:T(8,128)(2,1)S(1)} %pad_maximum_fusion.1), channel_id=1, source_target_pairs={{0,4},{1,3},{2,6},{3,1},{4,0},{5,7},{6,2},{7,5},{8,12},{9,11},{10,... | collective-permute-start | bytes 786440 | tf_op jit(solution)/shard_map/ppermute | solution.py:104
  17.6 2.2 %copy-start = (bf16[4,8192,64]{1,2,0:T(8,128)(2,1)S(1)}, bf16[4,8192,64]{1,2,0:T(8,128)(2,1)}, u32[]{:S(2)}) copy-start(bf16[4,8192,64]{1,2,0:T(8,128)(2,1)} %param.9) | copy-start | bytes 12582916
  19.8 2.2 %copy-start.1 = (bf16[4,8192,64]{1,2,0:T(8,128)(2,1)S(1)}, bf16[4,8192,64]{1,2,0:T(8,128)(2,1)}, u32[]{:S(2)}) copy-start(bf16[4,8192,64]{1,2,0:T(8,128)(2,1)} %param.10) | copy-start | bytes 12582916
  22.0 2.2 %copy-start.2 = (bf16[256,8192]{1,0:T(8,128)(2,1)S(1)}, bf16[256,8192]{1,0:T(8,128)(2,1)}, u32[]{:S(2)}) copy-start(bf16[256,8192]{1,0:T(8,128)(2,1)} %refs_2_.1) | copy-start | bytes 12582916
  23.4 11.6 %copy-start.5 = (s32[8]{0:T(128)S(1)}, s32[8]{0:T(128)}, u32[]{:S(2)}) copy-start(s32[8]{0:T(128)} %refs_0_.1) | copy-start | bytes 100
  23.4 11.5 %collective-permute-start.4 = (bf16[16,128,256]{2,1,0:T(8,128)(2,1)S(1)}, bf16[16,128,256]{2,1,0:T(8,128)(2,1)S(1)}, u32[]{:S(2)}, u32[]{:S(2)}) collective-permute-start(bf16[16,128,256]{2,1,0:T(8,128)(2,1)S(1)} %get-tuple-element.12), channel_id=1, source_target_pairs={{0,1},{1,0},{2,3},{3,2},{4,5},{5,4},{6,7},{7,6},{8,9},{9,8},{10,11... | collective-permute-start | bytes 3145736 | tf_op jit(solution)/shard_map/ppermute | solution.py:104
  23.5 12.9 %collective-permute-start.7 = (bf16[16,128,256]{2,1,0:T(8,128)(2,1)S(1)}, bf16[16,128,256]{2,1,0:T(8,128)(2,1)S(1)}, u32[]{:S(2)}, u32[]{:S(2)}) collective-permute-start(bf16[16,128,256]{2,1,0:T(8,128)(2,1)S(1)} %get-tuple-element.16), channel_id=1, source_target_pairs={{0,1},{1,0},{2,3},{3,2},{4,5},{5,4},{6,7},{7,6},{8,9},{9,8},{10,11... | collective-permute-start | bytes 3145736 | tf_op jit(solution)/shard_map/ppermute | solution.py:104
  25.5 10.9 %collective-permute-start.6 = (bf16[16,128,256]{2,1,0:T(8,128)(2,1)S(1)}, bf16[16,128,256]{2,1,0:T(8,128)(2,1)S(1)}, u32[]{:S(2)}, u32[]{:S(2)}) collective-permute-start(bf16[16,128,256]{2,1,0:T(8,128)(2,1)S(1)} %get-tuple-element.14), channel_id=1, source_target_pairs={{0,1},{1,0},{2,3},{3,2},{4,5},{5,4},{6,7},{7,6},{8,9},{9,8},{10,11... | collective-permute-start | bytes 3145736 | tf_op jit(solution)/shard_map/ppermute | solution.py:104
  25.7 9.2 %collective-permute-start.3 = (bf16[8,128,256]{2,1,0:T(8,128)(2,1)S(1)}, bf16[8,128,256]{2,1,0:T(8,128)(2,1)S(1)}, u32[]{:S(2)}, u32[]{:S(2)}) collective-permute-start(bf16[8,128,256]{2,1,0:T(8,128)(2,1)S(1)} %pad_maximum_fusion), channel_id=1, source_target_pairs={{0,2},{1,5},{2,0},{3,7},{4,6},{5,1},{6,4},{7,3},{8,10},{9,13},{10,... | collective-permute-start | bytes 1572872 | tf_op jit(solution)/shard_map/ppermute | solution.py:104
  36.3 1.3 %collective-permute-start.5 = (f32[128,64]{1,0:T(8,128)S(1)}, f32[128,64]{1,0:T(8,128)S(1)}, u32[]{:S(2)}, u32[]{:S(2)}) collective-permute-start(f32[128,64]{1,0:T(8,128)S(1)} %shrink.1.refs_2_), channel_id=1, source_target_pairs={{0,1},{1,0},{2,3},{3,2},{4,5},{5,4},{6,7},{7,6},{8,9},{9,8},{10,11... | collective-permute-start | bytes 98312 | tf_op jit(solution)/shard_map/ppermute | solution.py:104
  38.7 9.2 %collective-permute-start.8 = (bf16[8,128,256]{2,1,0:T(8,128)(2,1)S(1)}, bf16[8,128,256]{2,1,0:T(8,128)(2,1)S(1)}, u32[]{:S(2)}, u32[]{:S(2)}) collective-permute-start(bf16[8,128,256]{2,1,0:T(8,128)(2,1)S(1)} %expand.3), channel_id=1, source_target_pairs={{0,2},{1,5},{2,0},{3,7},{4,6},{5,1},{6,4},{7,3},{8,10},{9,13},{10,... | collective-permute-start | bytes 1572872 | tf_op jit(solution)/shard_map/ppermute | solution.py:104
  48.1 6.4 %collective-permute-start.9 = (bf16[4,128,256]{2,1,0:T(8,128)(2,1)S(1)}, bf16[4,128,256]{2,1,0:T(8,128)(2,1)S(1)}, u32[]{:S(2)}, u32[]{:S(2)}) collective-permute-start(bf16[4,128,256]{2,1,0:T(8,128)(2,1)S(1)} %slice.38), channel_id=1, source_target_pairs={{0,4},{1,3},{2,6},{3,1},{4,0},{5,7},{6,2},{7,5},{8,12},{9,11},{10,... | collective-permute-start | bytes 786440 | tf_op jit(solution)/shard_map/ppermute | solution.py:104
  54.6 5.0 %collective-permute-start.10 = (bf16[2,128,256]{2,1,0:T(8,128)(2,1)S(1)}, bf16[2,128,256]{2,1,0:T(8,128)(2,1)S(1)}, u32[]{:S(2)}, u32[]{:S(2)}) collective-permute-start(bf16[2,128,256]{2,1,0:T(8,128)(2,1)S(1)} %slice.39), channel_id=1, source_target_pairs={{0,8},{1,9},{2,10},{3,11},{4,12},{5,13},{6,14},{7,15},{8,0},{9,1},... | collective-permute-start | bytes 393224 | tf_op jit(solution)/shard_map/ppermute | solution.py:104
  59.7 5.9 %collective-permute-start.11 = (bf16[1,128,256]{2,1,0:T(8,128)(2,1)S(1)}, bf16[1,128,256]{2,1,0:T(8,128)(2,1)S(1)}, u32[]{:S(2)}, u32[]{:S(2)}) collective-permute-start(bf16[1,128,256]{2,1,0:T(8,128)(2,1)S(1)} %slice.40), channel_id=1, source_target_pairs={{0,16},{1,17},{2,18},{3,19},{4,20},{5,21},{6,22},{7,23},{8,24},{9,... | collective-permute-start | bytes 196616 | tf_op jit(solution)/shard_map/ppermute | solution.py:104

commit v2 on v1

--- a/solution.py
+++ b/solution.py
@@ -10,7 +10,7 @@
 
 ADAPTER_SCALE = 2.0
 
-CHUNKS = 1
+CHUNKS = 2
 
 PICKED = 2
 
@@ -122,29 +122,45 @@
     return place
 
 
-def compact_kernel(rows_ref, x_ref, *out_refs):
+def compact_kernel(chunks, rows_hbm, x_hbm, *refs):
+    out_refs, pick_ref, code_ref = refs[:chunks], refs[chunks], refs[chunks + 1]
+    rows_ref, x_ref, rows_sem, x_sem = refs[chunks + 2 :]
+    x_copy = pltpu.make_async_copy(x_hbm, x_ref, x_sem)
+    x_copy.start()
+    rows_copy = pltpu.make_async_copy(rows_hbm, rows_ref, rows_sem)
+    rows_copy.start()
+    rows_copy.wait()
     step = out_refs[0].shape[0]
-    live_rows = step * len(out_refs)
-    shape = (live_rows, x_ref.shape[0])
+    shape = (step * chunks, x_ref.shape[0])
     live_row = lax.broadcasted_iota(jnp.int32, shape, 0)
     layout_row = lax.broadcasted_iota(jnp.int32, shape, 1)
     pick = jnp.where(padded_row(live_row, rows_ref) == layout_row, 1.0, 0.0).astype(jnp.bfloat16)
+    x_copy.wait()
     rows = jnp.dot(pick, x_ref[...], preferred_element_type=jnp.float32).astype(jnp.bfloat16)
     for i, out_ref in enumerate(out_refs):
         out_ref[...] = rows[i * step : (i + 1) * step]
-
-
-def spread_rows_kernel(count, rows_ref, *refs):
+    shape = pick_ref.shape
+    live_row = lax.broadcasted_iota(jnp.int32, shape, 1)
+    layout_row = lax.broadcasted_iota(jnp.int32, shape, 0)
+    back = padded_row(live_row, rows_ref) == layout_row
+    pick_ref[...] = jnp.where(back, 1.0, 0.0).astype(jnp.bfloat16)
+    live_row = lax.broadcasted_iota(jnp.int32, code_ref.shape, 0)
+    segment = jnp.zeros(code_ref.shape, jnp.int32)
+    end = jnp.int32(0)
+    for s in range(rows_ref.shape[0] - 1):
+        end = end + rows_ref[s]
+        segment = segment + jnp.where(live_row >= end, 1, 0)
+    code_ref[...] = segment
+
+
+def spread_rows_kernel(count, pick_ref, *refs):
     keep_refs, got_refs, out_ref = refs[:count], refs[count : 2 * count], refs[2 * count]
     live = [
         (k[0] + g[0].astype(jnp.float32)).astype(jnp.bfloat16) for k, g in zip(keep_refs, got_refs)
     ]
     mixed = live[0] if count == 1 else jnp.concatenate(live, axis=0)
-    shape = (out_ref.shape[0], mixed.shape[0])
-    live_row = lax.broadcasted_iota(jnp.int32, shape, 1)
-    layout_row = lax.broadcasted_iota(jnp.int32, shape, 0)
-    pick = jnp.where(padded_row(live_row, rows_ref) == layout_row, 1.0, 0.0).astype(jnp.bfloat16)
-    out_ref[...] = jnp.dot(pick, mixed, preferred_element_type=jnp.float32).astype(jnp.bfloat16)
+    out = jnp.dot(pick_ref[...], mixed, preferred_element_type=jnp.float32)
+    out_ref[...] = out.astype(jnp.bfloat16)
 
 
 def base_kernel(tables, chunks, info_ref, *refs):
@@ -160,64 +176,86 @@
             out_ref[p] = part.astype(out_ref.dtype)
 
 
-def tiles_kernel(tables, info_ref, down_ref, up_ref, down_send, up_send, down_keep, up_keep):
+def tiles_kernel(tables, info_ref, segment_ref, *refs):
+    down_hbm, up_hbm, down_send, up_send, down_keep, up_keep, code_ref = refs[:7]
+    held_ref, sems = refs[7:]
     me = info_ref[0]
     peer = jnp.bitwise_xor(me, 1)
     width = down_keep.shape[2]
-    for p in range(len(tables[0])):
-        for device, down_out, up_out in ((peer, down_send, up_send), (me, down_keep, up_keep)):
-            at = pl.multiple_of(block_at(device, p, tables) * width, width)
-            down_out[p] = down_ref[0, :, pl.ds(at, width)]
-            up_out[p] = up_ref[0, :, pl.ds(at, width)]
-
-
-def row_codes(first_row, shape, info_ref, rows_ref):
-    live_row = lax.broadcasted_iota(jnp.int32, shape, 0) + first_row
-    code = jnp.zeros(shape, jnp.int32)
-    start = jnp.int32(0)
-    for s in range(rows_ref.shape[0]):
-        end = start + rows_ref[s]
-        code = jnp.where((live_row >= start) & (live_row < end), info_ref[1 + PICKED + s], code)
-        start = end
-    return code
-
-
-def shrink_kernel(first_row, info_ref, rows_ref, x_ref, own_ref, peer_ref, out_ref):
-    positions, rows, _ = x_ref.shape
-    rank = out_ref.shape[1]
+    rank = down_hbm.shape[1]
+    copies = []
+    for j in range(PICKED):
+        for k, source in enumerate((down_hbm, up_hbm)):
+            at = 2 * j + k
+            copies.append(
+                pltpu.make_async_copy(source.at[info_ref[1 + j]], held_ref.at[at], sems.at[at])
+            )
+            copies[-1].start()
+    segment = segment_ref[...]
+    code = jnp.zeros(segment.shape, jnp.int32)
+    for s in range(info_ref.shape[0] - 1 - PICKED):
+        code = jnp.where(segment == s, info_ref[1 + PICKED + s], code)
+    code_ref[...] = code
+    for j in range(PICKED):
+        rows = slice(j * rank, (j + 1) * rank)
+        for k, (send, keep) in enumerate(((down_send, down_keep), (up_send, up_keep))):
+            copies[2 * j + k].wait()
+            for p in range(len(tables[0])):
+                for device, out in ((peer, send), (me, keep)):
+                    at = pl.multiple_of(block_at(device, p, tables) * width, width)
+                    out[p, rows, :] = held_ref[2 * j + k, :, pl.ds(at, width)]
+
+
+def shrink_sums(x_ref, own_ref, peer_ref, first, own, peer):
     contract = (((1,), (1,)), ((), ()))
-    own = jnp.zeros((rows, own_ref.shape[1]), jnp.float32)
-    peer = jnp.zeros((rows, own_ref.shape[1]), jnp.float32)
-    for p in range(positions):
+    for p in range(x_ref.shape[0]):
         x = x_ref[p]
-        own = own + lax.dot_general(x, own_ref[p], contract, preferred_element_type=jnp.float32)
-        peer = peer + lax.dot_general(x, peer_ref[p], contract, preferred_element_type=jnp.float32)
-    code = row_codes(first_row, (rows, rank), info_ref, rows_ref)
+        own = own + lax.dot_general(
+            x, own_ref[first + p], contract, preferred_element_type=jnp.float32
+        )
+        peer = peer + lax.dot_general(
+            x, peer_ref[first + p], contract, preferred_element_type=jnp.float32
+        )
+    return own, peer
+
+
+def shrink_start_kernel(x_ref, own_ref, peer_ref, out_ref):
+    zero = jnp.zeros(out_ref.shape[1:], jnp.float32)
+    out_ref[0], out_ref[1] = shrink_sums(x_ref, own_ref, peer_ref, 0, zero, zero)
+
+
+def shrink_kernel(code_ref, sums_ref, x_ref, own_ref, peer_ref, out_ref):
+    rows, rank = out_ref.shape
+    sums = shrink_sums(x_ref, own_ref, peer_ref, x_ref.shape[0], sums_ref[0], sums_ref[1])
+    code = code_ref[...]
     total = jnp.zeros((rows, rank), jnp.float32)
-    for place, part in enumerate((own, peer)):
+    for place, part in enumerate(sums):
         for j in range(PICKED):
             value = part[:, j * rank : (j + 1) * rank]
             total = total + jnp.where(code == 1 + place * PICKED + j, value, 0.0)
     out_ref[...] = total
 
 
-def expand_kernel(
-    first_row, info_ref, rows_ref, mine_ref, got_ref, keep_ref, base_ref, own_ref, peer_ref, out_ref
-):
-    rows, rank = mine_ref.shape
+def expand_kernel(first, row, code_ref, mine_ref, got_ref, keep_ref, base_ref, own_ref, peer_ref, out_ref):
+    positions, rows, _ = out_ref.shape
     half = (mine_ref[...] + got_ref[...]).astype(jnp.bfloat16)
-    code = row_codes(first_row, (rows, rank), info_ref, rows_ref)
+    code = code_ref[...]
     picked = [
         jnp.where(code == 1 + j, half.astype(jnp.float32), 0.0).astype(jnp.bfloat16)
         for j in range(2 * PICKED)
     ]
     own = jnp.concatenate(picked[:PICKED], axis=1)
     peer = jnp.concatenate(picked[PICKED:], axis=1)
-    for p in range(out_ref.shape[0]):
-        term = jnp.dot(own, own_ref[p], preferred_element_type=jnp.float32)
-        term = term + jnp.dot(peer, peer_ref[p], preferred_element_type=jnp.float32)
-        base = keep_ref[p] + base_ref[p].astype(jnp.float32)
+    for p in range(positions):
+        at = first + p
+        term = jnp.dot(own, own_ref[at], preferred_element_type=jnp.float32)
+        term = term + jnp.dot(peer, peer_ref[at], preferred_element_type=jnp.float32)
+        base = keep_ref[at, row : row + rows] + base_ref[at, row : row + rows].astype(jnp.float32)
         out_ref[p] = (base + ADAPTER_SCALE * term).astype(out_ref.dtype)
+
+
+def after(values, *earlier):
+    return lax.optimization_barrier((values, earlier))[0]
 
 
 def smem():
@@ -226,6 +264,10 @@
 
 def vmem():
     return pl.BlockSpec(memory_space=pltpu.VMEM)
+
+
+def in_hbm(value):
+    return pltpu.with_memory_space_constraint(value, pltpu.HBM)
 
 
 def params(**more):
@@ -268,84 +310,121 @@
     place = jnp.where(peer_here, PICKED + jnp.where(local == peer_low, 1, 2), place)
     info = jnp.concatenate([jnp.stack([me, own_low, own_high]), place]).astype(jnp.int32)
 
-    live = pl.pallas_call(
-        compact_kernel,
-        out_shape=[jax.ShapeDtypeStruct((step, width), bf16)] * CHUNKS,
-        in_specs=[smem(), vmem()],
-        out_specs=[vmem()] * CHUNKS,
+    hbm = pl.BlockSpec(memory_space=pltpu.HBM)
+    *live, pick, segment = pl.pallas_call(
+        lambda *refs: compact_kernel(CHUNKS, *refs),
+        out_shape=[jax.ShapeDtypeStruct((step, width), bf16)] * CHUNKS
+        + [
+            jax.ShapeDtypeStruct((total_rows, live_rows), bf16),
+            jax.ShapeDtypeStruct((live_rows, rank), jnp.int32),
+        ],
+        in_specs=[hbm, hbm],
+        out_specs=[vmem()] * (CHUNKS + 2),
+        scratch_shapes=[
+            pltpu.SMEM(segment_rows.shape, jnp.int32),
+            pltpu.VMEM(attention_output.shape, bf16),
+            pltpu.SemaphoreType.DMA,
+            pltpu.SemaphoreType.DMA,
+        ],
         compiler_params=params(),
         name="compact_rows",
-    )(segment_rows, attention_output)
-
-    tile = jax.ShapeDtypeStruct((positions, PICKED * rank, width), bf16)
-    tile_in = pl.BlockSpec((1, rank, down_weight.shape[1]), lambda j, info: (info[1 + j], 0, 0))
-    tile_out = pl.BlockSpec((positions, rank, width), lambda j, info: (0, j, 0))
-    down_send, up_send, down_own, up_own = pl.pallas_call(
-        lambda *refs: tiles_kernel(tables, *refs),
-        out_shape=[tile] * 4,
-        grid_spec=pltpu.PrefetchScalarGridSpec(
-            num_scalar_prefetch=1,
-            grid=(PICKED,),
-            in_specs=[tile_in, tile_in],
-            out_specs=[tile_out] * 4,
-        ),
-        compiler_params=params(dimension_semantics=("arbitrary",)),
-        name="cut_tiles",
-    )(info, jnp.transpose(down_weight, (0, 2, 1)), jnp.transpose(up_weight, (0, 2, 1)))
-    down_peer = exchange(down_send, 1, 1)
-    up_peer = exchange(up_send, 1, 1)
-
-    base_send, base_keep = pl.pallas_call(
-        lambda *refs: base_kernel(tables, CHUNKS, *refs),
-        out_shape=[
-            jax.ShapeDtypeStruct((positions, live_rows, width), bf16),
-            jax.ShapeDtypeStruct((positions, live_rows, width), f32),
-        ],
-        in_specs=[smem()] + [vmem()] * (CHUNKS + 1),
-        out_specs=[vmem()] * 2,
-        compiler_params=params(),
-        name="base_partials",
-    )(info, *live, output_weight)
-    base_got = exchange(base_send, 1, 1)
-
-    gathered = [part[None] for part in live]
-    for mask_even, mask_odd in zip(even_masks, odd_masks):
-        got = [exchange(part, mask_even, mask_odd) for part in gathered]
-        gathered = [jnp.concatenate(pair, axis=0) for pair in zip(gathered, got)]
-
-    half = positions // 2
-    totals = []
-    for i in range(CHUNKS):
-        mine = pl.pallas_call(
-            lambda *refs, i=i: shrink_kernel(i * step, *refs),
+    )(in_hbm(segment_rows), in_hbm(attention_output))
+
+    def cut_tiles(info):
+        tile = jax.ShapeDtypeStruct((positions, PICKED * rank, width), bf16)
+        return pl.pallas_call(
+            lambda *refs: tiles_kernel(tables, *refs),
+            out_shape=[tile] * 4 + [jax.ShapeDtypeStruct((live_rows, rank), jnp.int32)],
+            in_specs=[smem(), vmem(), hbm, hbm],
+            out_specs=[vmem()] * 5,
+            scratch_shapes=[
+                pltpu.VMEM((2 * PICKED, rank, down_weight.shape[1]), bf16),
+                pltpu.SemaphoreType.DMA((2 * PICKED,)),
+            ],
+            compiler_params=params(),
+            name="cut_tiles",
+        )(
+            info,
+            segment,
+            in_hbm(jnp.transpose(down_weight, (0, 2, 1))),
+            in_hbm(jnp.transpose(up_weight, (0, 2, 1))),
+        )
+
+    def base_partials(info):
+        return pl.pallas_call(
+            lambda *refs: base_kernel(tables, CHUNKS, *refs),
+            out_shape=[
+                jax.ShapeDtypeStruct((positions, live_rows, width), bf16),
+                jax.ShapeDtypeStruct((positions, live_rows, width), f32),
+            ],
+            in_specs=[smem()] + [vmem()] * (CHUNKS + 1),
+            out_specs=[vmem()] * 2,
+            compiler_params=params(),
+            name="base_partials",
+        )(info, *live, output_weight)
+
+    def shrink_start(x):
+        return pl.pallas_call(
+            shrink_start_kernel,
+            out_shape=jax.ShapeDtypeStruct((2, step, PICKED * rank), f32),
+            in_specs=[vmem()] * 3,
+            out_specs=vmem(),
+            compiler_params=params(),
+            name="shrink_start",
+        )(x, down_own, down_peer)
+
+    def shrink(i, sums, x):
+        return pl.pallas_call(
+            shrink_kernel,
             out_shape=jax.ShapeDtypeStruct((step, rank), f32),
-            in_specs=[smem()] * 2 + [vmem()] * 3,
+            in_specs=[vmem()] * 5,
             out_specs=vmem(),
             compiler_params=params(),
             name="shrink",
-        )(info, segment_rows, gathered[i], down_own, down_peer)
-        got = exchange(mine, 1, 1)
-
-        def expand(part, dtype, i=i, mine=mine, got=got):
-            whole = pl.BlockSpec((step, rank), lambda g: (0, 0))
-            rows_of = pl.BlockSpec((half, step, width), lambda g: (part, i, 0))
-            tiles_of = pl.BlockSpec((half, PICKED * rank, width), lambda g: (part, 0, 0))
-            return pl.pallas_call(
-                lambda *refs: expand_kernel(i * step, *refs),
-                grid=(1,),
-                out_shape=jax.ShapeDtypeStruct((half, step, width), dtype),
-                in_specs=[smem()] * 2 + [whole] * 2 + [rows_of] * 2 + [tiles_of] * 2,
-                out_specs=pl.BlockSpec((half, step, width), lambda g: (0, 0, 0)),
-                compiler_params=params(dimension_semantics=("arbitrary",)),
-                name="expand",
-            )(info, segment_rows, mine, got, base_keep, base_got, up_own, up_peer)
-
-        totals.append((expand(0, f32), expand(1, bf16)))
-
-    keep = [pair[0] for pair in totals]
-    send = [pair[1] for pair in totals]
-    got = None
-    for k, (mask_even, mask_odd) in enumerate(zip(reversed(even_masks), reversed(odd_masks))):
+        )(codes[i], sums, x, down_own, down_peer)
+
+    def expand(i, part, dtype):
+        return pl.pallas_call(
+            lambda *refs: expand_kernel(part * half, i * step, *refs),
+            out_shape=jax.ShapeDtypeStruct((half, step, width), dtype),
+            in_specs=[vmem()] * 7,
+            out_specs=vmem(),
+            compiler_params=params(),
+            name="expand",
+        )(codes[i], mine[i], theirs[i], base_keep, base_got, up_own, up_peer)
+
+    stages = list(zip(even_masks, odd_masks))
+    cut_at, base_at = len(stages) - 2, len(stages) - 1
+    gathered = [part[None] for part in live]
+    for k, (mask_even, mask_odd) in enumerate(stages):
+        got = [exchange(part, mask_even, mask_odd) for part in gathered]
+        done = ()
+        if k == base_at:
+            base_send, base_keep = base_partials(after(info, gathered) if k else info)
+            base_got = exchange(base_send, 1, 1)
+            done = (base_send,)
+        if k == cut_at:
+            down_send, up_send, down_own, up_own, code = cut_tiles(after(info, gathered))
+            down_peer = exchange(down_send, 1, 1)
+            up_peer = exchange(up_send, 1, 1)
+            done = (down_send,)
+        if k < len(stages) - 1:
+            gathered = [jnp.concatenate(pair, axis=0) for pair in zip(gathered, got)]
+        if done:
+            gathered = after(gathered, *done)
+
+    half = positions // 2
+    codes = [code[i * step : (i + 1) * step] for i in range(CHUNKS)]
+    sums = [shrink_start(part) for part in gathered]
+    mine, theirs, send = [], [], []
+    for i in range(CHUNKS):
+        last = got[i] if i == 0 else after(got[i], send[i - 1])
+        mine.append(shrink(i, sums[i], last))
+        theirs.append(exchange(mine[i], 1, 1))
+        send.append(expand(i, 1, bf16))
+    keep = [expand(i, 0, f32) for i in range(CHUNKS)]
+
+    for k, (mask_even, mask_odd) in enumerate(reversed(stages)):
         if k:
             left = keep[0].shape[0] // 2
             sums = [a + b.astype(f32) for a, b in zip(keep, got)]
@@ -355,11 +434,11 @@
     return pl.pallas_call(
         lambda *refs: spread_rows_kernel(CHUNKS, *refs),
         out_shape=jax.ShapeDtypeStruct((total_rows, width), bf16),
-        in_specs=[smem()] + [vmem()] * (2 * CHUNKS),
+        in_specs=[vmem()] * (2 * CHUNKS + 1),
         out_specs=vmem(),
         compiler_params=params(),
         name="spread_rows",
-    )(segment_rows, *keep, *got)
+    )(pick, *keep, *got)
 
 
 def per_device(*arrays):

time: 67.3 us -> 58 us (0.86)
  waiting for transfers between devices: 34.7 us -> 19.1 us
  starting transfers between devices: 13.7 us -> 24.8 us
  local copies, waits for them, and re-layouts: 6.26 us -> 0.08 us
  Pallas kernels: 8.24 us -> 9.82 us
    ppermute x12 -> x21, waiting for transfers between devices: 34.7 us -> 19.1 us  [exchange(): return lax.ppermute(value, 'replica', pairs)]
    ppermute x12 -> x21, starting transfers between devices: 13.7 us -> 24.8 us  [exchange(): return lax.ppermute(value, 'replica', pairs)]
    unnamed x16 -> x2, local copies, waits for them, and re-layouts: 6.17 us -> 0.01 us
    pallas_call x6 -> x11, Pallas kernels: 6.87 us -> 9.02 us  [the longest x1 3.16 us: cut_tiles(): pl.pallas_call(lambda *refs: tiles_kernel(tables, *refs), out_shape=[tile...]
  transfers between devices with their start and end apart: 12 -> 21, of which waited for: 8 -> 9; matrix products, arithmetic and copies ran while one was open for 4% -> 5% of each run, Pallas kernels for 8% -> 14%
where the time goes in v2:
time: 58 us; the launch traced here: 57.8 us
  starting transfers between devices  24.8 us (43%)
  waiting for transfers between devices  19.1 us (33%)
  Pallas kernels  9.82 us (17%)
  other arithmetic  2.55 us (4%)
  between operations  1.48 us (3%)
    ppermute x21, starting transfers between devices, exchange(): return lax.ppermute(value, 'replica', pairs)  24.8 us
    ppermute x21, waiting for transfers between devices, exchange(): return lax.ppermute(value, 'replica', pairs)  19.1 us
    pallas_call x1, Pallas kernels, cut_tiles(): pl.pallas_call(lambda *refs: tiles_kernel(tables, *refs), out_shape=[tile...  3.16 us
    pallas_call x4, Pallas kernels, expand(): pl.pallas_call(lambda *refs: expand_kernel(part * half, i * step, *refs),...  1.37 us
    pallas_call x1, Pallas kernels, base_partials(): pl.pallas_call(lambda *refs: base_kernel(tables, CHUNKS, *refs), out_shap...  1.36 us
  transfers between devices with their start and end apart: 21, of which 9 were waited for; matrix products, arithmetic and copies ran while one was open for 5% of the time, Pallas kernels for 14%

profile of v2, /device:TPU:0, one launch (start us, length us, event | category | flops | bytes accessed | tf_op | source)
XLA Modules:
  0.0 57.8 jit_solution(8321518620485779412)
XLA Ops:
  0.0 1.1 %compact_rows.1 = (bf16[64,256]{1,0:T(8,128)(2,1)S(1)}, bf16[64,256]{1,0:T(8,128)(2,1)S(1)}, bf16[152,128]{1,0:T(8,128)(2,1)S(1)}, s32[128,64]{1,0:T(8,128)S(1)}) custom-call(s32[8]{0:T(128)} %refs_0_.1, bf16[152,256]{1,0:T(8,128)(2,1)} %refs_1_.1), custom_call_target="tpu_custom_call" | custom-call | tf_op jit(solution)/shard_map/compact_rows/pallas_call | solution.py:314
  1.1 4.1 %collective-permute-start = (bf16[1,64,256]{2,1,0:T(8,128)(2,1)S(1)}, bf16[1,64,256]{2,1,0:T(8,128)(2,1)S(1)}, u32[]{:S(2)}, u32[]{:S(2)}) collective-permute-start(bf16[1,64,256]{2,1,0:T(8,128)(2,1)S(1)} %bitcast.7), channel_id=1, source_target_pairs={{0,16},{1,17},{2,18},{3,19},{4,20},{5,21},{6,22},{7,23},{8,24},{9,... | collective-permute-start | bytes 98312 | tf_op jit(solution)/shard_map/ppermute | solution.py:104
  5.3 0.9 %select_reduce_fusion = s32[8]{0:T(128)S(1)} fusion(s32[128]{0:T(128)} %param.11, s32[8]{0:T(128)} %param.12), kind=kLoop, calls=%fused_computation.18 | loop fusion | flops 3064 | bytes 576 | tf_op jit(solution)/shard_map/reduce_sum | solution.py:33
  8.1 1.9 %collective-permute-start.1 = (bf16[2,64,256]{2,1,0:T(8,128)(2,1)S(1)}, bf16[2,64,256]{2,1,0:T(8,128)(2,1)S(1)}, u32[]{:S(2)}, u32[]{:S(2)}) collective-permute-start(bf16[2,64,256]{2,1,0:T(8,128)(2,1)S(1)} %pad_maximum_fusion.4), channel_id=1, source_target_pairs={{0,8},{1,9},{2,10},{3,11},{4,12},{5,13},{6,14},{7,15},{8,0},{9,1},... | collective-permute-start | bytes 196616 | tf_op jit(solution)/shard_map/ppermute | solution.py:104
  10.0 1.6 %collective-permute-start.3 = (bf16[2,64,256]{2,1,0:T(8,128)(2,1)S(1)}, bf16[2,64,256]{2,1,0:T(8,128)(2,1)S(1)}, u32[]{:S(2)}, u32[]{:S(2)}) collective-permute-start(bf16[2,64,256]{2,1,0:T(8,128)(2,1)S(1)} %pad_maximum_fusion.5), channel_id=1, source_target_pairs={{0,8},{1,9},{2,10},{3,11},{4,12},{5,13},{6,14},{7,15},{8,0},{9,1},... | collective-permute-start | bytes 196616 | tf_op jit(solution)/shard_map/ppermute | solution.py:104
  11.7 1.4 %collective-permute-done.1 = bf16[2,64,256]{2,1,0:T(8,128)(2,1)S(1)} collective-permute-done((bf16[2,64,256]{2,1,0:T(8,128)(2,1)S(1)}, bf16[2,64,256]{2,1,0:T(8,128)(2,1)S(1)}, u32[]{:S(2)}, u32[]{:S(2)}) %collective-permute-start.1) | collective-permute-done | bytes 65568 | tf_op jit(solution)/shard_map/ppermute | solution.py:104
  13.1 1.6 %collective-permute-start.4 = (bf16[4,64,256]{2,1,0:T(8,128)(2,1)S(1)}, bf16[4,64,256]{2,1,0:T(8,128)(2,1)S(1)}, u32[]{:S(2)}, u32[]{:S(2)}) collective-permute-start(bf16[4,64,256]{2,1,0:T(8,128)(2,1)S(1)} %pad_maximum_fusion.2), channel_id=1, source_target_pairs={{0,4},{1,3},{2,6},{3,1},{4,0},{5,7},{6,2},{7,5},{8,12},{9,11},{10,... | collective-permute-start | bytes 393224 | tf_op jit(solution)/shard_map/ppermute | solution.py:104
  14.7 1.3 %collective-permute-start.5 = (bf16[4,64,256]{2,1,0:T(8,128)(2,1)S(1)}, bf16[4,64,256]{2,1,0:T(8,128)(2,1)S(1)}, u32[]{:S(2)}, u32[]{:S(2)}) collective-permute-start(bf16[4,64,256]{2,1,0:T(8,128)(2,1)S(1)} %pad_maximum_fusion.3), channel_id=1, source_target_pairs={{0,4},{1,3},{2,6},{3,1},{4,0},{5,7},{6,2},{7,5},{8,12},{9,11},{10,... | collective-permute-start | bytes 393224 | tf_op jit(solution)/shard_map/ppermute | solution.py:104
  16.7 3.2 %cut_tiles.1 = (bf16[16,128,256]{2,1,0:T(8,128)(2,1)S(1)}, bf16[16,128,256]{2,1,0:T(8,128)(2,1)S(1)}, bf16[16,128,256]{2,1,0:T(8,128)(2,1)S(1)}, bf16[16,128,256]{2,1,0:T(8,128)(2,1)S(1)}, s32[128,64]{1,0:T(8,128)S(1)}) custom-call(s32[11]{0:T(128)S(1)} %pad_add_fusion.refs_0_, s32[128,64]{1,0:T(8,128)S(1)} %get-tuple-element.27.refs_1_, ...), custom_call_target="tpu_custom_call" | custom-call | tf_op jit(solution)/shard_map/cut_tiles/pallas_call | solution.py:335
  20.5 1.4 %base_partials.1 = (bf16[16,128,256]{2,1,0:T(8,128)(2,1)S(1)}, f32[16,128,256]{2,1,0:T(8,128)S(1)}) custom-call(s32[11]{0:T(128)S(1)} %pad_add_fusion.refs_0_, bf16[64,256]{1,0:T(8,128)(2,1)S(1)} %get-tuple-element.24.refs_1_, bf16[64,256]{1,0:T(8,128)(2,1)S(1)} %get-tuple-element.25.refs_2_, bf16[256,8192]{1,0:T(8,128)(2,1)S(1)} %copy-done), custom_call_target="tpu_custom_call" | custom-call | tf_op jit(solution)/shard_map/base_partials/pallas_call | solution.py:354
  22.0 1.5 %collective-permute-start.7 = (bf16[8,64,256]{2,1,0:T(8,128)(2,1)S(1)}, bf16[8,64,256]{2,1,0:T(8,128)(2,1)S(1)}, u32[]{:S(2)}, u32[]{:S(2)}) collective-permute-start(bf16[8,64,256]{2,1,0:T(8,128)(2,1)S(1)} %pad_maximum_fusion.x_ref), channel_id=1, source_target_pairs={{0,2},{1,5},{2,0},{3,7},{4,6},{5,1},{6,4},{7,3},{8,10},{9,13},{10,... | collective-permute-start | bytes 786440 | tf_op jit(solution)/shard_map/ppermute | solution.py:104
  24.5 3.9 %collective-permute-done.7.x_ref = bf16[8,64,256]{2,1,0:T(8,128)(2,1)S(1)} collective-permute-done((bf16[8,64,256]{2,1,0:T(8,128)(2,1)S(1)}, bf16[8,64,256]{2,1,0:T(8,128)(2,1)S(1)}, u32[]{:S(2)}, u32[]{:S(2)}) %collective-permute-start.7) | collective-permute-done | bytes 262176 | tf_op jit(solution)/shard_map/ppermute | solution.py:104
  29.0 1.2 %collective-permute-done.8.refs_2_ = f32[64,64]{1,0:T(8,128)S(1)} collective-permute-done((f32[64,64]{1,0:T(8,128)S(1)}, f32[64,64]{1,0:T(8,128)S(1)}, u32[]{:S(2)}, u32[]{:S(2)}) %collective-permute-start.8) | collective-permute-done | bytes 16416 | tf_op jit(solution)/shard_map/ppermute | solution.py:104
  30.6 1.5 %collective-permute-start.11 = (bf16[8,64,256]{2,1,0:T(8,128)(2,1)S(1)}, bf16[8,64,256]{2,1,0:T(8,128)(2,1)S(1)}, u32[]{:S(2)}, u32[]{:S(2)}) collective-permute-start(bf16[8,64,256]{2,1,0:T(8,128)(2,1)S(1)} %expand.5), channel_id=1, source_target_pairs={{0,2},{1,5},{2,0},{3,7},{4,6},{5,1},{6,4},{7,3},{8,10},{9,13},{10,... | collective-permute-start | bytes 786440 | tf_op jit(solution)/shard_map/ppermute | solution.py:104
  33.2 1.2 %collective-permute-done.15.refs_2_ = f32[64,64]{1,0:T(8,128)S(1)} collective-permute-done((f32[64,64]{1,0:T(8,128)S(1)}, f32[64,64]{1,0:T(8,128)S(1)}, u32[]{:S(2)}, u32[]{:S(2)}) %collective-permute-start.15) | collective-permute-done | bytes 16416 | tf_op jit(solution)/shard_map/ppermute | solution.py:104
  36.1 0.9 %collective-permute-done.11 = bf16[8,64,256]{2,1,0:T(8,128)(2,1)S(1)} collective-permute-done((bf16[8,64,256]{2,1,0:T(8,128)(2,1)S(1)}, bf16[8,64,256]{2,1,0:T(8,128)(2,1)S(1)}, u32[]{:S(2)}, u32[]{:S(2)}) %collective-permute-start.11) | collective-permute-done | bytes 262176 | tf_op jit(solution)/shard_map/ppermute | solution.py:104
  37.9 4.7 %collective-permute-done.16 = bf16[8,64,256]{2,1,0:T(8,128)(2,1)S(1)} collective-permute-done((bf16[8,64,256]{2,1,0:T(8,128)(2,1)S(1)}, bf16[8,64,256]{2,1,0:T(8,128)(2,1)S(1)}, u32[]{:S(2)}, u32[]{:S(2)}) %collective-permute-start.16) | collective-permute-done | bytes 262176 | tf_op jit(solution)/shard_map/ppermute | solution.py:104
  42.7 0.9 %collective-permute-start.17 = (bf16[4,64,256]{2,1,0:T(8,128)(2,1)S(1)}, bf16[4,64,256]{2,1,0:T(8,128)(2,1)S(1)}, u32[]{:S(2)}, u32[]{:S(2)}) collective-permute-start(bf16[4,64,256]{2,1,0:T(8,128)(2,1)S(1)} %slice.84), channel_id=1, source_target_pairs={{0,4},{1,3},{2,6},{3,1},{4,0},{5,7},{6,2},{7,5},{8,12},{9,11},{10,... | collective-permute-start | bytes 393224 | tf_op jit(solution)/shard_map/ppermute | solution.py:104
  43.6 1.3 %collective-permute-start.13 = (bf16[2,64,256]{2,1,0:T(8,128)(2,1)S(1)}, bf16[2,64,256]{2,1,0:T(8,128)(2,1)S(1)}, u32[]{:S(2)}, u32[]{:S(2)}) collective-permute-start(bf16[2,64,256]{2,1,0:T(8,128)(2,1)S(1)} %slice.87), channel_id=1, source_target_pairs={{0,8},{1,9},{2,10},{3,11},{4,12},{5,13},{6,14},{7,15},{8,0},{9,1},... | collective-permute-start | bytes 196616 | tf_op jit(solution)/shard_map/ppermute | solution.py:104
  44.9 2.8 %collective-permute-done.17 = bf16[4,64,256]{2,1,0:T(8,128)(2,1)S(1)} collective-permute-done((bf16[4,64,256]{2,1,0:T(8,128)(2,1)S(1)}, bf16[4,64,256]{2,1,0:T(8,128)(2,1)S(1)}, u32[]{:S(2)}, u32[]{:S(2)}) %collective-permute-start.17) | collective-permute-done | bytes 131104 | tf_op jit(solution)/shard_map/ppermute | solution.py:104
  47.8 1.6 %collective-permute-start.18 = (bf16[2,64,256]{2,1,0:T(8,128)(2,1)S(1)}, bf16[2,64,256]{2,1,0:T(8,128)(2,1)S(1)}, u32[]{:S(2)}, u32[]{:S(2)}) collective-permute-start(bf16[2,64,256]{2,1,0:T(8,128)(2,1)S(1)} %slice.86), channel_id=1, source_target_pairs={{0,8},{1,9},{2,10},{3,11},{4,12},{5,13},{6,14},{7,15},{8,0},{9,1},... | collective-permute-start | bytes 196616 | tf_op jit(solution)/shard_map/ppermute | solution.py:104
  49.4 1.9 %collective-permute-start.19 = (bf16[1,64,256]{2,1,0:T(8,128)(2,1)S(1)}, bf16[1,64,256]{2,1,0:T(8,128)(2,1)S(1)}, u32[]{:S(2)}, u32[]{:S(2)}) collective-permute-start(bf16[1,64,256]{2,1,0:T(8,128)(2,1)S(1)} %slice.89), channel_id=1, source_target_pairs={{0,16},{1,17},{2,18},{3,19},{4,20},{5,21},{6,22},{7,23},{8,24},{9,... | collective-permute-start | bytes 98312 | tf_op jit(solution)/shard_map/ppermute | solution.py:104
  52.1 2.6 %collective-permute-start.20 = (bf16[1,64,256]{2,1,0:T(8,128)(2,1)S(1)}, bf16[1,64,256]{2,1,0:T(8,128)(2,1)S(1)}, u32[]{:S(2)}, u32[]{:S(2)}) collective-permute-start(bf16[1,64,256]{2,1,0:T(8,128)(2,1)S(1)} %slice.88), channel_id=1, source_target_pairs={{0,16},{1,17},{2,18},{3,19},{4,20},{5,21},{6,22},{7,23},{8,24},{9,... | collective-permute-start | bytes 98312 | tf_op jit(solution)/shard_map/ppermute | solution.py:104
  54.8 2.2 %collective-permute-done.20.refs_4_ = bf16[1,64,256]{2,1,0:T(8,128)(2,1)S(1)} collective-permute-done((bf16[1,64,256]{2,1,0:T(8,128)(2,1)S(1)}, bf16[1,64,256]{2,1,0:T(8,128)(2,1)S(1)}, u32[]{:S(2)}, u32[]{:S(2)}) %collective-permute-start.20) | collective-permute-done | bytes 32800 | tf_op jit(solution)/shard_map/ppermute | solution.py:104
  (57 shorter events, 9.7 us)
Async XLA Ops:
  1.1 6.9 %collective-permute-start = (bf16[1,64,256]{2,1,0:T(8,128)(2,1)S(1)}, bf16[1,64,256]{2,1,0:T(8,128)(2,1)S(1)}, u32[]{:S(2)}, u32[]{:S(2)}) collective-permute-start(bf16[1,64,256]{2,1,0:T(8,128)(2,1)S(1)} %bitcast.7), channel_id=1, source_target_pairs={{0,16},{1,17},{2,18},{3,19},{4,20},{5,21},{6,22},{7,23},{8,24},{9,... | collective-permute-start | bytes 98312 | tf_op jit(solution)/shard_map/ppermute | solution.py:104
  5.2 4.8 %collective-permute-start.2 = (bf16[1,64,256]{2,1,0:T(8,128)(2,1)S(1)}, bf16[1,64,256]{2,1,0:T(8,128)(2,1)S(1)}, u32[]{:S(2)}, u32[]{:S(2)}) collective-permute-start(bf16[1,64,256]{2,1,0:T(8,128)(2,1)S(1)} %bitcast.11), channel_id=1, source_target_pairs={{0,16},{1,17},{2,18},{3,19},{4,20},{5,21},{6,22},{7,23},{8,24},{9,... | collective-permute-start | bytes 98312 | tf_op jit(solution)/shard_map/ppermute | solution.py:104
  8.1 5.0 %collective-permute-start.1 = (bf16[2,64,256]{2,1,0:T(8,128)(2,1)S(1)}, bf16[2,64,256]{2,1,0:T(8,128)(2,1)S(1)}, u32[]{:S(2)}, u32[]{:S(2)}) collective-permute-start(bf16[2,64,256]{2,1,0:T(8,128)(2,1)S(1)} %pad_maximum_fusion.4), channel_id=1, source_target_pairs={{0,8},{1,9},{2,10},{3,11},{4,12},{5,13},{6,14},{7,15},{8,0},{9,1},... | collective-permute-start | bytes 196616 | tf_op jit(solution)/shard_map/ppermute | solution.py:104
  10.0 4.6 %collective-permute-start.3 = (bf16[2,64,256]{2,1,0:T(8,128)(2,1)S(1)}, bf16[2,64,256]{2,1,0:T(8,128)(2,1)S(1)}, u32[]{:S(2)}, u32[]{:S(2)}) collective-permute-start(bf16[2,64,256]{2,1,0:T(8,128)(2,1)S(1)} %pad_maximum_fusion.5), channel_id=1, source_target_pairs={{0,8},{1,9},{2,10},{3,11},{4,12},{5,13},{6,14},{7,15},{8,0},{9,1},... | collective-permute-start | bytes 196616 | tf_op jit(solution)/shard_map/ppermute | solution.py:104
  13.1 7.3 %collective-permute-start.4 = (bf16[4,64,256]{2,1,0:T(8,128)(2,1)S(1)}, bf16[4,64,256]{2,1,0:T(8,128)(2,1)S(1)}, u32[]{:S(2)}, u32[]{:S(2)}) collective-permute-start(bf16[4,64,256]{2,1,0:T(8,128)(2,1)S(1)} %pad_maximum_fusion.2), channel_id=1, source_target_pairs={{0,4},{1,3},{2,6},{3,1},{4,0},{5,7},{6,2},{7,5},{8,12},{9,11},{10,... | collective-permute-start | bytes 393224 | tf_op jit(solution)/shard_map/ppermute | solution.py:104
  14.7 5.7 %collective-permute-start.5 = (bf16[4,64,256]{2,1,0:T(8,128)(2,1)S(1)}, bf16[4,64,256]{2,1,0:T(8,128)(2,1)S(1)}, u32[]{:S(2)}, u32[]{:S(2)}) collective-permute-start(bf16[4,64,256]{2,1,0:T(8,128)(2,1)S(1)} %pad_maximum_fusion.3), channel_id=1, source_target_pairs={{0,4},{1,3},{2,6},{3,1},{4,0},{5,7},{6,2},{7,5},{8,12},{9,11},{10,... | collective-permute-start | bytes 393224 | tf_op jit(solution)/shard_map/ppermute | solution.py:104
  16.7 3.8 %copy-start = (bf16[256,8192]{1,0:T(8,128)(2,1)S(1)}, bf16[256,8192]{1,0:T(8,128)(2,1)}, u32[]{:S(2)}) copy-start(bf16[256,8192]{1,0:T(8,128)(2,1)} %refs_3_.1) | copy-start | bytes 12582916
  19.8 9.2 %collective-permute-start.10 = (bf16[16,128,256]{2,1,0:T(8,128)(2,1)S(1)}, bf16[16,128,256]{2,1,0:T(8,128)(2,1)S(1)}, u32[]{:S(2)}, u32[]{:S(2)}) collective-permute-start(bf16[16,128,256]{2,1,0:T(8,128)(2,1)S(1)} %get-tuple-element.38), channel_id=1, source_target_pairs={{0,1},{1,0},{2,3},{3,2},{4,5},{5,4},{6,7},{7,6},{8,9},{9,8},{10,11... | collective-permute-start | bytes 3145736 | tf_op jit(solution)/shard_map/ppermute | solution.py:104
  19.9 4.1 %collective-permute-start.6 = (bf16[16,128,256]{2,1,0:T(8,128)(2,1)S(1)}, bf16[16,128,256]{2,1,0:T(8,128)(2,1)S(1)}, u32[]{:S(2)}, u32[]{:S(2)}) collective-permute-start(bf16[16,128,256]{2,1,0:T(8,128)(2,1)S(1)} %get-tuple-element.29), channel_id=1, source_target_pairs={{0,1},{1,0},{2,3},{3,2},{4,5},{5,4},{6,7},{7,6},{8,9},{9,8},{10,11... | collective-permute-start | bytes 3145736 | tf_op jit(solution)/shard_map/ppermute | solution.py:104
  21.9 8.3 %collective-permute-start.9 = (bf16[16,128,256]{2,1,0:T(8,128)(2,1)S(1)}, bf16[16,128,256]{2,1,0:T(8,128)(2,1)S(1)}, u32[]{:S(2)}, u32[]{:S(2)}) collective-permute-start(bf16[16,128,256]{2,1,0:T(8,128)(2,1)S(1)} %get-tuple-element.33), channel_id=1, source_target_pairs={{0,1},{1,0},{2,3},{3,2},{4,5},{5,4},{6,7},{7,6},{8,9},{9,8},{10,11... | collective-permute-start | bytes 3145736 | tf_op jit(solution)/shard_map/ppermute | solution.py:104
  22.0 6.4 %collective-permute-start.7 = (bf16[8,64,256]{2,1,0:T(8,128)(2,1)S(1)}, bf16[8,64,256]{2,1,0:T(8,128)(2,1)S(1)}, u32[]{:S(2)}, u32[]{:S(2)}) collective-permute-start(bf16[8,64,256]{2,1,0:T(8,128)(2,1)S(1)} %pad_maximum_fusion.x_ref), channel_id=1, source_target_pairs={{0,2},{1,5},{2,0},{3,7},{4,6},{5,1},{6,4},{7,3},{8,10},{9,13},{10,... | collective-permute-start | bytes 786440 | tf_op jit(solution)/shard_map/ppermute | solution.py:104
  23.5 9.1 %collective-permute-start.14 = (bf16[8,64,256]{2,1,0:T(8,128)(2,1)S(1)}, bf16[8,64,256]{2,1,0:T(8,128)(2,1)S(1)}, u32[]{:S(2)}, u32[]{:S(2)}) collective-permute-start(bf16[8,64,256]{2,1,0:T(8,128)(2,1)S(1)} %pad_maximum_fusion.1.x_ref), channel_id=1, source_target_pairs={{0,2},{1,5},{2,0},{3,7},{4,6},{5,1},{6,4},{7,3},{8,10},{9,13},{10,... | collective-permute-start | bytes 786440 | tf_op jit(solution)/shard_map/ppermute | solution.py:104
  28.9 1.3 %collective-permute-start.8 = (f32[64,64]{1,0:T(8,128)S(1)}, f32[64,64]{1,0:T(8,128)S(1)}, u32[]{:S(2)}, u32[]{:S(2)}) collective-permute-start(f32[64,64]{1,0:T(8,128)S(1)} %shrink.2.refs_1_), channel_id=1, source_target_pairs={{0,1},{1,0},{2,3},{3,2},{4,5},{5,4},{6,7},{7,6},{8,9},{9,8},{10,11... | collective-permute-start | bytes 49160 | tf_op jit(solution)/shard_map/ppermute | solution.py:104
  30.6 6.4 %collective-permute-start.11 = (bf16[8,64,256]{2,1,0:T(8,128)(2,1)S(1)}, bf16[8,64,256]{2,1,0:T(8,128)(2,1)S(1)}, u32[]{:S(2)}, u32[]{:S(2)}) collective-permute-start(bf16[8,64,256]{2,1,0:T(8,128)(2,1)S(1)} %expand.5), channel_id=1, source_target_pairs={{0,2},{1,5},{2,0},{3,7},{4,6},{5,1},{6,4},{7,3},{8,10},{9,13},{10,... | collective-permute-start | bytes 786440 | tf_op jit(solution)/shard_map/ppermute | solution.py:104
  33.1 1.3 %collective-permute-start.15 = (f32[64,64]{1,0:T(8,128)S(1)}, f32[64,64]{1,0:T(8,128)S(1)}, u32[]{:S(2)}, u32[]{:S(2)}) collective-permute-start(f32[64,64]{1,0:T(8,128)S(1)} %shrink.3.refs_1_), channel_id=1, source_target_pairs={{0,1},{1,0},{2,3},{3,2},{4,5},{5,4},{6,7},{7,6},{8,9},{9,8},{10,11... | collective-permute-start | bytes 49160 | tf_op jit(solution)/shard_map/ppermute | solution.py:104
  34.7 7.8 %collective-permute-start.16 = (bf16[8,64,256]{2,1,0:T(8,128)(2,1)S(1)}, bf16[8,64,256]{2,1,0:T(8,128)(2,1)S(1)}, u32[]{:S(2)}, u32[]{:S(2)}) collective-permute-start(bf16[8,64,256]{2,1,0:T(8,128)(2,1)S(1)} %expand.7), channel_id=1, source_target_pairs={{0,2},{1,5},{2,0},{3,7},{4,6},{5,1},{6,4},{7,3},{8,10},{9,13},{10,... | collective-permute-start | bytes 786440 | tf_op jit(solution)/shard_map/ppermute | solution.py:104
  37.1 6.5 %collective-permute-start.12 = (bf16[4,64,256]{2,1,0:T(8,128)(2,1)S(1)}, bf16[4,64,256]{2,1,0:T(8,128)(2,1)S(1)}, u32[]{:S(2)}, u32[]{:S(2)}) collective-permute-start(bf16[4,64,256]{2,1,0:T(8,128)(2,1)S(1)} %slice.85), channel_id=1, source_target_pairs={{0,4},{1,3},{2,6},{3,1},{4,0},{5,7},{6,2},{7,5},{8,12},{9,11},{10,... | collective-permute-start | bytes 393224 | tf_op jit(solution)/shard_map/ppermute | solution.py:104
  42.7 5.0 %collective-permute-start.17 = (bf16[4,64,256]{2,1,0:T(8,128)(2,1)S(1)}, bf16[4,64,256]{2,1,0:T(8,128)(2,1)S(1)}, u32[]{:S(2)}, u32[]{:S(2)}) collective-permute-start(bf16[4,64,256]{2,1,0:T(8,128)(2,1)S(1)} %slice.84), channel_id=1, source_target_pairs={{0,4},{1,3},{2,6},{3,1},{4,0},{5,7},{6,2},{7,5},{8,12},{9,11},{10,... | collective-permute-start | bytes 393224 | tf_op jit(solution)/shard_map/ppermute | solution.py:104
  43.6 5.8 %collective-permute-start.13 = (bf16[2,64,256]{2,1,0:T(8,128)(2,1)S(1)}, bf16[2,64,256]{2,1,0:T(8,128)(2,1)S(1)}, u32[]{:S(2)}, u32[]{:S(2)}) collective-permute-start(bf16[2,64,256]{2,1,0:T(8,128)(2,1)S(1)} %slice.87), channel_id=1, source_target_pairs={{0,8},{1,9},{2,10},{3,11},{4,12},{5,13},{6,14},{7,15},{8,0},{9,1},... | collective-permute-start | bytes 196616 | tf_op jit(solution)/shard_map/ppermute | solution.py:104
  47.8 4.3 %collective-permute-start.18 = (bf16[2,64,256]{2,1,0:T(8,128)(2,1)S(1)}, bf16[2,64,256]{2,1,0:T(8,128)(2,1)S(1)}, u32[]{:S(2)}, u32[]{:S(2)}) collective-permute-start(bf16[2,64,256]{2,1,0:T(8,128)(2,1)S(1)} %slice.86), channel_id=1, source_target_pairs={{0,8},{1,9},{2,10},{3,11},{4,12},{5,13},{6,14},{7,15},{8,0},{9,1},... | collective-permute-start | bytes 196616 | tf_op jit(solution)/shard_map/ppermute | solution.py:104
  49.4 5.3 %collective-permute-start.19 = (bf16[1,64,256]{2,1,0:T(8,128)(2,1)S(1)}, bf16[1,64,256]{2,1,0:T(8,128)(2,1)S(1)}, u32[]{:S(2)}, u32[]{:S(2)}) collective-permute-start(bf16[1,64,256]{2,1,0:T(8,128)(2,1)S(1)} %slice.89), channel_id=1, source_target_pairs={{0,16},{1,17},{2,18},{3,19},{4,20},{5,21},{6,22},{7,23},{8,24},{9,... | collective-permute-start | bytes 98312 | tf_op jit(solution)/shard_map/ppermute | solution.py:104
  52.1 4.9 %collective-permute-start.20 = (bf16[1,64,256]{2,1,0:T(8,128)(2,1)S(1)}, bf16[1,64,256]{2,1,0:T(8,128)(2,1)S(1)}, u32[]{:S(2)}, u32[]{:S(2)}) collective-permute-start(bf16[1,64,256]{2,1,0:T(8,128)(2,1)S(1)} %slice.88), channel_id=1, source_target_pairs={{0,16},{1,17},{2,18},{3,19},{4,20},{5,21},{6,22},{7,23},{8,24},{9,... | collective-permute-start | bytes 98312 | tf_op jit(solution)/shard_map/ppermute | solution.py:104

commit v3 on v2

v3 whole, which is shorter than its diff:
```python
import jax
import jax.numpy as jnp
from jax import lax
from jax.experimental import pallas as pl
from jax.experimental.pallas import tpu as pltpu
from jax.sharding import PartitionSpec as P

BLOCK = 4


ADAPTER_SCALE = 2.0

PICKED = 2

VMEM_LIMIT = 16 * 1024 * 1024


def segment_member(segment_rows, total_rows, block_rows):
    padded = (segment_rows + block_rows - 1) // block_rows * block_rows
    starts = jnp.cumsum(padded) - padded
    row_ids = jnp.arange(total_rows, dtype=jnp.int32)
    inside = (row_ids[:, None] >= starts[None, :]) & (
        row_ids[:, None] < (starts + segment_rows)[None, :]
    )
    return inside.astype(jnp.float32)


def slot_lookup(store_adapter_ids, segment_adapter):
    positions = jnp.arange(store_adapter_ids.shape[0], dtype=jnp.int32)
    equal = store_adapter_ids[None, :] == segment_adapter[:, None]
    return jnp.sum(jnp.where(equal, positions[None, :], 0), axis=1)


def tile_side(
    attention_output,
    output_weight,
    down_weight,
    up_weight,
    store_adapter_ids,
    segment_adapter,
    segment_rows,
):
    device_list = lax.axis_size("replica")
    total_rows, feature_columns = attention_output.shape
    holding_count, hidden_width, adapter_rank_size = down_weight.shape
    seg_count = segment_rows.shape[0]
    member = segment_member(segment_rows, total_rows, BLOCK)
    active_rows = jnp.sum(member, axis=1)
    slot_for_adapter = slot_lookup(store_adapter_ids, segment_adapter)
    partial_value = jnp.dot(attention_output, output_weight, preferred_element_type=jnp.float32)
    down_pieces = down_weight.reshape(
        holding_count, device_list, feature_columns, adapter_rank_size
    )
    up_pieces = up_weight.reshape(holding_count, device_list, feature_columns, adapter_rank_size)
    tile_pairs = jnp.concatenate([down_pieces, up_pieces], axis=3)
    arrived = lax.all_to_all(tile_pairs, "replica", split_axis=1, concat_axis=0, tiled=True)
    arrived = arrived.reshape(-1, feature_columns, 2 * adapter_rank_size)
    seg_tiles = arrived[slot_for_adapter]
    a_part = seg_tiles[:, :, :adapter_rank_size]
    b_part = seg_tiles[:, :, adapter_rank_size:]
    a_matrix = jnp.transpose(a_part, (1, 0, 2)).reshape(
        feature_columns, seg_count * adapter_rank_size
    )
    shrink_all = jnp.dot(attention_output, a_matrix, preferred_element_type=jnp.float32)
    shrink_all = shrink_all.reshape(total_rows, seg_count, adapter_rank_size)
    shrink_part = jnp.einsum("ps,psr->pr", member, shrink_all)
    base_column_block = lax.psum_scatter(partial_value, "replica", scatter_dimension=1, tiled=True)
    shrink = lax.psum(shrink_part, "replica")
    shrink_half = shrink.astype(jnp.bfloat16)
    spread = (member[:, :, None] * shrink_half.astype(jnp.float32)[:, None, :]).astype(jnp.bfloat16)
    spread = spread.reshape(total_rows, seg_count * adapter_rank_size)
    b_matrix = jnp.transpose(b_part, (0, 2, 1)).reshape(
        seg_count * adapter_rank_size, feature_columns
    )
    adapter_column_block = jnp.dot(spread, b_matrix, preferred_element_type=jnp.float32)
    mixed = active_rows[:, None] * (base_column_block + ADAPTER_SCALE * adapter_column_block)
    return mixed.astype(jnp.bfloat16)


def stage_masks(device_count):
    masks = []
    mask = device_count // 2
    while mask >= 2:
        masks.append(mask)
        mask //= 2
    other = list(masks)
    if len(other) >= 2:
        other[-1], other[-2] = other[-2], other[-1]
    return masks, other


def stage_groups(even, odd):
    pairs = list(zip(even, odd))
    groups = [pairs[:2]] + [[pair] for pair in pairs[2:]] if len(pairs) > 2 else [[p] for p in pairs]
    found = []
    for group in groups:
        masks = [(0, 0)]
        for even_mask, odd_mask in group:
            masks = masks + [(a ^ even_mask, b ^ odd_mask) for a, b in masks]
        found.append(masks[1:])
    return found


def chain_rows(live_rows):
    return live_rows - live_rows // 2, live_rows // 2


def position_masks(masks):
    found = [0]
    for mask in masks:
        found = found + [value ^ mask for value in found]
    return found


def exchange(value, mask_even, mask_odd):
    count = lax.axis_size("replica")
    pairs = [(i, i ^ (mask_odd if i & 1 else mask_even)) for i in range(count)]
    return lax.ppermute(value, "replica", pairs)


def block_at(device, position, tables):
    even, odd = tables[0][position], tables[1][position]
    if even == odd:
        return jnp.bitwise_xor(device, even)
    return jnp.bitwise_xor(device, jnp.where(jnp.bitwise_and(device, 1) == 0, even, odd))


def padded_row(live_row, rows_ref):
    place = live_row
    end = jnp.int32(0)
    for s in range(rows_ref.shape[0]):
        count = rows_ref[s]
        gap = (BLOCK - count % BLOCK) % BLOCK
        end = end + count
        place = place + jnp.where(live_row >= end, gap, 0)
    return place


def compact_kernel(rows_hbm, x_hbm, wanted_hbm, store_hbm, *refs):
    out_ref, pick_ref, code_ref, slot_ref, rows_ref, x_ref, wanted_ref, store_ref, sems = refs
    rows_copy, x_copy, wanted_copy, store_copy = (
        pltpu.make_async_copy(source, target, sems.at[i])
        for i, (source, target) in enumerate(
            (
                (rows_hbm, rows_ref),
                (x_hbm, x_ref),
                (wanted_hbm, wanted_ref),
                (store_hbm, store_ref),
            )
        )
    )
    for copy in (rows_copy, x_copy, wanted_copy, store_copy):
        copy.start()
    rows_copy.wait()
    shape = (out_ref.shape[0], x_ref.shape[0])
    live_row = lax.broadcasted_iota(jnp.int32, shape, 0)
    layout_row = lax.broadcasted_iota(jnp.int32, shape, 1)
    pick = jnp.where(padded_row(live_row, rows_ref) == layout_row, 1.0, 0.0).astype(jnp.bfloat16)
    x_copy.wait()
    rows = jnp.dot(pick, x_ref[...], preferred_element_type=jnp.float32)
    out_ref[...] = rows.astype(jnp.bfloat16)
    shape = pick_ref.shape
    live_row = lax.broadcasted_iota(jnp.int32, shape, 1)
    layout_row = lax.broadcasted_iota(jnp.int32, shape, 0)
    back = padded_row(live_row, rows_ref) == layout_row
    pick_ref[...] = jnp.where(back, 1.0, 0.0).astype(jnp.bfloat16)
    live_row = lax.broadcasted_iota(jnp.int32, code_ref.shape, 0)
    segment = jnp.zeros(code_ref.shape, jnp.int32)
    end = jnp.int32(0)
    for s in range(rows_ref.shape[0] - 1):
        end = end + rows_ref[s]
        segment = segment + jnp.where(live_row >= end, 1, 0)
    code_ref[...] = segment
    wanted_copy.wait()
    store_copy.wait()
    shape = (wanted_ref.shape[0], store_ref.shape[1])
    row = lax.broadcasted_iota(jnp.int32, shape, 0)
    lane = lax.broadcasted_iota(jnp.int32, shape, 1)
    wanted = jnp.zeros(shape, jnp.int32)
    for s in range(shape[0]):
        wanted = jnp.where(row == s, wanted_ref[s], wanted)
    found = jnp.where(store_ref[...] == wanted, lane, 0).astype(jnp.float32)
    slot_ref[...] = jnp.broadcast_to(jnp.sum(found, axis=1, keepdims=True), slot_ref.shape)


def spread_rows_kernel(chains, pick_ref, *refs):
    keep_refs, got_refs, out_ref = refs[:chains], refs[chains:-1], refs[-1]
    each = len(got_refs) // chains
    live = []
    for i, keep_ref in enumerate(keep_refs):
        total = keep_ref[0]
        for got_ref in got_refs[i * each : (i + 1) * each]:
            total = total + got_ref[0].astype(jnp.float32)
        live.append(total.astype(jnp.bfloat16))
    mixed = live[0] if chains == 1 else jnp.concatenate(live, axis=0)
    out = jnp.dot(pick_ref[...], mixed, preferred_element_type=jnp.float32)
    out_ref[...] = out.astype(jnp.bfloat16)


def find_kernel(held, me_ref, slot_ref, segment_ref, info_ref, code_ref):
    me = me_ref[0]
    segs = slot_ref.shape[0]
    slot = slot_ref[:, :1]
    place = jnp.zeros((segs, 1), jnp.float32)
    for first, device in ((0, me), (PICKED, jnp.bitwise_xor(me, 1))):
        local = slot - (device * held).astype(jnp.float32)
        here = (local >= 0.0) & (local < held)
        low = jnp.minimum(jnp.min(jnp.where(here, local, float(held))), held - 1.0)
        place = jnp.where(here, jnp.where(local == low, first + 1.0, first + 2.0), place)
        if first == 0:
            info_ref[0] = me
            info_ref[1] = low.astype(jnp.int32)
            info_ref[2] = jnp.max(jnp.where(here, local, 0.0)).astype(jnp.int32)
    segment = segment_ref[...]
    code = jnp.zeros(segment.shape, jnp.float32)
    for s in range(segs):
        code = jnp.where(segment == s, place[s : s + 1, :], code)
    code_ref[...] = code


def base_kernel(tables, me_ref, x_ref, w_hbm, send_ref, keep_ref, w_ref, sems):
    me = me_ref[0]
    peer = jnp.bitwise_xor(me, 1)
    parts, group_width = w_ref.shape[0], w_ref.shape[2]
    width = x_ref.shape[1]
    group = group_width // width
    copies = []
    for g in range(parts):
        at = pl.multiple_of(jnp.bitwise_xor(me // group, g) * group_width, group_width)
        copies.append(
            pltpu.make_async_copy(w_hbm.at[:, pl.ds(at, group_width)], w_ref.at[g], sems.at[g])
        )
        copies[-1].start()
    x = x_ref[...]
    for g in range(parts):
        copies[g].wait()
        for p in range(len(tables[0])):
            if tables[0][p] // group != g:
                continue
            for device, out_ref in ((peer, send_ref), (me, keep_ref)):
                at = pl.multiple_of(block_at(device, p, tables) % group * width, width)
                part = jnp.dot(
                    x, w_ref[g, :, pl.ds(at, width)], preferred_element_type=jnp.float32
                )
                out_ref[p] = part.astype(out_ref.dtype)


def tiles_kernel(tables, info_ref, *refs):
    stores, outs, held_ref, sems = refs[:2], refs[2:6], refs[6], refs[7]
    me = info_ref[0]
    peer = jnp.bitwise_xor(me, 1)
    width = outs[0].shape[2]
    rank = stores[0].shape[1]
    copies = []
    for k, store in enumerate(stores):
        for j in range(PICKED):
            at = PICKED * k + j
            copies.append(
                pltpu.make_async_copy(store.at[info_ref[1 + j]], held_ref.at[at], sems.at[at])
            )
            copies[-1].start()
    for at, copy in enumerate(copies):
        copy.wait()
        k, j = at // PICKED, at % PICKED
        for p in range(len(tables[0])):
            for device, out in ((peer, outs[2 * k]), (me, outs[2 * k + 1])):
                lane = pl.multiple_of(block_at(device, p, tables) * width, width)
                out[p, j * rank : (j + 1) * rank, :] = held_ref[at, :, pl.ds(lane, width)]


def shrink_sums(places, x_ref, own_ref, peer_ref, own, peer):
    contract = (((1,), (1,)), ((), ()))
    for p, at in enumerate(places):
        x = x_ref[p]
        own = own + lax.dot_general(x, own_ref[at], contract, preferred_element_type=jnp.float32)
        peer = peer + lax.dot_general(x, peer_ref[at], contract, preferred_element_type=jnp.float32)
    return own, peer


def shrink_start_kernel(places, x_ref, own_ref, peer_ref, out_ref):
    zero = jnp.zeros(out_ref.shape[1:], jnp.float32)
    out_ref[0], out_ref[1] = shrink_sums(places, x_ref, own_ref, peer_ref, zero, zero)


def shrink_kernel(row, places, code_ref, sums_ref, x_ref, own_ref, peer_ref, out_ref):
    rows, rank = out_ref.shape
    sums = shrink_sums(places, x_ref, own_ref, peer_ref, sums_ref[0], sums_ref[1])
    code = code_ref[row : row + rows, :]
    total = jnp.zeros((rows, rank), jnp.float32)
    for place, part in enumerate(sums):
        for j in range(PICKED):
            value = part[:, j * rank : (j + 1) * rank]
            total = total + jnp.where(code == 1 + place * PICKED + j, value, 0.0)
    out_ref[...] = total


def expand_kernel(
    row, places, code_ref, mine_ref, got_ref, keep_ref, base_ref, own_ref, peer_ref, out_ref
):
    rows = out_ref.shape[1]
    half = (mine_ref[...] + got_ref[...]).astype(jnp.bfloat16)
    code = code_ref[row : row + rows, :]
    picked = [
        jnp.where(code == 1 + j, half.astype(jnp.float32), 0.0).astype(jnp.bfloat16)
        for j in range(2 * PICKED)
    ]
    own = jnp.concatenate(picked[:PICKED], axis=1)
    peer = jnp.concatenate(picked[PICKED:], axis=1)
    for p, at in enumerate(places):
        term = jnp.dot(own, own_ref[at], preferred_element_type=jnp.float32)
        term = term + jnp.dot(peer, peer_ref[at], preferred_element_type=jnp.float32)
        base = keep_ref[at, row : row + rows] + base_ref[at, row : row + rows].astype(jnp.float32)
        out_ref[p] = (base + ADAPTER_SCALE * term).astype(out_ref.dtype)


def after(values, *earlier):
    return lax.optimization_barrier((values, earlier))[0]


def smem():
    return pl.BlockSpec(memory_space=pltpu.SMEM)


def vmem():
    return pl.BlockSpec(memory_space=pltpu.VMEM)


def in_hbm(value):
    return pltpu.with_memory_space_constraint(value, pltpu.HBM)


def params(**more):
    return pltpu.CompilerParams(vmem_limit_bytes=VMEM_LIMIT, **more)


def owner_side(
    attention_output,
    output_weight,
    down_weight,
    up_weight,
    store_adapter_ids,
    segment_adapter,
    segment_rows,
):
    bf16, f32 = jnp.bfloat16, jnp.float32
    device_count = lax.axis_size("replica")
    me = lax.axis_index("replica")
    total_rows, width = attention_output.shape
    held, _, rank = down_weight.shape
    seg_count = segment_rows.shape[0]
    live_rows = total_rows - seg_count * (BLOCK - 1)
    sizes = chain_rows(live_rows)
    chains = len(sizes)
    starts = [sum(sizes[:i]) for i in range(chains)]
    even_masks, odd_masks = stage_masks(device_count)
    tables = (position_masks(even_masks), position_masks(odd_masks))
    positions = len(tables[0])
    half = positions // 2
    groups = stage_groups(even_masks, odd_masks)

    me = jnp.reshape(me, (1,))

    hbm = pl.BlockSpec(memory_space=pltpu.HBM)
    live, pick, segment, slots = pl.pallas_call(
        compact_kernel,
        out_shape=[
            jax.ShapeDtypeStruct((live_rows, width), bf16),
            jax.ShapeDtypeStruct((total_rows, live_rows), bf16),
            jax.ShapeDtypeStruct((live_rows, rank), jnp.int32),
            jax.ShapeDtypeStruct((seg_count, 128), f32),
        ],
        in_specs=[hbm] * 4,
        out_specs=[vmem()] * 4,
        scratch_shapes=[
            pltpu.SMEM(segment_rows.shape, jnp.int32),
            pltpu.VMEM(attention_output.shape, bf16),
            pltpu.SMEM(segment_adapter.shape, jnp.int32),
            pltpu.VMEM((1, store_adapter_ids.shape[0]), jnp.int32),
            pltpu.SemaphoreType.DMA((4,)),
        ],
        compiler_params=params(),
        name="compact_rows",
    )(
        in_hbm(segment_rows),
        in_hbm(attention_output),
        in_hbm(segment_adapter),
        in_hbm(jnp.reshape(store_adapter_ids, (1, -1))),
    )

    info, code = pl.pallas_call(
        lambda *refs: find_kernel(held, *refs),
        out_shape=[
            jax.ShapeDtypeStruct((1 + PICKED,), jnp.int32),
            jax.ShapeDtypeStruct((live_rows, rank), f32),
        ],
        in_specs=[smem(), vmem(), vmem()],
        out_specs=[smem(), vmem()],
        compiler_params=params(),
        name="find_adapters",
    )(me, slots, segment)

    def cut_tiles(info):
        return pl.pallas_call(
            lambda *refs: tiles_kernel(tables, *refs),
            out_shape=[jax.ShapeDtypeStruct((positions, PICKED * rank, width), bf16)] * 4,
            in_specs=[smem(), hbm, hbm],
            out_specs=[vmem()] * 4,
            scratch_shapes=[
                pltpu.VMEM((2 * PICKED, rank, down_weight.shape[1]), bf16),
                pltpu.SemaphoreType.DMA((2 * PICKED,)),
            ],
            compiler_params=params(),
            name="cut_tiles",
        )(
            info,
            in_hbm(jnp.transpose(down_weight, (0, 2, 1))),
            in_hbm(jnp.transpose(up_weight, (0, 2, 1))),
        )

    def base_partials(me):
        parts = 4
        return pl.pallas_call(
            lambda *refs: base_kernel(tables, *refs),
            out_shape=[
                jax.ShapeDtypeStruct((positions, live_rows, width), bf16),
                jax.ShapeDtypeStruct((positions, live_rows, width), f32),
            ],
            in_specs=[smem(), vmem(), hbm],
            out_specs=[vmem()] * 2,
            scratch_shapes=[
                pltpu.VMEM((parts, width, output_weight.shape[1] // parts), bf16),
                pltpu.SemaphoreType.DMA((parts,)),
            ],
            compiler_params=params(),
            name="base_partials",
        )(me, live, in_hbm(output_weight))

    def shrink_start(i, x):
        return pl.pallas_call(
            lambda *refs: shrink_start_kernel(range(half), *refs),
            out_shape=jax.ShapeDtypeStruct((2, sizes[i], PICKED * rank), f32),
            in_specs=[vmem()] * 3,
            out_specs=vmem(),
            compiler_params=params(),
            name="shrink_start",
        )(x, down_own, down_peer)

    def shrink(i, sums, x):
        return pl.pallas_call(
            lambda *refs: shrink_kernel(starts[i], range(half, positions), *refs),
            out_shape=jax.ShapeDtypeStruct((sizes[i], rank), f32),
            in_specs=[vmem()] * 5,
            out_specs=vmem(),
            compiler_params=params(),
            name="shrink",
        )(code, sums, x, down_own, down_peer)

    def expand(i, part, dtype):
        return pl.pallas_call(
            lambda *refs: expand_kernel(
                starts[i], range(part * half, (part + 1) * half), *refs
            ),
            out_shape=jax.ShapeDtypeStruct((half, sizes[i], width), dtype),
            in_specs=[vmem()] * 7,
            out_specs=vmem(),
            compiler_params=params(),
            name="expand",
        )(code, mine[i], theirs[i], base_keep, base_got, up_own, up_peer)

    def swap(parts, masks):
        return [exchange(part, *mask) for part, mask in zip(parts, masks)]

    stages = len(groups)
    cut_at = max(stages - 2, 0)
    gathered = live[None]
    for k, masks in enumerate(groups):
        before = gathered
        if k < stages - 1:
            got = swap([gathered] * len(masks), masks)
            gathered = jnp.concatenate([gathered, *got], axis=0)
        else:
            gathered = [gathered[:, a : a + n] for a, n in zip(starts, sizes)]
            got = [exchange(part, *masks[0]) for part in gathered]
        if k == 0:
            base_send, base_keep = base_partials(me)
            gathered, base_send = after((gathered, base_send))
            base_got = exchange(base_send, 1, 1)
        if k == cut_at:
            down_send, down_own, up_send, up_own = cut_tiles(after(info, before))
            gathered, down_send, up_send = after((gathered, down_send, up_send))
            down_peer = exchange(down_send, 1, 1)
            up_peer = exchange(up_send, 1, 1)

    sums = [shrink_start(i, part) for i, part in enumerate(gathered)]

    mine, theirs, send = [None] * chains, [None] * chains, [None] * chains
    for i in range(chains):
        last = got[i] if i == 0 else after(got[i], send[i - 1])
        mine[i] = shrink(i, sums[i], last)
        theirs[i] = exchange(mine[i], 1, 1)
        send[i] = expand(i, 1, bf16)
    keep = [expand(i, 0, f32) for i in range(chains)]

    send = [[value] for value in send]
    for k, masks in reversed(list(enumerate(groups))):
        if k < stages - 1:
            total = [a + sum(part.astype(f32) for part in b) for a, b in zip(keep, got)]
            if k == 0:
                total = [jnp.concatenate(total, axis=1)]
            left = total[0].shape[0] // (len(masks) + 1)
            keep = [value[:left] for value in total]
            send = [
                [value[(j + 1) * left : (j + 2) * left].astype(bf16) for j in range(len(masks))]
                for value in total
            ]
        got = [swap(parts, masks) for parts in send]
    return pl.pallas_call(
        lambda *refs: spread_rows_kernel(len(keep), *refs),
        out_shape=jax.ShapeDtypeStruct((total_rows, width), bf16),
        in_specs=[vmem()] * (1 + len(keep) * (1 + len(groups[0]))),
        out_specs=vmem(),
        compiler_params=params(),
        name="spread_rows",
    )(pick, *keep, *[part for parts in got for part in parts])


def per_device(*arrays):
    width, features = arrays[0].shape[1], arrays[1].shape[1]
    if width % 128 == 0 and lax.axis_size("replica") >= 4:
        return owner_side(*arrays)
    return tile_side(*arrays)


def solution(mesh):
    in_specs = (
        P("parts", "replica"),
        P("replica", None),
        P(("parts", "replica"), None, None),
        P(("parts", "replica"), None, None),
        P("parts"),
        P("parts"),
        P("parts"),
    )
    out_specs = P("parts", "replica")
    return jax.shard_map(
        per_device, mesh=mesh, in_specs=in_specs, out_specs=out_specs, check_vma=False
    )
```

time: 58 us -> 54.9 us (0.947)
  starting transfers between devices: 24.8 us -> 20.5 us
  waiting for transfers between devices: 19.1 us -> 22.1 us
  other arithmetic: 2.55 us -> 0.28 us
  Pallas kernels: 9.82 us -> 11.6 us
  between operations: 1.48 us -> 0.23 us
    ppermute x21 -> x18, starting transfers between devices: 24.8 us -> 20.5 us  [exchange(): return lax.ppermute(value, 'replica', pairs)]
    ppermute x21 -> x18, waiting for transfers between devices: 19.1 us -> 22.1 us  [exchange(): return lax.ppermute(value, 'replica', pairs)]
    pallas_call x12 -> x13, Pallas kernels: 9.82 us -> 11.6 us  [the longest x1 2.89 us: cut_tiles(): pl.pallas_call(lambda *refs: tiles_kernel(tables, *refs), out_shape=[jax....]
    reduce_sum x1 -> x0, other arithmetic: 0.85 us -> none  [slot_lookup(): return jnp.sum(jnp.where(equal, positions[None, :], 0), axis=1)]
    reduce_max x1 -> x0, other arithmetic: 0.71 us -> none  [picks(): high = jnp.max(jnp.where(here, local, 0))]
    concatenate x7 -> x3, other arithmetic: 0.8 us -> 0.09 us  [the longest x2 0.08 us: owner_side(): gathered = jnp.concatenate([gathered, *got], axis=0)]
  transfers between devices with their start and end apart: 21 -> 18, of which waited for: 9 -> 12; matrix products, arithmetic and copies ran while one was open for 5% -> 0% of each run, Pallas kernels for 14% -> 17%
where the time goes in v3:
time: 54.9 us; the launch traced here: 54.7 us
  waiting for transfers between devices  22.1 us (40%)
  starting transfers between devices  20.5 us (37%)
  Pallas kernels  11.6 us (21%)
    ppermute x18, waiting for transfers between devices, exchange(): return lax.ppermute(value, 'replica', pairs)  22.1 us
    ppermute x18, starting transfers between devices, exchange(): return lax.ppermute(value, 'replica', pairs)  20.5 us
    pallas_call x1, Pallas kernels, cut_tiles(): pl.pallas_call(lambda *refs: tiles_kernel(tables, *refs), out_shape=[jax....  2.89 us
    pallas_call x1, Pallas kernels, base_partials(): pl.pallas_call(lambda *refs: base_kernel(tables, *refs), out_shape=[jax.S...  2.53 us
    pallas_call x4, Pallas kernels, expand(): pl.pallas_call(lambda *refs: expand_kernel(starts[i], range(part * half,...  1.39 us
    pallas_call x1, Pallas kernels, owner_side(): pl.pallas_call(compact_kernel, out_shape=[jax.ShapeDtypeStruct((live_rows...  1.22 us
  transfers between devices with their start and end apart: 18, of which 12 were waited for; matrix products, arithmetic and copies ran while one was open for 0% of the time, Pallas kernels for 17%

profile of v3, /device:TPU:0, one launch (start us, length us, event | category | flops | bytes accessed | tf_op | source)
XLA Modules:
  0.0 54.7 jit_solution(11278238015291693772)
XLA Ops:
  0.0 1.2 %compact_rows.1 = (bf16[128,256]{1,0:T(8,128)(2,1)S(1)}, bf16[152,128]{1,0:T(8,128)(2,1)S(1)}, s32[128,64]{1,0:T(8,128)S(1)}, f32[8,128]{1,0:T(8,128)S(1)}) custom-call(s32[8]{0:T(128)} %rows_hbm.1, bf16[152,256]{1,0:T(8,128)(2,1)} %x_hbm.1, s32[8]{0:T(128)} %wanted_hbm.1, s32[1,128]{1,0:T(1,128)} %bitcast.11), custom_call_target="tpu_custom_call" | custom-call | tf_op jit(solution)/shard_map/compact_rows/pallas_call | solution.py:364
  1.2 5.1 %collective-permute-start.2 = (bf16[1,128,256]{2,1,0:T(8,128)(2,1)S(1)}, bf16[1,128,256]{2,1,0:T(8,128)(2,1)S(1)}, u32[]{:S(2)}, u32[]{:S(2)}) collective-permute-start(bf16[1,128,256]{2,1,0:T(8,128)(2,1)S(1)} %bitcast.5), channel_id=1, source_target_pairs={{0,24},{1,25},{2,26},{3,27},{4,28},{5,29},{6,30},{7,31},{8,16},{9,... | collective-permute-start | bytes 196616 | tf_op jit(solution)/shard_map/ppermute | solution.py:118
  7.0 2.5 %base_partials.1 = (bf16[16,128,256]{2,1,0:T(8,128)(2,1)S(1)}, f32[16,128,256]{2,1,0:T(8,128)S(1)}) custom-call(s32[1]{0:T(128)} %bitcast.1.refs_0_, bf16[128,256]{1,0:T(8,128)(2,1)S(1)} %get-tuple-element.28.refs_1_, bf16[256,8192]{1,0:T(8,128)(2,1)} %refs_2_.1), custom_call_target="tpu_custom_call" | custom-call | tf_op jit(solution)/shard_map/base_partials/pallas_call | solution.py:422
  9.5 1.5 %collective-permute-done.1 = bf16[1,128,256]{2,1,0:T(8,128)(2,1)S(1)} collective-permute-done((bf16[1,128,256]{2,1,0:T(8,128)(2,1)S(1)}, bf16[1,128,256]{2,1,0:T(8,128)(2,1)S(1)}, u32[]{:S(2)}, u32[]{:S(2)}) %collective-permute-start.1) | collective-permute-done | bytes 65568 | tf_op jit(solution)/shard_map/ppermute | solution.py:118
  11.0 1.0 %collective-permute-done = bf16[1,128,256]{2,1,0:T(8,128)(2,1)S(1)} collective-permute-done((bf16[1,128,256]{2,1,0:T(8,128)(2,1)S(1)}, bf16[1,128,256]{2,1,0:T(8,128)(2,1)S(1)}, u32[]{:S(2)}, u32[]{:S(2)}) %collective-permute-start) | collective-permute-done | bytes 65568 | tf_op jit(solution)/shard_map/ppermute | solution.py:118
  12.0 1.6 %collective-permute-start.3 = (bf16[4,128,256]{2,1,0:T(8,128)(2,1)S(1)}, bf16[4,128,256]{2,1,0:T(8,128)(2,1)S(1)}, u32[]{:S(2)}, u32[]{:S(2)}) collective-permute-start(bf16[4,128,256]{2,1,0:T(8,128)(2,1)S(1)} %pad_maximum_fusion.2), channel_id=1, source_target_pairs={{0,4},{1,3},{2,6},{3,1},{4,0},{5,7},{6,2},{7,5},{8,12},{9,11},{10,... | collective-permute-start | bytes 786440 | tf_op jit(solution)/shard_map/ppermute | solution.py:118
  14.3 2.9 %cut_tiles.1 = (bf16[16,128,256]{2,1,0:T(8,128)(2,1)S(1)}, bf16[16,128,256]{2,1,0:T(8,128)(2,1)S(1)}, bf16[16,128,256]{2,1,0:T(8,128)(2,1)S(1)}, bf16[16,128,256]{2,1,0:T(8,128)(2,1)S(1)}) custom-call(s32[3]{0:T(128)S(1)} %get-tuple-element.32.refs_0_, bf16[4,64,8192]{2,1,0:T(8,128)(2,1)} %bitcast.9, bf16[4,64,8192]{2,1,0:T(8,128)(2,1)} %bitcast.10), custom_call_target="tpu_custom_call" | custom-call | tf_op jit(solution)/shard_map/cut_tiles/pallas_call | solution.py:403
  17.2 1.2 %collective-permute-done.3 = bf16[4,128,256]{2,1,0:T(8,128)(2,1)S(1)} collective-permute-done((bf16[4,128,256]{2,1,0:T(8,128)(2,1)S(1)}, bf16[4,128,256]{2,1,0:T(8,128)(2,1)S(1)}, u32[]{:S(2)}, u32[]{:S(2)}) %collective-permute-start.3) | collective-permute-done | bytes 262176 | tf_op jit(solution)/shard_map/ppermute | solution.py:118
  19.2 1.6 %collective-permute-start.5 = (bf16[8,64,256]{2,1,0:T(8,128)(2,1)S(1)}, bf16[8,64,256]{2,1,0:T(8,128)(2,1)S(1)}, u32[]{:S(2)}, u32[]{:S(2)}) collective-permute-start(bf16[8,64,256]{2,1,0:T(8,128)(2,1)S(1)} %get-tuple-element.44.refs_0_), channel_id=1, source_target_pairs={{0,2},{1,5},{2,0},{3,7},{4,6},{5,1},{6,4},{7,3},{8,10},{9,13},{10,... | collective-permute-start | bytes 786440 | tf_op jit(solution)/shard_map/ppermute | solution.py:118
  21.8 3.9 %collective-permute-done.5.refs_2_ = bf16[8,64,256]{2,1,0:T(8,128)(2,1)S(1)} collective-permute-done((bf16[8,64,256]{2,1,0:T(8,128)(2,1)S(1)}, bf16[8,64,256]{2,1,0:T(8,128)(2,1)S(1)}, u32[]{:S(2)}, u32[]{:S(2)}) %collective-permute-start.5) | collective-permute-done | bytes 262176 | tf_op jit(solution)/shard_map/ppermute | solution.py:118
  26.3 1.2 %collective-permute-done.6.refs_2_ = f32[64,64]{1,0:T(8,128)S(1)} collective-permute-done((f32[64,64]{1,0:T(8,128)S(1)}, f32[64,64]{1,0:T(8,128)S(1)}, u32[]{:S(2)}, u32[]{:S(2)}) %collective-permute-start.6) | collective-permute-done | bytes 16416 | tf_op jit(solution)/shard_map/ppermute | solution.py:118
  27.8 1.6 %collective-permute-start.9 = (bf16[8,64,256]{2,1,0:T(8,128)(2,1)S(1)}, bf16[8,64,256]{2,1,0:T(8,128)(2,1)S(1)}, u32[]{:S(2)}, u32[]{:S(2)}) collective-permute-start(bf16[8,64,256]{2,1,0:T(8,128)(2,1)S(1)} %expand.5), channel_id=1, source_target_pairs={{0,2},{1,5},{2,0},{3,7},{4,6},{5,1},{6,4},{7,3},{8,10},{9,13},{10,... | collective-permute-start | bytes 786440 | tf_op jit(solution)/shard_map/ppermute | solution.py:118
  30.5 1.2 %collective-permute-done.12.refs_2_ = f32[64,64]{1,0:T(8,128)S(1)} collective-permute-done((f32[64,64]{1,0:T(8,128)S(1)}, f32[64,64]{1,0:T(8,128)S(1)}, u32[]{:S(2)}, u32[]{:S(2)}) %collective-permute-start.12) | collective-permute-done | bytes 16416 | tf_op jit(solution)/shard_map/ppermute | solution.py:118
  32.0 1.1 %collective-permute-start.13 = (bf16[8,64,256]{2,1,0:T(8,128)(2,1)S(1)}, bf16[8,64,256]{2,1,0:T(8,128)(2,1)S(1)}, u32[]{:S(2)}, u32[]{:S(2)}) collective-permute-start(bf16[8,64,256]{2,1,0:T(8,128)(2,1)S(1)} %expand.7), channel_id=1, source_target_pairs={{0,2},{1,5},{2,0},{3,7},{4,6},{5,1},{6,4},{7,3},{8,10},{9,13},{10,... | collective-permute-start | bytes 786440 | tf_op jit(solution)/shard_map/ppermute | solution.py:118
  34.3 1.6 %collective-permute-start.10 = (bf16[4,64,256]{2,1,0:T(8,128)(2,1)S(1)}, bf16[4,64,256]{2,1,0:T(8,128)(2,1)S(1)}, u32[]{:S(2)}, u32[]{:S(2)}) collective-permute-start(bf16[4,64,256]{2,1,0:T(8,128)(2,1)S(1)} %slice.65), channel_id=1, source_target_pairs={{0,4},{1,3},{2,6},{3,1},{4,0},{5,7},{6,2},{7,5},{8,12},{9,11},{10,... | collective-permute-start | bytes 393224 | tf_op jit(solution)/shard_map/ppermute | solution.py:118
  35.9 3.9 %collective-permute-done.13 = bf16[8,64,256]{2,1,0:T(8,128)(2,1)S(1)} collective-permute-done((bf16[8,64,256]{2,1,0:T(8,128)(2,1)S(1)}, bf16[8,64,256]{2,1,0:T(8,128)(2,1)S(1)}, u32[]{:S(2)}, u32[]{:S(2)}) %collective-permute-start.13) | collective-permute-done | bytes 262176 | tf_op jit(solution)/shard_map/ppermute | solution.py:118
  40.0 1.6 %collective-permute-start.14 = (bf16[4,64,256]{2,1,0:T(8,128)(2,1)S(1)}, bf16[4,64,256]{2,1,0:T(8,128)(2,1)S(1)}, u32[]{:S(2)}, u32[]{:S(2)}) collective-permute-start(bf16[4,64,256]{2,1,0:T(8,128)(2,1)S(1)} %slice.64), channel_id=1, source_target_pairs={{0,4},{1,3},{2,6},{3,1},{4,0},{5,7},{6,2},{7,5},{8,12},{9,11},{10,... | collective-permute-start | bytes 393224 | tf_op jit(solution)/shard_map/ppermute | solution.py:118
  41.6 3.4 %collective-permute-done.14 = bf16[4,64,256]{2,1,0:T(8,128)(2,1)S(1)} collective-permute-done((bf16[4,64,256]{2,1,0:T(8,128)(2,1)S(1)}, bf16[4,64,256]{2,1,0:T(8,128)(2,1)S(1)}, u32[]{:S(2)}, u32[]{:S(2)}) %collective-permute-start.14) | collective-permute-done | bytes 131104 | tf_op jit(solution)/shard_map/ppermute | solution.py:118
  45.1 2.0 %collective-permute-start.15 = (bf16[1,128,256]{2,1,0:T(8,128)(2,1)S(1)}, bf16[1,128,256]{2,1,0:T(8,128)(2,1)S(1)}, u32[]{:S(2)}, u32[]{:S(2)}) collective-permute-start(bf16[1,128,256]{2,1,0:T(8,128)(2,1)S(1)} %get-tuple-element.47), channel_id=1, source_target_pairs={{0,16},{1,17},{2,18},{3,19},{4,20},{5,21},{6,22},{7,23},{8,24},{9,... | collective-permute-start | bytes 196616 | tf_op jit(solution)/shard_map/ppermute | solution.py:118
  47.1 0.8 %collective-permute-start.16 = (bf16[1,128,256]{2,1,0:T(8,128)(2,1)S(1)}, bf16[1,128,256]{2,1,0:T(8,128)(2,1)S(1)}, u32[]{:S(2)}, u32[]{:S(2)}) collective-permute-start(bf16[1,128,256]{2,1,0:T(8,128)(2,1)S(1)} %get-tuple-element.46), channel_id=1, source_target_pairs={{0,8},{1,9},{2,10},{3,11},{4,12},{5,13},{6,14},{7,15},{8,0},{9,1},... | collective-permute-start | bytes 196616 | tf_op jit(solution)/shard_map/ppermute | solution.py:118
  47.9 1.7 %collective-permute-start.17 = (bf16[1,128,256]{2,1,0:T(8,128)(2,1)S(1)}, bf16[1,128,256]{2,1,0:T(8,128)(2,1)S(1)}, u32[]{:S(2)}, u32[]{:S(2)}) collective-permute-start(bf16[1,128,256]{2,1,0:T(8,128)(2,1)S(1)} %get-tuple-element.45), channel_id=1, source_target_pairs={{0,24},{1,25},{2,26},{3,27},{4,28},{5,29},{6,30},{7,31},{8,16},{9,... | collective-permute-start | bytes 196616 | tf_op jit(solution)/shard_map/ppermute | solution.py:118
  50.3 1.1 %collective-permute-done.16.refs_3_ = bf16[1,128,256]{2,1,0:T(8,128)(2,1)S(1)} collective-permute-done((bf16[1,128,256]{2,1,0:T(8,128)(2,1)S(1)}, bf16[1,128,256]{2,1,0:T(8,128)(2,1)S(1)}, u32[]{:S(2)}, u32[]{:S(2)}) %collective-permute-start.16) | collective-permute-done | bytes 65568 | tf_op jit(solution)/shard_map/ppermute | solution.py:118
  51.4 2.6 %collective-permute-done.17.refs_4_ = bf16[1,128,256]{2,1,0:T(8,128)(2,1)S(1)} collective-permute-done((bf16[1,128,256]{2,1,0:T(8,128)(2,1)S(1)}, bf16[1,128,256]{2,1,0:T(8,128)(2,1)S(1)}, u32[]{:S(2)}, u32[]{:S(2)}) %collective-permute-start.17) | collective-permute-done | bytes 65568 | tf_op jit(solution)/shard_map/ppermute | solution.py:118
  53.9 0.8 %spread_rows.1 = bf16[152,256]{1,0:T(8,128)(2,1)} custom-call(bf16[152,128]{1,0:T(8,128)(2,1)S(1)} %get-tuple-element.24.refs_0_, f32[1,128,256]{2,1,0:T(8,128)S(1)} %fusion.1.refs_1_, bf16[1,128,256]{2,1,0:T(8,128)(2,1)S(1)} %collective-permute-done.15.refs_2_, bf16[1,128,256]{2,1,0:T(8,128)(2,1)S(1)} %collective-permute-done.16.refs_3_, ...), custom_call_target="tpu_custom_call" | custom-call | tf_op jit(solution)/shard_map/spread_rows/pallas_call | solution.py:517
  (37 shorter events, 7.6 us)
Async XLA Ops:
  1.2 8.3 %collective-permute-start.2 = (bf16[1,128,256]{2,1,0:T(8,128)(2,1)S(1)}, bf16[1,128,256]{2,1,0:T(8,128)(2,1)S(1)}, u32[]{:S(2)}, u32[]{:S(2)}) collective-permute-start(bf16[1,128,256]{2,1,0:T(8,128)(2,1)S(1)} %bitcast.5), channel_id=1, source_target_pairs={{0,24},{1,25},{2,26},{3,27},{4,28},{5,29},{6,30},{7,31},{8,16},{9,... | collective-permute-start | bytes 196616 | tf_op jit(solution)/shard_map/ppermute | solution.py:118
  6.3 4.7 %collective-permute-start.1 = (bf16[1,128,256]{2,1,0:T(8,128)(2,1)S(1)}, bf16[1,128,256]{2,1,0:T(8,128)(2,1)S(1)}, u32[]{:S(2)}, u32[]{:S(2)}) collective-permute-start(bf16[1,128,256]{2,1,0:T(8,128)(2,1)S(1)} %bitcast.6), channel_id=1, source_target_pairs={{0,8},{1,9},{2,10},{3,11},{4,12},{5,13},{6,14},{7,15},{8,0},{9,1},... | collective-permute-start | bytes 196616 | tf_op jit(solution)/shard_map/ppermute | solution.py:118
  6.3 5.6 %collective-permute-start = (bf16[1,128,256]{2,1,0:T(8,128)(2,1)S(1)}, bf16[1,128,256]{2,1,0:T(8,128)(2,1)S(1)}, u32[]{:S(2)}, u32[]{:S(2)}) collective-permute-start(bf16[1,128,256]{2,1,0:T(8,128)(2,1)S(1)} %bitcast.7), channel_id=1, source_target_pairs={{0,16},{1,17},{2,18},{3,19},{4,20},{5,21},{6,22},{7,23},{8,24},{9,... | collective-permute-start | bytes 196616 | tf_op jit(solution)/shard_map/ppermute | solution.py:118
  12.0 6.4 %collective-permute-start.3 = (bf16[4,128,256]{2,1,0:T(8,128)(2,1)S(1)}, bf16[4,128,256]{2,1,0:T(8,128)(2,1)S(1)}, u32[]{:S(2)}, u32[]{:S(2)}) collective-permute-start(bf16[4,128,256]{2,1,0:T(8,128)(2,1)S(1)} %pad_maximum_fusion.2), channel_id=1, source_target_pairs={{0,4},{1,3},{2,6},{3,1},{4,0},{5,7},{6,2},{7,5},{8,12},{9,11},{10,... | collective-permute-start | bytes 786440 | tf_op jit(solution)/shard_map/ppermute | solution.py:118
  18.5 2.8 %collective-permute-start.4 = (bf16[16,128,256]{2,1,0:T(8,128)(2,1)S(1)}, bf16[16,128,256]{2,1,0:T(8,128)(2,1)S(1)}, u32[]{:S(2)}, u32[]{:S(2)}) collective-permute-start(bf16[16,128,256]{2,1,0:T(8,128)(2,1)S(1)} %get-tuple-element.37), channel_id=1, source_target_pairs={{0,1},{1,0},{2,3},{3,2},{4,5},{5,4},{6,7},{7,6},{8,9},{9,8},{10,11... | collective-permute-start | bytes 3145736 | tf_op jit(solution)/shard_map/ppermute | solution.py:118
  18.6 7.7 %collective-permute-start.7 = (bf16[16,128,256]{2,1,0:T(8,128)(2,1)S(1)}, bf16[16,128,256]{2,1,0:T(8,128)(2,1)S(1)}, u32[]{:S(2)}, u32[]{:S(2)}) collective-permute-start(bf16[16,128,256]{2,1,0:T(8,128)(2,1)S(1)} %get-tuple-element.39), channel_id=1, source_target_pairs={{0,1},{1,0},{2,3},{3,2},{4,5},{5,4},{6,7},{7,6},{8,9},{9,8},{10,11... | collective-permute-start | bytes 3145736 | tf_op jit(solution)/shard_map/ppermute | solution.py:118
  19.1 7.2 %collective-permute-start.8 = (bf16[16,128,256]{2,1,0:T(8,128)(2,1)S(1)}, bf16[16,128,256]{2,1,0:T(8,128)(2,1)S(1)}, u32[]{:S(2)}, u32[]{:S(2)}) collective-permute-start(bf16[16,128,256]{2,1,0:T(8,128)(2,1)S(1)} %get-tuple-element.41), channel_id=1, source_target_pairs={{0,1},{1,0},{2,3},{3,2},{4,5},{5,4},{6,7},{7,6},{8,9},{9,8},{10,11... | collective-permute-start | bytes 3145736 | tf_op jit(solution)/shard_map/ppermute | solution.py:118
  19.2 6.4 %collective-permute-start.5 = (bf16[8,64,256]{2,1,0:T(8,128)(2,1)S(1)}, bf16[8,64,256]{2,1,0:T(8,128)(2,1)S(1)}, u32[]{:S(2)}, u32[]{:S(2)}) collective-permute-start(bf16[8,64,256]{2,1,0:T(8,128)(2,1)S(1)} %get-tuple-element.44.refs_0_), channel_id=1, source_target_pairs={{0,2},{1,5},{2,0},{3,7},{4,6},{5,1},{6,4},{7,3},{8,10},{9,13},{10,... | collective-permute-start | bytes 786440 | tf_op jit(solution)/shard_map/ppermute | solution.py:118
  20.8 9.1 %collective-permute-start.11 = (bf16[8,64,256]{2,1,0:T(8,128)(2,1)S(1)}, bf16[8,64,256]{2,1,0:T(8,128)(2,1)S(1)}, u32[]{:S(2)}, u32[]{:S(2)}) collective-permute-start(bf16[8,64,256]{2,1,0:T(8,128)(2,1)S(1)} %get-tuple-element.43.refs_0_), channel_id=1, source_target_pairs={{0,2},{1,5},{2,0},{3,7},{4,6},{5,1},{6,4},{7,3},{8,10},{9,13},{10,... | collective-permute-start | bytes 786440 | tf_op jit(solution)/shard_map/ppermute | solution.py:118
  26.2 1.3 %collective-permute-start.6 = (f32[64,64]{1,0:T(8,128)S(1)}, f32[64,64]{1,0:T(8,128)S(1)}, u32[]{:S(2)}, u32[]{:S(2)}) collective-permute-start(f32[64,64]{1,0:T(8,128)S(1)} %shrink.2.refs_1_), channel_id=1, source_target_pairs={{0,1},{1,0},{2,3},{3,2},{4,5},{5,4},{6,7},{7,6},{8,9},{9,8},{10,11... | collective-permute-start | bytes 49160 | tf_op jit(solution)/shard_map/ppermute | solution.py:118
  27.8 6.4 %collective-permute-start.9 = (bf16[8,64,256]{2,1,0:T(8,128)(2,1)S(1)}, bf16[8,64,256]{2,1,0:T(8,128)(2,1)S(1)}, u32[]{:S(2)}, u32[]{:S(2)}) collective-permute-start(bf16[8,64,256]{2,1,0:T(8,128)(2,1)S(1)} %expand.5), channel_id=1, source_target_pairs={{0,2},{1,5},{2,0},{3,7},{4,6},{5,1},{6,4},{7,3},{8,10},{9,13},{10,... | collective-permute-start | bytes 786440 | tf_op jit(solution)/shard_map/ppermute | solution.py:118
  30.4 1.3 %collective-permute-start.12 = (f32[64,64]{1,0:T(8,128)S(1)}, f32[64,64]{1,0:T(8,128)S(1)}, u32[]{:S(2)}, u32[]{:S(2)}) collective-permute-start(f32[64,64]{1,0:T(8,128)S(1)} %shrink.3.refs_1_), channel_id=1, source_target_pairs={{0,1},{1,0},{2,3},{3,2},{4,5},{5,4},{6,7},{7,6},{8,9},{9,8},{10,11... | collective-permute-start | bytes 49160 | tf_op jit(solution)/shard_map/ppermute | solution.py:118
  32.0 7.8 %collective-permute-start.13 = (bf16[8,64,256]{2,1,0:T(8,128)(2,1)S(1)}, bf16[8,64,256]{2,1,0:T(8,128)(2,1)S(1)}, u32[]{:S(2)}, u32[]{:S(2)}) collective-permute-start(bf16[8,64,256]{2,1,0:T(8,128)(2,1)S(1)} %expand.7), channel_id=1, source_target_pairs={{0,2},{1,5},{2,0},{3,7},{4,6},{5,1},{6,4},{7,3},{8,10},{9,13},{10,... | collective-permute-start | bytes 786440 | tf_op jit(solution)/shard_map/ppermute | solution.py:118
  34.3 7.2 %collective-permute-start.10 = (bf16[4,64,256]{2,1,0:T(8,128)(2,1)S(1)}, bf16[4,64,256]{2,1,0:T(8,128)(2,1)S(1)}, u32[]{:S(2)}, u32[]{:S(2)}) collective-permute-start(bf16[4,64,256]{2,1,0:T(8,128)(2,1)S(1)} %slice.65), channel_id=1, source_target_pairs={{0,4},{1,3},{2,6},{3,1},{4,0},{5,7},{6,2},{7,5},{8,12},{9,11},{10,... | collective-permute-start | bytes 393224 | tf_op jit(solution)/shard_map/ppermute | solution.py:118
  40.0 5.0 %collective-permute-start.14 = (bf16[4,64,256]{2,1,0:T(8,128)(2,1)S(1)}, bf16[4,64,256]{2,1,0:T(8,128)(2,1)S(1)}, u32[]{:S(2)}, u32[]{:S(2)}) collective-permute-start(bf16[4,64,256]{2,1,0:T(8,128)(2,1)S(1)} %slice.64), channel_id=1, source_target_pairs={{0,4},{1,3},{2,6},{3,1},{4,0},{5,7},{6,2},{7,5},{8,12},{9,11},{10,... | collective-permute-start | bytes 393224 | tf_op jit(solution)/shard_map/ppermute | solution.py:118
  45.1 5.2 %collective-permute-start.15 = (bf16[1,128,256]{2,1,0:T(8,128)(2,1)S(1)}, bf16[1,128,256]{2,1,0:T(8,128)(2,1)S(1)}, u32[]{:S(2)}, u32[]{:S(2)}) collective-permute-start(bf16[1,128,256]{2,1,0:T(8,128)(2,1)S(1)} %get-tuple-element.47), channel_id=1, source_target_pairs={{0,16},{1,17},{2,18},{3,19},{4,20},{5,21},{6,22},{7,23},{8,24},{9,... | collective-permute-start | bytes 196616 | tf_op jit(solution)/shard_map/ppermute | solution.py:118
  47.1 4.3 %collective-permute-start.16 = (bf16[1,128,256]{2,1,0:T(8,128)(2,1)S(1)}, bf16[1,128,256]{2,1,0:T(8,128)(2,1)S(1)}, u32[]{:S(2)}, u32[]{:S(2)}) collective-permute-start(bf16[1,128,256]{2,1,0:T(8,128)(2,1)S(1)} %get-tuple-element.46), channel_id=1, source_target_pairs={{0,8},{1,9},{2,10},{3,11},{4,12},{5,13},{6,14},{7,15},{8,0},{9,1},... | collective-permute-start | bytes 196616 | tf_op jit(solution)/shard_map/ppermute | solution.py:118
  47.9 6.1 %collective-permute-start.17 = (bf16[1,128,256]{2,1,0:T(8,128)(2,1)S(1)}, bf16[1,128,256]{2,1,0:T(8,128)(2,1)S(1)}, u32[]{:S(2)}, u32[]{:S(2)}) collective-permute-start(bf16[1,128,256]{2,1,0:T(8,128)(2,1)S(1)} %get-tuple-element.45), channel_id=1, source_target_pairs={{0,24},{1,25},{2,26},{3,27},{4,28},{5,29},{6,30},{7,31},{8,16},{9,... | collective-permute-start | bytes 196616 | tf_op jit(solution)/shard_map/ppermute | solution.py:118

commit v4 on v3

--- a/solution.py
+++ b/solution.py
@@ -482,17 +482,20 @@
             gathered = [gathered[:, a : a + n] for a, n in zip(starts, sizes)]
             got = [exchange(part, *masks[0]) for part in gathered]
         if k == 0:
-            base_send, base_keep = base_partials(me)
+            down_send, down_own, up_send, up_own = cut_tiles(info)
+            gathered, down_send, up_send, code = after((gathered, down_send, up_send, code))
+            down_peer = exchange(down_send, 1, 1)
+            up_peer = exchange(up_send, 1, 1)
+        if k == cut_at:
+            gathered, down_peer = after((gathered, down_peer))
+        if k == cut_at:
+            base_send, base_keep = base_partials(after(me, before))
             gathered, base_send = after((gathered, base_send))
             base_got = exchange(base_send, 1, 1)
-        if k == cut_at:
-            down_send, down_own, up_send, up_own = cut_tiles(after(info, before))
-            gathered, down_send, up_send = after((gathered, down_send, up_send))
-            down_peer = exchange(down_send, 1, 1)
-            up_peer = exchange(up_send, 1, 1)
 
     sums = [shrink_start(i, part) for i, part in enumerate(gathered)]
 
+    got[0] = after(got[0], sums)
     mine, theirs, send = [None] * chains, [None] * chains, [None] * chains
     for i in range(chains):
         last = got[i] if i == 0 else after(got[i], send[i - 1])

time: 54.9 us -> 52.8 us (0.962)
  waiting for transfers between devices: 22.1 us -> 20.4 us
    ppermute x18, waiting for transfers between devices: 22.1 us -> 20.4 us  [exchange(): return lax.ppermute(value, 'replica', pairs)]
  transfers between devices with their start and end apart: 18 -> 18, of which waited for: 12 -> 12; matrix products, arithmetic and copies ran while one was open for 0% -> 0% of each run, Pallas kernels for 17% -> 18%
where the time goes in v4:
time: 52.8 us; the launch traced here: 52.7 us
  waiting for transfers between devices  20.4 us (39%)
  starting transfers between devices  20.2 us (38%)
  Pallas kernels  11.6 us (22%)
    ppermute x18, waiting for transfers between devices, exchange(): return lax.ppermute(value, 'replica', pairs)  20.4 us
    ppermute x18, starting transfers between devices, exchange(): return lax.ppermute(value, 'replica', pairs)  20.2 us
    pallas_call x1, Pallas kernels, cut_tiles(): pl.pallas_call(lambda *refs: tiles_kernel(tables, *refs), out_shape=[jax....  2.89 us
    pallas_call x1, Pallas kernels, base_partials(): pl.pallas_call(lambda *refs: base_kernel(tables, *refs), out_shape=[jax.S...  2.53 us
    pallas_call x4, Pallas kernels, expand(): pl.pallas_call(lambda *refs: expand_kernel(starts[i], range(part * half,...  1.39 us
    pallas_call x1, Pallas kernels, owner_side(): pl.pallas_call(compact_kernel, out_shape=[jax.ShapeDtypeStruct((live_rows...  1.22 us
    pallas_call x2, Pallas kernels, shrink(): pl.pallas_call(lambda *refs: shrink_kernel(starts[i], range(half, positio...  1.08 us
  transfers between devices with their start and end apart: 18, of which 12 were waited for; matrix products, arithmetic and copies ran while one was open for 0% of the time, Pallas kernels for 18%

profile of v4, /device:TPU:0, one launch (start us, length us, event | category | flops | bytes accessed | tf_op | source)
XLA Modules:
  0.0 52.7 jit_solution(16232345314636354052)
XLA Ops:
  0.0 1.2 %compact_rows.1 = (bf16[128,256]{1,0:T(8,128)(2,1)S(1)}, bf16[152,128]{1,0:T(8,128)(2,1)S(1)}, s32[128,64]{1,0:T(8,128)S(1)}, f32[8,128]{1,0:T(8,128)S(1)}) custom-call(s32[8]{0:T(128)} %rows_hbm.1, bf16[152,256]{1,0:T(8,128)(2,1)} %x_hbm.1, s32[8]{0:T(128)} %wanted_hbm.1, s32[1,128]{1,0:T(1,128)} %bitcast.11), custom_call_target="tpu_custom_call" | custom-call | tf_op jit(solution)/shard_map/compact_rows/pallas_call | solution.py:364
  1.2 5.1 %collective-permute-start.2 = (bf16[1,128,256]{2,1,0:T(8,128)(2,1)S(1)}, bf16[1,128,256]{2,1,0:T(8,128)(2,1)S(1)}, u32[]{:S(2)}, u32[]{:S(2)}) collective-permute-start(bf16[1,128,256]{2,1,0:T(8,128)(2,1)S(1)} %bitcast.5), channel_id=1, source_target_pairs={{0,24},{1,25},{2,26},{3,27},{4,28},{5,29},{6,30},{7,31},{8,16},{9,... | collective-permute-start | bytes 196616 | tf_op jit(solution)/shard_map/ppermute | solution.py:118
  7.0 0.7 %find_adapters.1 = (s32[3]{0:T(128)S(1)}, f32[128,64]{1,0:T(8,128)S(1)}) custom-call(s32[1]{0:T(128)} %bitcast.2.refs_0_, f32[8,128]{1,0:T(8,128)S(1)} %get-tuple-element.30.refs_1_, s32[128,64]{1,0:T(8,128)S(1)} %get-tuple-element.31.refs_2_), custom_call_target="tpu_custom_call" | custom-call | tf_op jit(solution)/shard_map/find_adapters/pallas_call | solution.py:390
  7.7 2.9 %cut_tiles.1 = (bf16[16,128,256]{2,1,0:T(8,128)(2,1)S(1)}, bf16[16,128,256]{2,1,0:T(8,128)(2,1)S(1)}, bf16[16,128,256]{2,1,0:T(8,128)(2,1)S(1)}, bf16[16,128,256]{2,1,0:T(8,128)(2,1)S(1)}) custom-call(s32[3]{0:T(128)S(1)} %get-tuple-element.32.refs_0_, bf16[4,64,8192]{2,1,0:T(8,128)(2,1)} %bitcast.9, bf16[4,64,8192]{2,1,0:T(8,128)(2,1)} %bitcast.10), custom_call_target="tpu_custom_call" | custom-call | tf_op jit(solution)/shard_map/cut_tiles/pallas_call | solution.py:403
  11.0 1.0 %collective-permute-done = bf16[1,128,256]{2,1,0:T(8,128)(2,1)S(1)} collective-permute-done((bf16[1,128,256]{2,1,0:T(8,128)(2,1)S(1)}, bf16[1,128,256]{2,1,0:T(8,128)(2,1)S(1)}, u32[]{:S(2)}, u32[]{:S(2)}) %collective-permute-start) | collective-permute-done | bytes 65568 | tf_op jit(solution)/shard_map/ppermute | solution.py:118
  12.1 1.6 %collective-permute-start.3 = (bf16[4,128,256]{2,1,0:T(8,128)(2,1)S(1)}, bf16[4,128,256]{2,1,0:T(8,128)(2,1)S(1)}, u32[]{:S(2)}, u32[]{:S(2)}) collective-permute-start(bf16[4,128,256]{2,1,0:T(8,128)(2,1)S(1)} %pad_maximum_fusion.2), channel_id=1, source_target_pairs={{0,4},{1,3},{2,6},{3,1},{4,0},{5,7},{6,2},{7,5},{8,12},{9,11},{10,... | collective-permute-start | bytes 786440 | tf_op jit(solution)/shard_map/ppermute | solution.py:118
  13.8 2.5 %base_partials.1 = (bf16[16,128,256]{2,1,0:T(8,128)(2,1)S(1)}, f32[16,128,256]{2,1,0:T(8,128)S(1)}) custom-call(s32[1]{0:T(128)} %bitcast.2.refs_0_, bf16[128,256]{1,0:T(8,128)(2,1)S(1)} %get-tuple-element.29.refs_1_, bf16[256,8192]{1,0:T(8,128)(2,1)} %refs_2_.1), custom_call_target="tpu_custom_call" | custom-call | tf_op jit(solution)/shard_map/base_partials/pallas_call | solution.py:422
  16.3 2.2 %collective-permute-done.3 = bf16[4,128,256]{2,1,0:T(8,128)(2,1)S(1)} collective-permute-done((bf16[4,128,256]{2,1,0:T(8,128)(2,1)S(1)}, bf16[4,128,256]{2,1,0:T(8,128)(2,1)S(1)}, u32[]{:S(2)}, u32[]{:S(2)}) %collective-permute-start.3) | collective-permute-done | bytes 262176 | tf_op jit(solution)/shard_map/ppermute | solution.py:118
  18.7 1.6 %collective-permute-start.5 = (bf16[8,64,256]{2,1,0:T(8,128)(2,1)S(1)}, bf16[8,64,256]{2,1,0:T(8,128)(2,1)S(1)}, u32[]{:S(2)}, u32[]{:S(2)}) collective-permute-start(bf16[8,64,256]{2,1,0:T(8,128)(2,1)S(1)} %get-tuple-element.52.refs_0_), channel_id=1, source_target_pairs={{0,2},{1,5},{2,0},{3,7},{4,6},{5,1},{6,4},{7,3},{8,10},{9,13},{10,... | collective-permute-start | bytes 786440 | tf_op jit(solution)/shard_map/ppermute | solution.py:118
  21.8 3.4 %collective-permute-done.5.refs_2_ = bf16[8,64,256]{2,1,0:T(8,128)(2,1)S(1)} collective-permute-done((bf16[8,64,256]{2,1,0:T(8,128)(2,1)S(1)}, bf16[8,64,256]{2,1,0:T(8,128)(2,1)S(1)}, u32[]{:S(2)}, u32[]{:S(2)}) %collective-permute-start.5) | collective-permute-done | bytes 262176 | tf_op jit(solution)/shard_map/ppermute | solution.py:118
  25.8 1.2 %collective-permute-done.6.refs_2_ = f32[64,64]{1,0:T(8,128)S(1)} collective-permute-done((f32[64,64]{1,0:T(8,128)S(1)}, f32[64,64]{1,0:T(8,128)S(1)}, u32[]{:S(2)}, u32[]{:S(2)}) %collective-permute-start.6) | collective-permute-done | bytes 16416 | tf_op jit(solution)/shard_map/ppermute | solution.py:118
  27.3 1.6 %collective-permute-start.9 = (bf16[8,64,256]{2,1,0:T(8,128)(2,1)S(1)}, bf16[8,64,256]{2,1,0:T(8,128)(2,1)S(1)}, u32[]{:S(2)}, u32[]{:S(2)}) collective-permute-start(bf16[8,64,256]{2,1,0:T(8,128)(2,1)S(1)} %expand.5), channel_id=1, source_target_pairs={{0,2},{1,5},{2,0},{3,7},{4,6},{5,1},{6,4},{7,3},{8,10},{9,13},{10,... | collective-permute-start | bytes 786440 | tf_op jit(solution)/shard_map/ppermute | solution.py:118
  29.5 1.2 %collective-permute-done.12.refs_2_ = f32[64,64]{1,0:T(8,128)S(1)} collective-permute-done((f32[64,64]{1,0:T(8,128)S(1)}, f32[64,64]{1,0:T(8,128)S(1)}, u32[]{:S(2)}, u32[]{:S(2)}) %collective-permute-start.12) | collective-permute-done | bytes 16416 | tf_op jit(solution)/shard_map/ppermute | solution.py:118
  31.1 1.1 %collective-permute-start.13 = (bf16[8,64,256]{2,1,0:T(8,128)(2,1)S(1)}, bf16[8,64,256]{2,1,0:T(8,128)(2,1)S(1)}, u32[]{:S(2)}, u32[]{:S(2)}) collective-permute-start(bf16[8,64,256]{2,1,0:T(8,128)(2,1)S(1)} %expand.7), channel_id=1, source_target_pairs={{0,2},{1,5},{2,0},{3,7},{4,6},{5,1},{6,4},{7,3},{8,10},{9,13},{10,... | collective-permute-start | bytes 786440 | tf_op jit(solution)/shard_map/ppermute | solution.py:118
  32.9 0.9 %collective-permute-done.9 = bf16[8,64,256]{2,1,0:T(8,128)(2,1)S(1)} collective-permute-done((bf16[8,64,256]{2,1,0:T(8,128)(2,1)S(1)}, bf16[8,64,256]{2,1,0:T(8,128)(2,1)S(1)}, u32[]{:S(2)}, u32[]{:S(2)}) %collective-permute-start.9) | collective-permute-done | bytes 262176 | tf_op jit(solution)/shard_map/ppermute | solution.py:118
  33.9 1.6 %collective-permute-start.10 = (bf16[4,64,256]{2,1,0:T(8,128)(2,1)S(1)}, bf16[4,64,256]{2,1,0:T(8,128)(2,1)S(1)}, u32[]{:S(2)}, u32[]{:S(2)}) collective-permute-start(bf16[4,64,256]{2,1,0:T(8,128)(2,1)S(1)} %slice.65), channel_id=1, source_target_pairs={{0,4},{1,3},{2,6},{3,1},{4,0},{5,7},{6,2},{7,5},{8,12},{9,11},{10,... | collective-permute-start | bytes 393224 | tf_op jit(solution)/shard_map/ppermute | solution.py:118
  35.5 3.5 %collective-permute-done.13 = bf16[8,64,256]{2,1,0:T(8,128)(2,1)S(1)} collective-permute-done((bf16[8,64,256]{2,1,0:T(8,128)(2,1)S(1)}, bf16[8,64,256]{2,1,0:T(8,128)(2,1)S(1)}, u32[]{:S(2)}, u32[]{:S(2)}) %collective-permute-start.13) | collective-permute-done | bytes 262176 | tf_op jit(solution)/shard_map/ppermute | solution.py:118
  39.0 1.6 %collective-permute-start.14 = (bf16[4,64,256]{2,1,0:T(8,128)(2,1)S(1)}, bf16[4,64,256]{2,1,0:T(8,128)(2,1)S(1)}, u32[]{:S(2)}, u32[]{:S(2)}) collective-permute-start(bf16[4,64,256]{2,1,0:T(8,128)(2,1)S(1)} %slice.64), channel_id=1, source_target_pairs={{0,4},{1,3},{2,6},{3,1},{4,0},{5,7},{6,2},{7,5},{8,12},{9,11},{10,... | collective-permute-start | bytes 393224 | tf_op jit(solution)/shard_map/ppermute | solution.py:118
  40.6 3.4 %collective-permute-done.14 = bf16[4,64,256]{2,1,0:T(8,128)(2,1)S(1)} collective-permute-done((bf16[4,64,256]{2,1,0:T(8,128)(2,1)S(1)}, bf16[4,64,256]{2,1,0:T(8,128)(2,1)S(1)}, u32[]{:S(2)}, u32[]{:S(2)}) %collective-permute-start.14) | collective-permute-done | bytes 131104 | tf_op jit(solution)/shard_map/ppermute | solution.py:118
  44.1 2.5 %collective-permute-start.17 = (bf16[1,128,256]{2,1,0:T(8,128)(2,1)S(1)}, bf16[1,128,256]{2,1,0:T(8,128)(2,1)S(1)}, u32[]{:S(2)}, u32[]{:S(2)}) collective-permute-start(bf16[1,128,256]{2,1,0:T(8,128)(2,1)S(1)} %get-tuple-element.53), channel_id=1, source_target_pairs={{0,24},{1,25},{2,26},{3,27},{4,28},{5,29},{6,30},{7,31},{8,16},{9,... | collective-permute-start | bytes 196616 | tf_op jit(solution)/shard_map/ppermute | solution.py:118
  46.7 1.9 %collective-permute-start.15 = (bf16[1,128,256]{2,1,0:T(8,128)(2,1)S(1)}, bf16[1,128,256]{2,1,0:T(8,128)(2,1)S(1)}, u32[]{:S(2)}, u32[]{:S(2)}) collective-permute-start(bf16[1,128,256]{2,1,0:T(8,128)(2,1)S(1)} %get-tuple-element.55), channel_id=1, source_target_pairs={{0,16},{1,17},{2,18},{3,19},{4,20},{5,21},{6,22},{7,23},{8,24},{9,... | collective-permute-start | bytes 196616 | tf_op jit(solution)/shard_map/ppermute | solution.py:118
  48.6 1.7 %collective-permute-done.17.refs_4_ = bf16[1,128,256]{2,1,0:T(8,128)(2,1)S(1)} collective-permute-done((bf16[1,128,256]{2,1,0:T(8,128)(2,1)S(1)}, bf16[1,128,256]{2,1,0:T(8,128)(2,1)S(1)}, u32[]{:S(2)}, u32[]{:S(2)}) %collective-permute-start.17) | collective-permute-done | bytes 65568 | tf_op jit(solution)/shard_map/ppermute | solution.py:118
  51.0 0.9 %collective-permute-done.15.refs_2_ = bf16[1,128,256]{2,1,0:T(8,128)(2,1)S(1)} collective-permute-done((bf16[1,128,256]{2,1,0:T(8,128)(2,1)S(1)}, bf16[1,128,256]{2,1,0:T(8,128)(2,1)S(1)}, u32[]{:S(2)}, u32[]{:S(2)}) %collective-permute-start.15) | collective-permute-done | bytes 65568 | tf_op jit(solution)/shard_map/ppermute | solution.py:118
  51.9 0.8 %spread_rows.1 = bf16[152,256]{1,0:T(8,128)(2,1)} custom-call(bf16[152,128]{1,0:T(8,128)(2,1)S(1)} %get-tuple-element.28.refs_0_, f32[1,128,256]{2,1,0:T(8,128)S(1)} %fusion.1.refs_1_, bf16[1,128,256]{2,1,0:T(8,128)(2,1)S(1)} %collective-permute-done.15.refs_2_, bf16[1,128,256]{2,1,0:T(8,128)(2,1)S(1)} %collective-permute-done.16.refs_3_, ...), custom_call_target="tpu_custom_call" | custom-call | tf_op jit(solution)/shard_map/spread_rows/pallas_call | solution.py:520
  (37 shorter events, 6.5 us)
Async XLA Ops:
  1.2 9.4 %collective-permute-start.2 = (bf16[1,128,256]{2,1,0:T(8,128)(2,1)S(1)}, bf16[1,128,256]{2,1,0:T(8,128)(2,1)S(1)}, u32[]{:S(2)}, u32[]{:S(2)}) collective-permute-start(bf16[1,128,256]{2,1,0:T(8,128)(2,1)S(1)} %bitcast.5), channel_id=1, source_target_pairs={{0,24},{1,25},{2,26},{3,27},{4,28},{5,29},{6,30},{7,31},{8,16},{9,... | collective-permute-start | bytes 196616 | tf_op jit(solution)/shard_map/ppermute | solution.py:118
  6.3 4.7 %collective-permute-start.1 = (bf16[1,128,256]{2,1,0:T(8,128)(2,1)S(1)}, bf16[1,128,256]{2,1,0:T(8,128)(2,1)S(1)}, u32[]{:S(2)}, u32[]{:S(2)}) collective-permute-start(bf16[1,128,256]{2,1,0:T(8,128)(2,1)S(1)} %bitcast.6), channel_id=1, source_target_pairs={{0,8},{1,9},{2,10},{3,11},{4,12},{5,13},{6,14},{7,15},{8,0},{9,1},... | collective-permute-start | bytes 196616 | tf_op jit(solution)/shard_map/ppermute | solution.py:118
  6.3 5.6 %collective-permute-start = (bf16[1,128,256]{2,1,0:T(8,128)(2,1)S(1)}, bf16[1,128,256]{2,1,0:T(8,128)(2,1)S(1)}, u32[]{:S(2)}, u32[]{:S(2)}) collective-permute-start(bf16[1,128,256]{2,1,0:T(8,128)(2,1)S(1)} %bitcast.7), channel_id=1, source_target_pairs={{0,16},{1,17},{2,18},{3,19},{4,20},{5,21},{6,22},{7,23},{8,24},{9,... | collective-permute-start | bytes 196616 | tf_op jit(solution)/shard_map/ppermute | solution.py:118
  12.0 6.6 %collective-permute-start.4 = (bf16[16,128,256]{2,1,0:T(8,128)(2,1)S(1)}, bf16[16,128,256]{2,1,0:T(8,128)(2,1)S(1)}, u32[]{:S(2)}, u32[]{:S(2)}) collective-permute-start(bf16[16,128,256]{2,1,0:T(8,128)(2,1)S(1)} %get-tuple-element.38), channel_id=1, source_target_pairs={{0,1},{1,0},{2,3},{3,2},{4,5},{5,4},{6,7},{7,6},{8,9},{9,8},{10,11... | collective-permute-start | bytes 3145736 | tf_op jit(solution)/shard_map/ppermute | solution.py:118
  12.1 6.4 %collective-permute-start.3 = (bf16[4,128,256]{2,1,0:T(8,128)(2,1)S(1)}, bf16[4,128,256]{2,1,0:T(8,128)(2,1)S(1)}, u32[]{:S(2)}, u32[]{:S(2)}) collective-permute-start(bf16[4,128,256]{2,1,0:T(8,128)(2,1)S(1)} %pad_maximum_fusion.2), channel_id=1, source_target_pairs={{0,4},{1,3},{2,6},{3,1},{4,0},{5,7},{6,2},{7,5},{8,12},{9,11},{10,... | collective-permute-start | bytes 786440 | tf_op jit(solution)/shard_map/ppermute | solution.py:118
  13.7 12.1 %collective-permute-start.8 = (bf16[16,128,256]{2,1,0:T(8,128)(2,1)S(1)}, bf16[16,128,256]{2,1,0:T(8,128)(2,1)S(1)}, u32[]{:S(2)}, u32[]{:S(2)}) collective-permute-start(bf16[16,128,256]{2,1,0:T(8,128)(2,1)S(1)} %get-tuple-element.49), channel_id=1, source_target_pairs={{0,1},{1,0},{2,3},{3,2},{4,5},{5,4},{6,7},{7,6},{8,9},{9,8},{10,11... | collective-permute-start | bytes 3145736 | tf_op jit(solution)/shard_map/ppermute | solution.py:118
  18.6 8.4 %collective-permute-start.7 = (bf16[16,128,256]{2,1,0:T(8,128)(2,1)S(1)}, bf16[16,128,256]{2,1,0:T(8,128)(2,1)S(1)}, u32[]{:S(2)}, u32[]{:S(2)}) collective-permute-start(bf16[16,128,256]{2,1,0:T(8,128)(2,1)S(1)} %get-tuple-element.47), channel_id=1, source_target_pairs={{0,1},{1,0},{2,3},{3,2},{4,5},{5,4},{6,7},{7,6},{8,9},{9,8},{10,11... | collective-permute-start | bytes 3145736 | tf_op jit(solution)/shard_map/ppermute | solution.py:118
  18.7 6.4 %collective-permute-start.5 = (bf16[8,64,256]{2,1,0:T(8,128)(2,1)S(1)}, bf16[8,64,256]{2,1,0:T(8,128)(2,1)S(1)}, u32[]{:S(2)}, u32[]{:S(2)}) collective-permute-start(bf16[8,64,256]{2,1,0:T(8,128)(2,1)S(1)} %get-tuple-element.52.refs_0_), channel_id=1, source_target_pairs={{0,2},{1,5},{2,0},{3,7},{4,6},{5,1},{6,4},{7,3},{8,10},{9,13},{10,... | collective-permute-start | bytes 786440 | tf_op jit(solution)/shard_map/ppermute | solution.py:118
  20.3 8.6 %collective-permute-start.11 = (bf16[8,64,256]{2,1,0:T(8,128)(2,1)S(1)}, bf16[8,64,256]{2,1,0:T(8,128)(2,1)S(1)}, u32[]{:S(2)}, u32[]{:S(2)}) collective-permute-start(bf16[8,64,256]{2,1,0:T(8,128)(2,1)S(1)} %get-tuple-element.51.refs_0_), channel_id=1, source_target_pairs={{0,2},{1,5},{2,0},{3,7},{4,6},{5,1},{6,4},{7,3},{8,10},{9,13},{10,... | collective-permute-start | bytes 786440 | tf_op jit(solution)/shard_map/ppermute | solution.py:118
  25.7 1.3 %collective-permute-start.6 = (f32[64,64]{1,0:T(8,128)S(1)}, f32[64,64]{1,0:T(8,128)S(1)}, u32[]{:S(2)}, u32[]{:S(2)}) collective-permute-start(f32[64,64]{1,0:T(8,128)S(1)} %shrink.2.refs_1_), channel_id=1, source_target_pairs={{0,1},{1,0},{2,3},{3,2},{4,5},{5,4},{6,7},{7,6},{8,9},{9,8},{10,11... | collective-permute-start | bytes 49160 | tf_op jit(solution)/shard_map/ppermute | solution.py:118
  27.3 6.4 %collective-permute-start.9 = (bf16[8,64,256]{2,1,0:T(8,128)(2,1)S(1)}, bf16[8,64,256]{2,1,0:T(8,128)(2,1)S(1)}, u32[]{:S(2)}, u32[]{:S(2)}) collective-permute-start(bf16[8,64,256]{2,1,0:T(8,128)(2,1)S(1)} %expand.5), channel_id=1, source_target_pairs={{0,2},{1,5},{2,0},{3,7},{4,6},{5,1},{6,4},{7,3},{8,10},{9,13},{10,... | collective-permute-start | bytes 786440 | tf_op jit(solution)/shard_map/ppermute | solution.py:118
  29.4 1.3 %collective-permute-start.12 = (f32[64,64]{1,0:T(8,128)S(1)}, f32[64,64]{1,0:T(8,128)S(1)}, u32[]{:S(2)}, u32[]{:S(2)}) collective-permute-start(f32[64,64]{1,0:T(8,128)S(1)} %shrink.3.refs_1_), channel_id=1, source_target_pairs={{0,1},{1,0},{2,3},{3,2},{4,5},{5,4},{6,7},{7,6},{8,9},{9,8},{10,11... | collective-permute-start | bytes 49160 | tf_op jit(solution)/shard_map/ppermute | solution.py:118
  31.1 7.8 %collective-permute-start.13 = (bf16[8,64,256]{2,1,0:T(8,128)(2,1)S(1)}, bf16[8,64,256]{2,1,0:T(8,128)(2,1)S(1)}, u32[]{:S(2)}, u32[]{:S(2)}) collective-permute-start(bf16[8,64,256]{2,1,0:T(8,128)(2,1)S(1)} %expand.7), channel_id=1, source_target_pairs={{0,2},{1,5},{2,0},{3,7},{4,6},{5,1},{6,4},{7,3},{8,10},{9,13},{10,... | collective-permute-start | bytes 786440 | tf_op jit(solution)/shard_map/ppermute | solution.py:118
  33.9 6.7 %collective-permute-start.10 = (bf16[4,64,256]{2,1,0:T(8,128)(2,1)S(1)}, bf16[4,64,256]{2,1,0:T(8,128)(2,1)S(1)}, u32[]{:S(2)}, u32[]{:S(2)}) collective-permute-start(bf16[4,64,256]{2,1,0:T(8,128)(2,1)S(1)} %slice.65), channel_id=1, source_target_pairs={{0,4},{1,3},{2,6},{3,1},{4,0},{5,7},{6,2},{7,5},{8,12},{9,11},{10,... | collective-permute-start | bytes 393224 | tf_op jit(solution)/shard_map/ppermute | solution.py:118
  39.0 5.0 %collective-permute-start.14 = (bf16[4,64,256]{2,1,0:T(8,128)(2,1)S(1)}, bf16[4,64,256]{2,1,0:T(8,128)(2,1)S(1)}, u32[]{:S(2)}, u32[]{:S(2)}) collective-permute-start(bf16[4,64,256]{2,1,0:T(8,128)(2,1)S(1)} %slice.64), channel_id=1, source_target_pairs={{0,4},{1,3},{2,6},{3,1},{4,0},{5,7},{6,2},{7,5},{8,12},{9,11},{10,... | collective-permute-start | bytes 393224 | tf_op jit(solution)/shard_map/ppermute | solution.py:118
  44.1 6.1 %collective-permute-start.17 = (bf16[1,128,256]{2,1,0:T(8,128)(2,1)S(1)}, bf16[1,128,256]{2,1,0:T(8,128)(2,1)S(1)}, u32[]{:S(2)}, u32[]{:S(2)}) collective-permute-start(bf16[1,128,256]{2,1,0:T(8,128)(2,1)S(1)} %get-tuple-element.53), channel_id=1, source_target_pairs={{0,24},{1,25},{2,26},{3,27},{4,28},{5,29},{6,30},{7,31},{8,16},{9,... | collective-permute-start | bytes 196616 | tf_op jit(solution)/shard_map/ppermute | solution.py:118
  46.6 4.3 %collective-permute-start.16 = (bf16[1,128,256]{2,1,0:T(8,128)(2,1)S(1)}, bf16[1,128,256]{2,1,0:T(8,128)(2,1)S(1)}, u32[]{:S(2)}, u32[]{:S(2)}) collective-permute-start(bf16[1,128,256]{2,1,0:T(8,128)(2,1)S(1)} %get-tuple-element.54), channel_id=1, source_target_pairs={{0,8},{1,9},{2,10},{3,11},{4,12},{5,13},{6,14},{7,15},{8,0},{9,1},... | collective-permute-start | bytes 196616 | tf_op jit(solution)/shard_map/ppermute | solution.py:118
  46.7 5.2 %collective-permute-start.15 = (bf16[1,128,256]{2,1,0:T(8,128)(2,1)S(1)}, bf16[1,128,256]{2,1,0:T(8,128)(2,1)S(1)}, u32[]{:S(2)}, u32[]{:S(2)}) collective-permute-start(bf16[1,128,256]{2,1,0:T(8,128)(2,1)S(1)} %get-tuple-element.55), channel_id=1, source_target_pairs={{0,16},{1,17},{2,18},{3,19},{4,20},{5,21},{6,22},{7,23},{8,24},{9,... | collective-permute-start | bytes 196616 | tf_op jit(solution)/shard_map/ppermute | solution.py:118

commit v5 on v4

--- a/solution.py
+++ b/solution.py
@@ -99,6 +99,12 @@
             masks = masks + [(a ^ even_mask, b ^ odd_mask) for a, b in masks]
         found.append(masks[1:])
     return found
+
+
+def turned(position, stages):
+    high, low = 1 << (stages - 1), 1 << (stages - 2)
+    rest = position & ~(high | low)
+    return rest | (low if position & high else 0) | (high if position & low else 0)
 
 
 def chain_rows(live_rows):
@@ -357,6 +363,13 @@
     positions = len(tables[0])
     half = positions // 2
     groups = stage_groups(even_masks, odd_masks)
+    plain = list(range(positions))
+    orders, places = [groups] * chains, [plain] * chains
+    if len(groups) > 2:
+        other = groups[:-2] + groups[-2:][::-1]
+        moved = [turned(p, len(even_masks)) for p in plain]
+        orders = [other if i % 2 else groups for i in range(chains)]
+        places = [moved if i % 2 else plain for i in range(chains)]
 
     me = jnp.reshape(me, (1,))
 
@@ -458,7 +471,7 @@
     def expand(i, part, dtype):
         return pl.pallas_call(
             lambda *refs: expand_kernel(
-                starts[i], range(part * half, (part + 1) * half), *refs
+                starts[i], places[i][part * half : (part + 1) * half], *refs
             ),
             out_shape=jax.ShapeDtypeStruct((half, sizes[i], width), dtype),
             in_specs=[vmem()] * 7,
@@ -516,7 +529,7 @@
                 [value[(j + 1) * left : (j + 2) * left].astype(bf16) for j in range(len(masks))]
                 for value in total
             ]
-        got = [swap(parts, masks) for parts in send]
+        got = [swap(parts, order[k]) for parts, order in zip(send, orders)]
     return pl.pallas_call(
         lambda *refs: spread_rows_kernel(len(keep), *refs),
         out_shape=jax.ShapeDtypeStruct((total_rows, width), bf16),

time: 52.8 us -> 51.6 us (0.977)
  waiting for transfers between devices: 20.4 us -> 19.1 us
    ppermute x18, waiting for transfers between devices: 20.4 us -> 19.1 us  [exchange(): return lax.ppermute(value, 'replica', pairs)]
  transfers between devices with their start and end apart: 18 -> 18, of which waited for: 12 -> 12; matrix products, arithmetic and copies ran while one was open for 0% -> 1% of each run, Pallas kernels for 18% -> 19%
where the time goes in v5:
time: 51.6 us; the launch traced here: 51.4 us
  starting transfers between devices  20.2 us (39%)
  waiting for transfers between devices  19.1 us (37%)
  Pallas kernels  11.6 us (22%)
    ppermute x18, starting transfers between devices, exchange(): return lax.ppermute(value, 'replica', pairs)  20.2 us
    ppermute x18, waiting for transfers between devices, exchange(): return lax.ppermute(value, 'replica', pairs)  19.1 us
    pallas_call x1, Pallas kernels, cut_tiles(): pl.pallas_call(lambda *refs: tiles_kernel(tables, *refs), out_shape=[jax....  2.89 us
    pallas_call x1, Pallas kernels, base_partials(): pl.pallas_call(lambda *refs: base_kernel(tables, *refs), out_shape=[jax.S...  2.53 us
    pallas_call x4, Pallas kernels, expand(): pl.pallas_call(lambda *refs: expand_kernel(starts[i], places[i][part * ha...  1.39 us
    pallas_call x1, Pallas kernels, owner_side(): pl.pallas_call(compact_kernel, out_shape=[jax.ShapeDtypeStruct((live_rows...  1.22 us
    pallas_call x2, Pallas kernels, shrink(): pl.pallas_call(lambda *refs: shrink_kernel(starts[i], range(half, positio...  1.08 us
  transfers between devices with their start and end apart: 18, of which 12 were waited for; matrix products, arithmetic and copies ran while one was open for 1% of the time, Pallas kernels for 19%

profile of v5, /device:TPU:0, one launch (start us, length us, event | category | flops | bytes accessed | tf_op | source)
XLA Modules:
  0.0 51.4 jit_solution(3667884146256652577)
XLA Ops:
  0.0 1.2 %compact_rows.1 = (bf16[128,256]{1,0:T(8,128)(2,1)S(1)}, bf16[152,128]{1,0:T(8,128)(2,1)S(1)}, s32[128,64]{1,0:T(8,128)S(1)}, f32[8,128]{1,0:T(8,128)S(1)}) custom-call(s32[8]{0:T(128)} %rows_hbm.1, bf16[152,256]{1,0:T(8,128)(2,1)} %x_hbm.1, s32[8]{0:T(128)} %wanted_hbm.1, s32[1,128]{1,0:T(1,128)} %bitcast.11), custom_call_target="tpu_custom_call" | custom-call | tf_op jit(solution)/shard_map/compact_rows/pallas_call | solution.py:377
  1.2 5.1 %collective-permute-start.2 = (bf16[1,128,256]{2,1,0:T(8,128)(2,1)S(1)}, bf16[1,128,256]{2,1,0:T(8,128)(2,1)S(1)}, u32[]{:S(2)}, u32[]{:S(2)}) collective-permute-start(bf16[1,128,256]{2,1,0:T(8,128)(2,1)S(1)} %bitcast.5), channel_id=1, source_target_pairs={{0,24},{1,25},{2,26},{3,27},{4,28},{5,29},{6,30},{7,31},{8,16},{9,... | collective-permute-start | bytes 196616 | tf_op jit(solution)/shard_map/ppermute | solution.py:124
  6.3 0.6 %collective-permute-start = (bf16[1,128,256]{2,1,0:T(8,128)(2,1)S(1)}, bf16[1,128,256]{2,1,0:T(8,128)(2,1)S(1)}, u32[]{:S(2)}, u32[]{:S(2)}) collective-permute-start(bf16[1,128,256]{2,1,0:T(8,128)(2,1)S(1)} %bitcast.7), channel_id=1, source_target_pairs={{0,16},{1,17},{2,18},{3,19},{4,20},{5,21},{6,22},{7,23},{8,24},{9,... | collective-permute-start | bytes 196616 | tf_op jit(solution)/shard_map/ppermute | solution.py:124
  7.0 0.7 %find_adapters.1 = (s32[3]{0:T(128)S(1)}, f32[128,64]{1,0:T(8,128)S(1)}) custom-call(s32[1]{0:T(128)} %bitcast.2.refs_0_, f32[8,128]{1,0:T(8,128)S(1)} %get-tuple-element.30.refs_1_, s32[128,64]{1,0:T(8,128)S(1)} %get-tuple-element.31.refs_2_), custom_call_target="tpu_custom_call" | custom-call | tf_op jit(solution)/shard_map/find_adapters/pallas_call | solution.py:403
  7.7 2.9 %cut_tiles.1 = (bf16[16,128,256]{2,1,0:T(8,128)(2,1)S(1)}, bf16[16,128,256]{2,1,0:T(8,128)(2,1)S(1)}, bf16[16,128,256]{2,1,0:T(8,128)(2,1)S(1)}, bf16[16,128,256]{2,1,0:T(8,128)(2,1)S(1)}) custom-call(s32[3]{0:T(128)S(1)} %get-tuple-element.32.refs_0_, bf16[4,64,8192]{2,1,0:T(8,128)(2,1)} %bitcast.9, bf16[4,64,8192]{2,1,0:T(8,128)(2,1)} %bitcast.10), custom_call_target="tpu_custom_call" | custom-call | tf_op jit(solution)/shard_map/cut_tiles/pallas_call | solution.py:416
  11.0 1.0 %collective-permute-done = bf16[1,128,256]{2,1,0:T(8,128)(2,1)S(1)} collective-permute-done((bf16[1,128,256]{2,1,0:T(8,128)(2,1)S(1)}, bf16[1,128,256]{2,1,0:T(8,128)(2,1)S(1)}, u32[]{:S(2)}, u32[]{:S(2)}) %collective-permute-start) | collective-permute-done | bytes 65568 | tf_op jit(solution)/shard_map/ppermute | solution.py:124
  12.1 1.6 %collective-permute-start.3 = (bf16[4,128,256]{2,1,0:T(8,128)(2,1)S(1)}, bf16[4,128,256]{2,1,0:T(8,128)(2,1)S(1)}, u32[]{:S(2)}, u32[]{:S(2)}) collective-permute-start(bf16[4,128,256]{2,1,0:T(8,128)(2,1)S(1)} %pad_maximum_fusion.2), channel_id=1, source_target_pairs={{0,4},{1,3},{2,6},{3,1},{4,0},{5,7},{6,2},{7,5},{8,12},{9,11},{10,... | collective-permute-start | bytes 786440 | tf_op jit(solution)/shard_map/ppermute | solution.py:124
  13.8 2.5 %base_partials.1 = (bf16[16,128,256]{2,1,0:T(8,128)(2,1)S(1)}, f32[16,128,256]{2,1,0:T(8,128)S(1)}) custom-call(s32[1]{0:T(128)} %bitcast.2.refs_0_, bf16[128,256]{1,0:T(8,128)(2,1)S(1)} %get-tuple-element.29.refs_1_, bf16[256,8192]{1,0:T(8,128)(2,1)} %refs_2_.1), custom_call_target="tpu_custom_call" | custom-call | tf_op jit(solution)/shard_map/base_partials/pallas_call | solution.py:435
  16.3 2.2 %collective-permute-done.3 = bf16[4,128,256]{2,1,0:T(8,128)(2,1)S(1)} collective-permute-done((bf16[4,128,256]{2,1,0:T(8,128)(2,1)S(1)}, bf16[4,128,256]{2,1,0:T(8,128)(2,1)S(1)}, u32[]{:S(2)}, u32[]{:S(2)}) %collective-permute-start.3) | collective-permute-done | bytes 262176 | tf_op jit(solution)/shard_map/ppermute | solution.py:124
  18.7 1.6 %collective-permute-start.5 = (bf16[8,64,256]{2,1,0:T(8,128)(2,1)S(1)}, bf16[8,64,256]{2,1,0:T(8,128)(2,1)S(1)}, u32[]{:S(2)}, u32[]{:S(2)}) collective-permute-start(bf16[8,64,256]{2,1,0:T(8,128)(2,1)S(1)} %get-tuple-element.52.refs_0_), channel_id=1, source_target_pairs={{0,2},{1,5},{2,0},{3,7},{4,6},{5,1},{6,4},{7,3},{8,10},{9,13},{10,... | collective-permute-start | bytes 786440 | tf_op jit(solution)/shard_map/ppermute | solution.py:124
  21.8 3.4 %collective-permute-done.5.refs_2_ = bf16[8,64,256]{2,1,0:T(8,128)(2,1)S(1)} collective-permute-done((bf16[8,64,256]{2,1,0:T(8,128)(2,1)S(1)}, bf16[8,64,256]{2,1,0:T(8,128)(2,1)S(1)}, u32[]{:S(2)}, u32[]{:S(2)}) %collective-permute-start.5) | collective-permute-done | bytes 262176 | tf_op jit(solution)/shard_map/ppermute | solution.py:124
  25.8 1.2 %collective-permute-done.6.refs_2_ = f32[64,64]{1,0:T(8,128)S(1)} collective-permute-done((f32[64,64]{1,0:T(8,128)S(1)}, f32[64,64]{1,0:T(8,128)S(1)}, u32[]{:S(2)}, u32[]{:S(2)}) %collective-permute-start.6) | collective-permute-done | bytes 16416 | tf_op jit(solution)/shard_map/ppermute | solution.py:124
  27.3 1.6 %collective-permute-start.9 = (bf16[8,64,256]{2,1,0:T(8,128)(2,1)S(1)}, bf16[8,64,256]{2,1,0:T(8,128)(2,1)S(1)}, u32[]{:S(2)}, u32[]{:S(2)}) collective-permute-start(bf16[8,64,256]{2,1,0:T(8,128)(2,1)S(1)} %expand.5), channel_id=1, source_target_pairs={{0,2},{1,5},{2,0},{3,7},{4,6},{5,1},{6,4},{7,3},{8,10},{9,13},{10,... | collective-permute-start | bytes 786440 | tf_op jit(solution)/shard_map/ppermute | solution.py:124
  29.5 1.2 %collective-permute-done.12.refs_2_ = f32[64,64]{1,0:T(8,128)S(1)} collective-permute-done((f32[64,64]{1,0:T(8,128)S(1)}, f32[64,64]{1,0:T(8,128)S(1)}, u32[]{:S(2)}, u32[]{:S(2)}) %collective-permute-start.12) | collective-permute-done | bytes 16416 | tf_op jit(solution)/shard_map/ppermute | solution.py:124
  31.1 1.6 %collective-permute-start.13 = (bf16[8,64,256]{2,1,0:T(8,128)(2,1)S(1)}, bf16[8,64,256]{2,1,0:T(8,128)(2,1)S(1)}, u32[]{:S(2)}, u32[]{:S(2)}) collective-permute-start(bf16[8,64,256]{2,1,0:T(8,128)(2,1)S(1)} %expand.7), channel_id=1, source_target_pairs={{0,4},{1,3},{2,6},{3,1},{4,0},{5,7},{6,2},{7,5},{8,12},{9,11},{10,... | collective-permute-start | bytes 786440 | tf_op jit(solution)/shard_map/ppermute | solution.py:124
  33.9 1.6 %collective-permute-start.10 = (bf16[4,64,256]{2,1,0:T(8,128)(2,1)S(1)}, bf16[4,64,256]{2,1,0:T(8,128)(2,1)S(1)}, u32[]{:S(2)}, u32[]{:S(2)}) collective-permute-start(bf16[4,64,256]{2,1,0:T(8,128)(2,1)S(1)} %slice.65), channel_id=1, source_target_pairs={{0,4},{1,3},{2,6},{3,1},{4,0},{5,7},{6,2},{7,5},{8,12},{9,11},{10,... | collective-permute-start | bytes 393224 | tf_op jit(solution)/shard_map/ppermute | solution.py:124
  35.5 2.1 %collective-permute-done.13 = bf16[8,64,256]{2,1,0:T(8,128)(2,1)S(1)} collective-permute-done((bf16[8,64,256]{2,1,0:T(8,128)(2,1)S(1)}, bf16[8,64,256]{2,1,0:T(8,128)(2,1)S(1)}, u32[]{:S(2)}, u32[]{:S(2)}) %collective-permute-start.13) | collective-permute-done | bytes 262176 | tf_op jit(solution)/shard_map/ppermute | solution.py:124
  37.6 1.1 %collective-permute-start.14 = (bf16[4,64,256]{2,1,0:T(8,128)(2,1)S(1)}, bf16[4,64,256]{2,1,0:T(8,128)(2,1)S(1)}, u32[]{:S(2)}, u32[]{:S(2)}) collective-permute-start(bf16[4,64,256]{2,1,0:T(8,128)(2,1)S(1)} %slice.64), channel_id=1, source_target_pairs={{0,2},{1,5},{2,0},{3,7},{4,6},{5,1},{6,4},{7,3},{8,10},{9,13},{10,... | collective-permute-start | bytes 393224 | tf_op jit(solution)/shard_map/ppermute | solution.py:124
  39.0 3.7 %collective-permute-done.14 = bf16[4,64,256]{2,1,0:T(8,128)(2,1)S(1)} collective-permute-done((bf16[4,64,256]{2,1,0:T(8,128)(2,1)S(1)}, bf16[4,64,256]{2,1,0:T(8,128)(2,1)S(1)}, u32[]{:S(2)}, u32[]{:S(2)}) %collective-permute-start.14) | collective-permute-done | bytes 131104 | tf_op jit(solution)/shard_map/ppermute | solution.py:124
  42.7 2.5 %collective-permute-start.17 = (bf16[1,128,256]{2,1,0:T(8,128)(2,1)S(1)}, bf16[1,128,256]{2,1,0:T(8,128)(2,1)S(1)}, u32[]{:S(2)}, u32[]{:S(2)}) collective-permute-start(bf16[1,128,256]{2,1,0:T(8,128)(2,1)S(1)} %get-tuple-element.53), channel_id=1, source_target_pairs={{0,24},{1,25},{2,26},{3,27},{4,28},{5,29},{6,30},{7,31},{8,16},{9,... | collective-permute-start | bytes 196616 | tf_op jit(solution)/shard_map/ppermute | solution.py:124
  45.3 1.9 %collective-permute-start.15 = (bf16[1,128,256]{2,1,0:T(8,128)(2,1)S(1)}, bf16[1,128,256]{2,1,0:T(8,128)(2,1)S(1)}, u32[]{:S(2)}, u32[]{:S(2)}) collective-permute-start(bf16[1,128,256]{2,1,0:T(8,128)(2,1)S(1)} %get-tuple-element.55), channel_id=1, source_target_pairs={{0,16},{1,17},{2,18},{3,19},{4,20},{5,21},{6,22},{7,23},{8,24},{9,... | collective-permute-start | bytes 196616 | tf_op jit(solution)/shard_map/ppermute | solution.py:124
  47.2 2.4 %collective-permute-done.17.refs_4_ = bf16[1,128,256]{2,1,0:T(8,128)(2,1)S(1)} collective-permute-done((bf16[1,128,256]{2,1,0:T(8,128)(2,1)S(1)}, bf16[1,128,256]{2,1,0:T(8,128)(2,1)S(1)}, u32[]{:S(2)}, u32[]{:S(2)}) %collective-permute-start.17) | collective-permute-done | bytes 65568 | tf_op jit(solution)/shard_map/ppermute | solution.py:124
  49.6 1.0 %collective-permute-done.16.refs_3_ = bf16[1,128,256]{2,1,0:T(8,128)(2,1)S(1)} collective-permute-done((bf16[1,128,256]{2,1,0:T(8,128)(2,1)S(1)}, bf16[1,128,256]{2,1,0:T(8,128)(2,1)S(1)}, u32[]{:S(2)}, u32[]{:S(2)}) %collective-permute-start.16) | collective-permute-done | bytes 65568 | tf_op jit(solution)/shard_map/ppermute | solution.py:124
  50.6 0.8 %spread_rows.1 = bf16[152,256]{1,0:T(8,128)(2,1)} custom-call(bf16[152,128]{1,0:T(8,128)(2,1)S(1)} %get-tuple-element.28.refs_0_, f32[1,128,256]{2,1,0:T(8,128)S(1)} %fusion.1.refs_1_, bf16[1,128,256]{2,1,0:T(8,128)(2,1)S(1)} %collective-permute-done.15.refs_2_, bf16[1,128,256]{2,1,0:T(8,128)(2,1)S(1)} %collective-permute-done.16.refs_3_, ...), custom_call_target="tpu_custom_call" | custom-call | tf_op jit(solution)/shard_map/spread_rows/pallas_call | solution.py:533
  (37 shorter events, 5.8 us)
Async XLA Ops:
  1.2 9.4 %collective-permute-start.2 = (bf16[1,128,256]{2,1,0:T(8,128)(2,1)S(1)}, bf16[1,128,256]{2,1,0:T(8,128)(2,1)S(1)}, u32[]{:S(2)}, u32[]{:S(2)}) collective-permute-start(bf16[1,128,256]{2,1,0:T(8,128)(2,1)S(1)} %bitcast.5), channel_id=1, source_target_pairs={{0,24},{1,25},{2,26},{3,27},{4,28},{5,29},{6,30},{7,31},{8,16},{9,... | collective-permute-start | bytes 196616 | tf_op jit(solution)/shard_map/ppermute | solution.py:124
  6.3 4.7 %collective-permute-start.1 = (bf16[1,128,256]{2,1,0:T(8,128)(2,1)S(1)}, bf16[1,128,256]{2,1,0:T(8,128)(2,1)S(1)}, u32[]{:S(2)}, u32[]{:S(2)}) collective-permute-start(bf16[1,128,256]{2,1,0:T(8,128)(2,1)S(1)} %bitcast.6), channel_id=1, source_target_pairs={{0,8},{1,9},{2,10},{3,11},{4,12},{5,13},{6,14},{7,15},{8,0},{9,1},... | collective-permute-start | bytes 196616 | tf_op jit(solution)/shard_map/ppermute | solution.py:124
  6.3 5.6 %collective-permute-start = (bf16[1,128,256]{2,1,0:T(8,128)(2,1)S(1)}, bf16[1,128,256]{2,1,0:T(8,128)(2,1)S(1)}, u32[]{:S(2)}, u32[]{:S(2)}) collective-permute-start(bf16[1,128,256]{2,1,0:T(8,128)(2,1)S(1)} %bitcast.7), channel_id=1, source_target_pairs={{0,16},{1,17},{2,18},{3,19},{4,20},{5,21},{6,22},{7,23},{8,24},{9,... | collective-permute-start | bytes 196616 | tf_op jit(solution)/shard_map/ppermute | solution.py:124
  12.0 6.6 %collective-permute-start.4 = (bf16[16,128,256]{2,1,0:T(8,128)(2,1)S(1)}, bf16[16,128,256]{2,1,0:T(8,128)(2,1)S(1)}, u32[]{:S(2)}, u32[]{:S(2)}) collective-permute-start(bf16[16,128,256]{2,1,0:T(8,128)(2,1)S(1)} %get-tuple-element.38), channel_id=1, source_target_pairs={{0,1},{1,0},{2,3},{3,2},{4,5},{5,4},{6,7},{7,6},{8,9},{9,8},{10,11... | collective-permute-start | bytes 3145736 | tf_op jit(solution)/shard_map/ppermute | solution.py:124
  12.1 6.4 %collective-permute-start.3 = (bf16[4,128,256]{2,1,0:T(8,128)(2,1)S(1)}, bf16[4,128,256]{2,1,0:T(8,128)(2,1)S(1)}, u32[]{:S(2)}, u32[]{:S(2)}) collective-permute-start(bf16[4,128,256]{2,1,0:T(8,128)(2,1)S(1)} %pad_maximum_fusion.2), channel_id=1, source_target_pairs={{0,4},{1,3},{2,6},{3,1},{4,0},{5,7},{6,2},{7,5},{8,12},{9,11},{10,... | collective-permute-start | bytes 786440 | tf_op jit(solution)/shard_map/ppermute | solution.py:124
  13.7 12.1 %collective-permute-start.8 = (bf16[16,128,256]{2,1,0:T(8,128)(2,1)S(1)}, bf16[16,128,256]{2,1,0:T(8,128)(2,1)S(1)}, u32[]{:S(2)}, u32[]{:S(2)}) collective-permute-start(bf16[16,128,256]{2,1,0:T(8,128)(2,1)S(1)} %get-tuple-element.49), channel_id=1, source_target_pairs={{0,1},{1,0},{2,3},{3,2},{4,5},{5,4},{6,7},{7,6},{8,9},{9,8},{10,11... | collective-permute-start | bytes 3145736 | tf_op jit(solution)/shard_map/ppermute | solution.py:124
  18.6 8.4 %collective-permute-start.7 = (bf16[16,128,256]{2,1,0:T(8,128)(2,1)S(1)}, bf16[16,128,256]{2,1,0:T(8,128)(2,1)S(1)}, u32[]{:S(2)}, u32[]{:S(2)}) collective-permute-start(bf16[16,128,256]{2,1,0:T(8,128)(2,1)S(1)} %get-tuple-element.47), channel_id=1, source_target_pairs={{0,1},{1,0},{2,3},{3,2},{4,5},{5,4},{6,7},{7,6},{8,9},{9,8},{10,11... | collective-permute-start | bytes 3145736 | tf_op jit(solution)/shard_map/ppermute | solution.py:124
  18.7 6.4 %collective-permute-start.5 = (bf16[8,64,256]{2,1,0:T(8,128)(2,1)S(1)}, bf16[8,64,256]{2,1,0:T(8,128)(2,1)S(1)}, u32[]{:S(2)}, u32[]{:S(2)}) collective-permute-start(bf16[8,64,256]{2,1,0:T(8,128)(2,1)S(1)} %get-tuple-element.52.refs_0_), channel_id=1, source_target_pairs={{0,2},{1,5},{2,0},{3,7},{4,6},{5,1},{6,4},{7,3},{8,10},{9,13},{10,... | collective-permute-start | bytes 786440 | tf_op jit(solution)/shard_map/ppermute | solution.py:124
  20.3 8.6 %collective-permute-start.11 = (bf16[8,64,256]{2,1,0:T(8,128)(2,1)S(1)}, bf16[8,64,256]{2,1,0:T(8,128)(2,1)S(1)}, u32[]{:S(2)}, u32[]{:S(2)}) collective-permute-start(bf16[8,64,256]{2,1,0:T(8,128)(2,1)S(1)} %get-tuple-element.51.refs_0_), channel_id=1, source_target_pairs={{0,2},{1,5},{2,0},{3,7},{4,6},{5,1},{6,4},{7,3},{8,10},{9,13},{10,... | collective-permute-start | bytes 786440 | tf_op jit(solution)/shard_map/ppermute | solution.py:124
  25.7 1.3 %collective-permute-start.6 = (f32[64,64]{1,0:T(8,128)S(1)}, f32[64,64]{1,0:T(8,128)S(1)}, u32[]{:S(2)}, u32[]{:S(2)}) collective-permute-start(f32[64,64]{1,0:T(8,128)S(1)} %shrink.2.refs_1_), channel_id=1, source_target_pairs={{0,1},{1,0},{2,3},{3,2},{4,5},{5,4},{6,7},{7,6},{8,9},{9,8},{10,11... | collective-permute-start | bytes 49160 | tf_op jit(solution)/shard_map/ppermute | solution.py:124
  27.3 6.4 %collective-permute-start.9 = (bf16[8,64,256]{2,1,0:T(8,128)(2,1)S(1)}, bf16[8,64,256]{2,1,0:T(8,128)(2,1)S(1)}, u32[]{:S(2)}, u32[]{:S(2)}) collective-permute-start(bf16[8,64,256]{2,1,0:T(8,128)(2,1)S(1)} %expand.5), channel_id=1, source_target_pairs={{0,2},{1,5},{2,0},{3,7},{4,6},{5,1},{6,4},{7,3},{8,10},{9,13},{10,... | collective-permute-start | bytes 786440 | tf_op jit(solution)/shard_map/ppermute | solution.py:124
  29.4 1.3 %collective-permute-start.12 = (f32[64,64]{1,0:T(8,128)S(1)}, f32[64,64]{1,0:T(8,128)S(1)}, u32[]{:S(2)}, u32[]{:S(2)}) collective-permute-start(f32[64,64]{1,0:T(8,128)S(1)} %shrink.3.refs_1_), channel_id=1, source_target_pairs={{0,1},{1,0},{2,3},{3,2},{4,5},{5,4},{6,7},{7,6},{8,9},{9,8},{10,11... | collective-permute-start | bytes 49160 | tf_op jit(solution)/shard_map/ppermute | solution.py:124
  31.1 6.4 %collective-permute-start.13 = (bf16[8,64,256]{2,1,0:T(8,128)(2,1)S(1)}, bf16[8,64,256]{2,1,0:T(8,128)(2,1)S(1)}, u32[]{:S(2)}, u32[]{:S(2)}) collective-permute-start(bf16[8,64,256]{2,1,0:T(8,128)(2,1)S(1)} %expand.7), channel_id=1, source_target_pairs={{0,4},{1,3},{2,6},{3,1},{4,0},{5,7},{6,2},{7,5},{8,12},{9,11},{10,... | collective-permute-start | bytes 786440 | tf_op jit(solution)/shard_map/ppermute | solution.py:124
  33.9 5.1 %collective-permute-start.10 = (bf16[4,64,256]{2,1,0:T(8,128)(2,1)S(1)}, bf16[4,64,256]{2,1,0:T(8,128)(2,1)S(1)}, u32[]{:S(2)}, u32[]{:S(2)}) collective-permute-start(bf16[4,64,256]{2,1,0:T(8,128)(2,1)S(1)} %slice.65), channel_id=1, source_target_pairs={{0,4},{1,3},{2,6},{3,1},{4,0},{5,7},{6,2},{7,5},{8,12},{9,11},{10,... | collective-permute-start | bytes 393224 | tf_op jit(solution)/shard_map/ppermute | solution.py:124
  37.6 5.0 %collective-permute-start.14 = (bf16[4,64,256]{2,1,0:T(8,128)(2,1)S(1)}, bf16[4,64,256]{2,1,0:T(8,128)(2,1)S(1)}, u32[]{:S(2)}, u32[]{:S(2)}) collective-permute-start(bf16[4,64,256]{2,1,0:T(8,128)(2,1)S(1)} %slice.64), channel_id=1, source_target_pairs={{0,2},{1,5},{2,0},{3,7},{4,6},{5,1},{6,4},{7,3},{8,10},{9,13},{10,... | collective-permute-start | bytes 393224 | tf_op jit(solution)/shard_map/ppermute | solution.py:124
  42.7 6.9 %collective-permute-start.17 = (bf16[1,128,256]{2,1,0:T(8,128)(2,1)S(1)}, bf16[1,128,256]{2,1,0:T(8,128)(2,1)S(1)}, u32[]{:S(2)}, u32[]{:S(2)}) collective-permute-start(bf16[1,128,256]{2,1,0:T(8,128)(2,1)S(1)} %get-tuple-element.53), channel_id=1, source_target_pairs={{0,24},{1,25},{2,26},{3,27},{4,28},{5,29},{6,30},{7,31},{8,16},{9,... | collective-permute-start | bytes 196616 | tf_op jit(solution)/shard_map/ppermute | solution.py:124
  45.2 5.4 %collective-permute-start.16 = (bf16[1,128,256]{2,1,0:T(8,128)(2,1)S(1)}, bf16[1,128,256]{2,1,0:T(8,128)(2,1)S(1)}, u32[]{:S(2)}, u32[]{:S(2)}) collective-permute-start(bf16[1,128,256]{2,1,0:T(8,128)(2,1)S(1)} %get-tuple-element.54), channel_id=1, source_target_pairs={{0,8},{1,9},{2,10},{3,11},{4,12},{5,13},{6,14},{7,15},{8,0},{9,1},... | collective-permute-start | bytes 196616 | tf_op jit(solution)/shard_map/ppermute | solution.py:124
  45.3 5.3 %collective-permute-start.15 = (bf16[1,128,256]{2,1,0:T(8,128)(2,1)S(1)}, bf16[1,128,256]{2,1,0:T(8,128)(2,1)S(1)}, u32[]{:S(2)}, u32[]{:S(2)}) collective-permute-start(bf16[1,128,256]{2,1,0:T(8,128)(2,1)S(1)} %get-tuple-element.55), channel_id=1, source_target_pairs={{0,16},{1,17},{2,18},{3,19},{4,20},{5,21},{6,22},{7,23},{8,24},{9,... | collective-permute-start | bytes 196616 | tf_op jit(solution)/shard_map/ppermute | solution.py:124

commit v6 on v5

--- a/solution.py
+++ b/solution.py
@@ -500,8 +500,6 @@
             down_peer = exchange(down_send, 1, 1)
             up_peer = exchange(up_send, 1, 1)
         if k == cut_at:
-            gathered, down_peer = after((gathered, down_peer))
-        if k == cut_at:
             base_send, base_keep = base_partials(after(me, before))
             gathered, base_send = after((gathered, base_send))
             base_got = exchange(base_send, 1, 1)

time: 51.6 us -> 51.6 us (level)
  no operation moved by 1% of the time
where the time goes in v6:
time: 51.6 us; the launch traced here: 51.3 us
  starting transfers between devices  20.4 us (40%)
  waiting for transfers between devices  18.7 us (36%)
  Pallas kernels  11.6 us (22%)
    ppermute x18, starting transfers between devices, exchange(): return lax.ppermute(value, 'replica', pairs)  20.4 us
    ppermute x18, waiting for transfers between devices, exchange(): return lax.ppermute(value, 'replica', pairs)  18.7 us
    pallas_call x1, Pallas kernels, cut_tiles(): pl.pallas_call(lambda *refs: tiles_kernel(tables, *refs), out_shape=[jax....  2.89 us
    pallas_call x1, Pallas kernels, base_partials(): pl.pallas_call(lambda *refs: base_kernel(tables, *refs), out_shape=[jax.S...  2.52 us
    pallas_call x4, Pallas kernels, expand(): pl.pallas_call(lambda *refs: expand_kernel(starts[i], places[i][part * ha...  1.4 us
    pallas_call x1, Pallas kernels, owner_side(): pl.pallas_call(compact_kernel, out_shape=[jax.ShapeDtypeStruct((live_rows...  1.22 us
    pallas_call x2, Pallas kernels, shrink(): pl.pallas_call(lambda *refs: shrink_kernel(starts[i], range(half, positio...  1.09 us
  transfers between devices with their start and end apart: 18, of which 12 were waited for; matrix products, arithmetic and copies ran while one was open for 1% of the time, Pallas kernels for 19%

profile of v6, /device:TPU:0, one launch (start us, length us, event | category | flops | bytes accessed | tf_op | source)
XLA Modules:
  0.0 51.3 jit_solution(12895647868809161577)
XLA Ops:
  0.0 1.2 %compact_rows.1 = (bf16[128,256]{1,0:T(8,128)(2,1)S(1)}, bf16[152,128]{1,0:T(8,128)(2,1)S(1)}, s32[128,64]{1,0:T(8,128)S(1)}, f32[8,128]{1,0:T(8,128)S(1)}) custom-call(s32[8]{0:T(128)} %rows_hbm.1, bf16[152,256]{1,0:T(8,128)(2,1)} %x_hbm.1, s32[8]{0:T(128)} %wanted_hbm.1, s32[1,128]{1,0:T(1,128)} %bitcast.11), custom_call_target="tpu_custom_call" | custom-call | tf_op jit(solution)/shard_map/compact_rows/pallas_call | solution.py:377
  1.2 5.1 %collective-permute-start.2 = (bf16[1,128,256]{2,1,0:T(8,128)(2,1)S(1)}, bf16[1,128,256]{2,1,0:T(8,128)(2,1)S(1)}, u32[]{:S(2)}, u32[]{:S(2)}) collective-permute-start(bf16[1,128,256]{2,1,0:T(8,128)(2,1)S(1)} %bitcast.5), channel_id=1, source_target_pairs={{0,24},{1,25},{2,26},{3,27},{4,28},{5,29},{6,30},{7,31},{8,16},{9,... | collective-permute-start | bytes 196616 | tf_op jit(solution)/shard_map/ppermute | solution.py:124
  6.3 0.6 %collective-permute-start = (bf16[1,128,256]{2,1,0:T(8,128)(2,1)S(1)}, bf16[1,128,256]{2,1,0:T(8,128)(2,1)S(1)}, u32[]{:S(2)}, u32[]{:S(2)}) collective-permute-start(bf16[1,128,256]{2,1,0:T(8,128)(2,1)S(1)} %bitcast.7), channel_id=1, source_target_pairs={{0,16},{1,17},{2,18},{3,19},{4,20},{5,21},{6,22},{7,23},{8,24},{9,... | collective-permute-start | bytes 196616 | tf_op jit(solution)/shard_map/ppermute | solution.py:124
  7.0 0.7 %find_adapters.1 = (s32[3]{0:T(128)S(1)}, f32[128,64]{1,0:T(8,128)S(1)}) custom-call(s32[1]{0:T(128)} %bitcast.2.refs_0_, f32[8,128]{1,0:T(8,128)S(1)} %get-tuple-element.28.refs_1_, s32[128,64]{1,0:T(8,128)S(1)} %get-tuple-element.29.refs_2_), custom_call_target="tpu_custom_call" | custom-call | tf_op jit(solution)/shard_map/find_adapters/pallas_call | solution.py:403
  7.7 2.9 %cut_tiles.1 = (bf16[16,128,256]{2,1,0:T(8,128)(2,1)S(1)}, bf16[16,128,256]{2,1,0:T(8,128)(2,1)S(1)}, bf16[16,128,256]{2,1,0:T(8,128)(2,1)S(1)}, bf16[16,128,256]{2,1,0:T(8,128)(2,1)S(1)}) custom-call(s32[3]{0:T(128)S(1)} %get-tuple-element.30.refs_0_, bf16[4,64,8192]{2,1,0:T(8,128)(2,1)} %bitcast.9, bf16[4,64,8192]{2,1,0:T(8,128)(2,1)} %bitcast.10), custom_call_target="tpu_custom_call" | custom-call | tf_op jit(solution)/shard_map/cut_tiles/pallas_call | solution.py:416
  11.0 1.0 %collective-permute-done = bf16[1,128,256]{2,1,0:T(8,128)(2,1)S(1)} collective-permute-done((bf16[1,128,256]{2,1,0:T(8,128)(2,1)S(1)}, bf16[1,128,256]{2,1,0:T(8,128)(2,1)S(1)}, u32[]{:S(2)}, u32[]{:S(2)}) %collective-permute-start) | collective-permute-done | bytes 65568 | tf_op jit(solution)/shard_map/ppermute | solution.py:124
  12.0 1.6 %collective-permute-start.3 = (bf16[4,128,256]{2,1,0:T(8,128)(2,1)S(1)}, bf16[4,128,256]{2,1,0:T(8,128)(2,1)S(1)}, u32[]{:S(2)}, u32[]{:S(2)}) collective-permute-start(bf16[4,128,256]{2,1,0:T(8,128)(2,1)S(1)} %pad_maximum_fusion.2), channel_id=1, source_target_pairs={{0,4},{1,3},{2,6},{3,1},{4,0},{5,7},{6,2},{7,5},{8,12},{9,11},{10,... | collective-permute-start | bytes 786440 | tf_op jit(solution)/shard_map/ppermute | solution.py:124
  14.1 2.5 %base_partials.1 = (bf16[16,128,256]{2,1,0:T(8,128)(2,1)S(1)}, f32[16,128,256]{2,1,0:T(8,128)S(1)}) custom-call(s32[1]{0:T(128)} %bitcast.2.refs_0_, bf16[128,256]{1,0:T(8,128)(2,1)S(1)} %get-tuple-element.27.refs_1_, bf16[256,8192]{1,0:T(8,128)(2,1)} %refs_2_.1), custom_call_target="tpu_custom_call" | custom-call | tf_op jit(solution)/shard_map/base_partials/pallas_call | solution.py:435
  16.6 1.8 %collective-permute-done.3 = bf16[4,128,256]{2,1,0:T(8,128)(2,1)S(1)} collective-permute-done((bf16[4,128,256]{2,1,0:T(8,128)(2,1)S(1)}, bf16[4,128,256]{2,1,0:T(8,128)(2,1)S(1)}, u32[]{:S(2)}, u32[]{:S(2)}) %collective-permute-start.3) | collective-permute-done | bytes 262176 | tf_op jit(solution)/shard_map/ppermute | solution.py:124
  18.6 1.6 %collective-permute-start.5 = (bf16[8,64,256]{2,1,0:T(8,128)(2,1)S(1)}, bf16[8,64,256]{2,1,0:T(8,128)(2,1)S(1)}, u32[]{:S(2)}, u32[]{:S(2)}) collective-permute-start(bf16[8,64,256]{2,1,0:T(8,128)(2,1)S(1)} %get-tuple-element.48.refs_0_), channel_id=1, source_target_pairs={{0,2},{1,5},{2,0},{3,7},{4,6},{5,1},{6,4},{7,3},{8,10},{9,13},{10,... | collective-permute-start | bytes 786440 | tf_op jit(solution)/shard_map/ppermute | solution.py:124
  21.7 3.4 %collective-permute-done.5.refs_2_ = bf16[8,64,256]{2,1,0:T(8,128)(2,1)S(1)} collective-permute-done((bf16[8,64,256]{2,1,0:T(8,128)(2,1)S(1)}, bf16[8,64,256]{2,1,0:T(8,128)(2,1)S(1)}, u32[]{:S(2)}, u32[]{:S(2)}) %collective-permute-start.5) | collective-permute-done | bytes 262176 | tf_op jit(solution)/shard_map/ppermute | solution.py:124
  25.7 1.2 %collective-permute-done.6.refs_2_ = f32[64,64]{1,0:T(8,128)S(1)} collective-permute-done((f32[64,64]{1,0:T(8,128)S(1)}, f32[64,64]{1,0:T(8,128)S(1)}, u32[]{:S(2)}, u32[]{:S(2)}) %collective-permute-start.6) | collective-permute-done | bytes 16416 | tf_op jit(solution)/shard_map/ppermute | solution.py:124
  27.3 1.6 %collective-permute-start.9 = (bf16[8,64,256]{2,1,0:T(8,128)(2,1)S(1)}, bf16[8,64,256]{2,1,0:T(8,128)(2,1)S(1)}, u32[]{:S(2)}, u32[]{:S(2)}) collective-permute-start(bf16[8,64,256]{2,1,0:T(8,128)(2,1)S(1)} %expand.5), channel_id=1, source_target_pairs={{0,2},{1,5},{2,0},{3,7},{4,6},{5,1},{6,4},{7,3},{8,10},{9,13},{10,... | collective-permute-start | bytes 786440 | tf_op jit(solution)/shard_map/ppermute | solution.py:124
  29.4 1.2 %collective-permute-done.12.refs_2_ = f32[64,64]{1,0:T(8,128)S(1)} collective-permute-done((f32[64,64]{1,0:T(8,128)S(1)}, f32[64,64]{1,0:T(8,128)S(1)}, u32[]{:S(2)}, u32[]{:S(2)}) %collective-permute-start.12) | collective-permute-done | bytes 16416 | tf_op jit(solution)/shard_map/ppermute | solution.py:124
  31.0 1.6 %collective-permute-start.13 = (bf16[8,64,256]{2,1,0:T(8,128)(2,1)S(1)}, bf16[8,64,256]{2,1,0:T(8,128)(2,1)S(1)}, u32[]{:S(2)}, u32[]{:S(2)}) collective-permute-start(bf16[8,64,256]{2,1,0:T(8,128)(2,1)S(1)} %expand.7), channel_id=1, source_target_pairs={{0,4},{1,3},{2,6},{3,1},{4,0},{5,7},{6,2},{7,5},{8,12},{9,11},{10,... | collective-permute-start | bytes 786440 | tf_op jit(solution)/shard_map/ppermute | solution.py:124
  33.8 1.6 %collective-permute-start.10 = (bf16[4,64,256]{2,1,0:T(8,128)(2,1)S(1)}, bf16[4,64,256]{2,1,0:T(8,128)(2,1)S(1)}, u32[]{:S(2)}, u32[]{:S(2)}) collective-permute-start(bf16[4,64,256]{2,1,0:T(8,128)(2,1)S(1)} %slice.65), channel_id=1, source_target_pairs={{0,4},{1,3},{2,6},{3,1},{4,0},{5,7},{6,2},{7,5},{8,12},{9,11},{10,... | collective-permute-start | bytes 393224 | tf_op jit(solution)/shard_map/ppermute | solution.py:124
  35.4 2.1 %collective-permute-done.13 = bf16[8,64,256]{2,1,0:T(8,128)(2,1)S(1)} collective-permute-done((bf16[8,64,256]{2,1,0:T(8,128)(2,1)S(1)}, bf16[8,64,256]{2,1,0:T(8,128)(2,1)S(1)}, u32[]{:S(2)}, u32[]{:S(2)}) %collective-permute-start.13) | collective-permute-done | bytes 262176 | tf_op jit(solution)/shard_map/ppermute | solution.py:124
  37.5 1.1 %collective-permute-start.14 = (bf16[4,64,256]{2,1,0:T(8,128)(2,1)S(1)}, bf16[4,64,256]{2,1,0:T(8,128)(2,1)S(1)}, u32[]{:S(2)}, u32[]{:S(2)}) collective-permute-start(bf16[4,64,256]{2,1,0:T(8,128)(2,1)S(1)} %slice.64), channel_id=1, source_target_pairs={{0,2},{1,5},{2,0},{3,7},{4,6},{5,1},{6,4},{7,3},{8,10},{9,13},{10,... | collective-permute-start | bytes 393224 | tf_op jit(solution)/shard_map/ppermute | solution.py:124
  38.9 3.7 %collective-permute-done.14 = bf16[4,64,256]{2,1,0:T(8,128)(2,1)S(1)} collective-permute-done((bf16[4,64,256]{2,1,0:T(8,128)(2,1)S(1)}, bf16[4,64,256]{2,1,0:T(8,128)(2,1)S(1)}, u32[]{:S(2)}, u32[]{:S(2)}) %collective-permute-start.14) | collective-permute-done | bytes 131104 | tf_op jit(solution)/shard_map/ppermute | solution.py:124
  42.6 2.5 %collective-permute-start.17 = (bf16[1,128,256]{2,1,0:T(8,128)(2,1)S(1)}, bf16[1,128,256]{2,1,0:T(8,128)(2,1)S(1)}, u32[]{:S(2)}, u32[]{:S(2)}) collective-permute-start(bf16[1,128,256]{2,1,0:T(8,128)(2,1)S(1)} %get-tuple-element.49), channel_id=1, source_target_pairs={{0,24},{1,25},{2,26},{3,27},{4,28},{5,29},{6,30},{7,31},{8,16},{9,... | collective-permute-start | bytes 196616 | tf_op jit(solution)/shard_map/ppermute | solution.py:124
  45.2 1.9 %collective-permute-start.15 = (bf16[1,128,256]{2,1,0:T(8,128)(2,1)S(1)}, bf16[1,128,256]{2,1,0:T(8,128)(2,1)S(1)}, u32[]{:S(2)}, u32[]{:S(2)}) collective-permute-start(bf16[1,128,256]{2,1,0:T(8,128)(2,1)S(1)} %get-tuple-element.51), channel_id=1, source_target_pairs={{0,16},{1,17},{2,18},{3,19},{4,20},{5,21},{6,22},{7,23},{8,24},{9,... | collective-permute-start | bytes 196616 | tf_op jit(solution)/shard_map/ppermute | solution.py:124
  47.1 2.2 %collective-permute-done.17.refs_4_ = bf16[1,128,256]{2,1,0:T(8,128)(2,1)S(1)} collective-permute-done((bf16[1,128,256]{2,1,0:T(8,128)(2,1)S(1)}, bf16[1,128,256]{2,1,0:T(8,128)(2,1)S(1)}, u32[]{:S(2)}, u32[]{:S(2)}) %collective-permute-start.17) | collective-permute-done | bytes 65568 | tf_op jit(solution)/shard_map/ppermute | solution.py:124
  49.3 1.2 %collective-permute-done.16.refs_3_ = bf16[1,128,256]{2,1,0:T(8,128)(2,1)S(1)} collective-permute-done((bf16[1,128,256]{2,1,0:T(8,128)(2,1)S(1)}, bf16[1,128,256]{2,1,0:T(8,128)(2,1)S(1)}, u32[]{:S(2)}, u32[]{:S(2)}) %collective-permute-start.16) | collective-permute-done | bytes 65568 | tf_op jit(solution)/shard_map/ppermute | solution.py:124
  50.5 0.8 %spread_rows.1 = bf16[152,256]{1,0:T(8,128)(2,1)} custom-call(bf16[152,128]{1,0:T(8,128)(2,1)S(1)} %get-tuple-element.26.refs_0_, f32[1,128,256]{2,1,0:T(8,128)S(1)} %fusion.1.refs_1_, bf16[1,128,256]{2,1,0:T(8,128)(2,1)S(1)} %collective-permute-done.15.refs_2_, bf16[1,128,256]{2,1,0:T(8,128)(2,1)S(1)} %collective-permute-done.16.refs_3_, ...), custom_call_target="tpu_custom_call" | custom-call | tf_op jit(solution)/shard_map/spread_rows/pallas_call | solution.py:531
  (37 shorter events, 6.2 us)
Async XLA Ops:
  1.2 9.4 %collective-permute-start.2 = (bf16[1,128,256]{2,1,0:T(8,128)(2,1)S(1)}, bf16[1,128,256]{2,1,0:T(8,128)(2,1)S(1)}, u32[]{:S(2)}, u32[]{:S(2)}) collective-permute-start(bf16[1,128,256]{2,1,0:T(8,128)(2,1)S(1)} %bitcast.5), channel_id=1, source_target_pairs={{0,24},{1,25},{2,26},{3,27},{4,28},{5,29},{6,30},{7,31},{8,16},{9,... | collective-permute-start | bytes 196616 | tf_op jit(solution)/shard_map/ppermute | solution.py:124
  6.3 4.7 %collective-permute-start.1 = (bf16[1,128,256]{2,1,0:T(8,128)(2,1)S(1)}, bf16[1,128,256]{2,1,0:T(8,128)(2,1)S(1)}, u32[]{:S(2)}, u32[]{:S(2)}) collective-permute-start(bf16[1,128,256]{2,1,0:T(8,128)(2,1)S(1)} %bitcast.6), channel_id=1, source_target_pairs={{0,8},{1,9},{2,10},{3,11},{4,12},{5,13},{6,14},{7,15},{8,0},{9,1},... | collective-permute-start | bytes 196616 | tf_op jit(solution)/shard_map/ppermute | solution.py:124
  6.3 5.6 %collective-permute-start = (bf16[1,128,256]{2,1,0:T(8,128)(2,1)S(1)}, bf16[1,128,256]{2,1,0:T(8,128)(2,1)S(1)}, u32[]{:S(2)}, u32[]{:S(2)}) collective-permute-start(bf16[1,128,256]{2,1,0:T(8,128)(2,1)S(1)} %bitcast.7), channel_id=1, source_target_pairs={{0,16},{1,17},{2,18},{3,19},{4,20},{5,21},{6,22},{7,23},{8,24},{9,... | collective-permute-start | bytes 196616 | tf_op jit(solution)/shard_map/ppermute | solution.py:124
  12.0 6.4 %collective-permute-start.3 = (bf16[4,128,256]{2,1,0:T(8,128)(2,1)S(1)}, bf16[4,128,256]{2,1,0:T(8,128)(2,1)S(1)}, u32[]{:S(2)}, u32[]{:S(2)}) collective-permute-start(bf16[4,128,256]{2,1,0:T(8,128)(2,1)S(1)} %pad_maximum_fusion.2), channel_id=1, source_target_pairs={{0,4},{1,3},{2,6},{3,1},{4,0},{5,7},{6,2},{7,5},{8,12},{9,11},{10,... | collective-permute-start | bytes 786440 | tf_op jit(solution)/shard_map/ppermute | solution.py:124
  13.6 7.1 %collective-permute-start.4 = (bf16[16,128,256]{2,1,0:T(8,128)(2,1)S(1)}, bf16[16,128,256]{2,1,0:T(8,128)(2,1)S(1)}, u32[]{:S(2)}, u32[]{:S(2)}) collective-permute-start(bf16[16,128,256]{2,1,0:T(8,128)(2,1)S(1)} %get-tuple-element.40), channel_id=1, source_target_pairs={{0,1},{1,0},{2,3},{3,2},{4,5},{5,4},{6,7},{7,6},{8,9},{9,8},{10,11... | collective-permute-start | bytes 3145736 | tf_op jit(solution)/shard_map/ppermute | solution.py:124
  13.6 12.1 %collective-permute-start.8 = (bf16[16,128,256]{2,1,0:T(8,128)(2,1)S(1)}, bf16[16,128,256]{2,1,0:T(8,128)(2,1)S(1)}, u32[]{:S(2)}, u32[]{:S(2)}) collective-permute-start(bf16[16,128,256]{2,1,0:T(8,128)(2,1)S(1)} %get-tuple-element.45), channel_id=1, source_target_pairs={{0,1},{1,0},{2,3},{3,2},{4,5},{5,4},{6,7},{7,6},{8,9},{9,8},{10,11... | collective-permute-start | bytes 3145736 | tf_op jit(solution)/shard_map/ppermute | solution.py:124
  18.5 8.4 %collective-permute-start.7 = (bf16[16,128,256]{2,1,0:T(8,128)(2,1)S(1)}, bf16[16,128,256]{2,1,0:T(8,128)(2,1)S(1)}, u32[]{:S(2)}, u32[]{:S(2)}) collective-permute-start(bf16[16,128,256]{2,1,0:T(8,128)(2,1)S(1)} %get-tuple-element.43), channel_id=1, source_target_pairs={{0,1},{1,0},{2,3},{3,2},{4,5},{5,4},{6,7},{7,6},{8,9},{9,8},{10,11... | collective-permute-start | bytes 3145736 | tf_op jit(solution)/shard_map/ppermute | solution.py:124
  18.6 6.4 %collective-permute-start.5 = (bf16[8,64,256]{2,1,0:T(8,128)(2,1)S(1)}, bf16[8,64,256]{2,1,0:T(8,128)(2,1)S(1)}, u32[]{:S(2)}, u32[]{:S(2)}) collective-permute-start(bf16[8,64,256]{2,1,0:T(8,128)(2,1)S(1)} %get-tuple-element.48.refs_0_), channel_id=1, source_target_pairs={{0,2},{1,5},{2,0},{3,7},{4,6},{5,1},{6,4},{7,3},{8,10},{9,13},{10,... | collective-permute-start | bytes 786440 | tf_op jit(solution)/shard_map/ppermute | solution.py:124
  20.2 8.6 %collective-permute-start.11 = (bf16[8,64,256]{2,1,0:T(8,128)(2,1)S(1)}, bf16[8,64,256]{2,1,0:T(8,128)(2,1)S(1)}, u32[]{:S(2)}, u32[]{:S(2)}) collective-permute-start(bf16[8,64,256]{2,1,0:T(8,128)(2,1)S(1)} %get-tuple-element.47.refs_0_), channel_id=1, source_target_pairs={{0,2},{1,5},{2,0},{3,7},{4,6},{5,1},{6,4},{7,3},{8,10},{9,13},{10,... | collective-permute-start | bytes 786440 | tf_op jit(solution)/shard_map/ppermute | solution.py:124
  25.6 1.3 %collective-permute-start.6 = (f32[64,64]{1,0:T(8,128)S(1)}, f32[64,64]{1,0:T(8,128)S(1)}, u32[]{:S(2)}, u32[]{:S(2)}) collective-permute-start(f32[64,64]{1,0:T(8,128)S(1)} %shrink.2.refs_1_), channel_id=1, source_target_pairs={{0,1},{1,0},{2,3},{3,2},{4,5},{5,4},{6,7},{7,6},{8,9},{9,8},{10,11... | collective-permute-start | bytes 49160 | tf_op jit(solution)/shard_map/ppermute | solution.py:124
  27.3 6.4 %collective-permute-start.9 = (bf16[8,64,256]{2,1,0:T(8,128)(2,1)S(1)}, bf16[8,64,256]{2,1,0:T(8,128)(2,1)S(1)}, u32[]{:S(2)}, u32[]{:S(2)}) collective-permute-start(bf16[8,64,256]{2,1,0:T(8,128)(2,1)S(1)} %expand.5), channel_id=1, source_target_pairs={{0,2},{1,5},{2,0},{3,7},{4,6},{5,1},{6,4},{7,3},{8,10},{9,13},{10,... | collective-permute-start | bytes 786440 | tf_op jit(solution)/shard_map/ppermute | solution.py:124
  29.4 1.3 %collective-permute-start.12 = (f32[64,64]{1,0:T(8,128)S(1)}, f32[64,64]{1,0:T(8,128)S(1)}, u32[]{:S(2)}, u32[]{:S(2)}) collective-permute-start(f32[64,64]{1,0:T(8,128)S(1)} %shrink.3.refs_1_), channel_id=1, source_target_pairs={{0,1},{1,0},{2,3},{3,2},{4,5},{5,4},{6,7},{7,6},{8,9},{9,8},{10,11... | collective-permute-start | bytes 49160 | tf_op jit(solution)/shard_map/ppermute | solution.py:124
  31.0 6.4 %collective-permute-start.13 = (bf16[8,64,256]{2,1,0:T(8,128)(2,1)S(1)}, bf16[8,64,256]{2,1,0:T(8,128)(2,1)S(1)}, u32[]{:S(2)}, u32[]{:S(2)}) collective-permute-start(bf16[8,64,256]{2,1,0:T(8,128)(2,1)S(1)} %expand.7), channel_id=1, source_target_pairs={{0,4},{1,3},{2,6},{3,1},{4,0},{5,7},{6,2},{7,5},{8,12},{9,11},{10,... | collective-permute-start | bytes 786440 | tf_op jit(solution)/shard_map/ppermute | solution.py:124
  33.8 5.1 %collective-permute-start.10 = (bf16[4,64,256]{2,1,0:T(8,128)(2,1)S(1)}, bf16[4,64,256]{2,1,0:T(8,128)(2,1)S(1)}, u32[]{:S(2)}, u32[]{:S(2)}) collective-permute-start(bf16[4,64,256]{2,1,0:T(8,128)(2,1)S(1)} %slice.65), channel_id=1, source_target_pairs={{0,4},{1,3},{2,6},{3,1},{4,0},{5,7},{6,2},{7,5},{8,12},{9,11},{10,... | collective-permute-start | bytes 393224 | tf_op jit(solution)/shard_map/ppermute | solution.py:124
  37.5 5.0 %collective-permute-start.14 = (bf16[4,64,256]{2,1,0:T(8,128)(2,1)S(1)}, bf16[4,64,256]{2,1,0:T(8,128)(2,1)S(1)}, u32[]{:S(2)}, u32[]{:S(2)}) collective-permute-start(bf16[4,64,256]{2,1,0:T(8,128)(2,1)S(1)} %slice.64), channel_id=1, source_target_pairs={{0,2},{1,5},{2,0},{3,7},{4,6},{5,1},{6,4},{7,3},{8,10},{9,13},{10,... | collective-permute-start | bytes 393224 | tf_op jit(solution)/shard_map/ppermute | solution.py:124
  42.6 6.6 %collective-permute-start.17 = (bf16[1,128,256]{2,1,0:T(8,128)(2,1)S(1)}, bf16[1,128,256]{2,1,0:T(8,128)(2,1)S(1)}, u32[]{:S(2)}, u32[]{:S(2)}) collective-permute-start(bf16[1,128,256]{2,1,0:T(8,128)(2,1)S(1)} %get-tuple-element.49), channel_id=1, source_target_pairs={{0,24},{1,25},{2,26},{3,27},{4,28},{5,29},{6,30},{7,31},{8,16},{9,... | collective-permute-start | bytes 196616 | tf_op jit(solution)/shard_map/ppermute | solution.py:124
  45.1 5.4 %collective-permute-start.16 = (bf16[1,128,256]{2,1,0:T(8,128)(2,1)S(1)}, bf16[1,128,256]{2,1,0:T(8,128)(2,1)S(1)}, u32[]{:S(2)}, u32[]{:S(2)}) collective-permute-start(bf16[1,128,256]{2,1,0:T(8,128)(2,1)S(1)} %get-tuple-element.50), channel_id=1, source_target_pairs={{0,8},{1,9},{2,10},{3,11},{4,12},{5,13},{6,14},{7,15},{8,0},{9,1},... | collective-permute-start | bytes 196616 | tf_op jit(solution)/shard_map/ppermute | solution.py:124
  45.2 5.3 %collective-permute-start.15 = (bf16[1,128,256]{2,1,0:T(8,128)(2,1)S(1)}, bf16[1,128,256]{2,1,0:T(8,128)(2,1)S(1)}, u32[]{:S(2)}, u32[]{:S(2)}) collective-permute-start(bf16[1,128,256]{2,1,0:T(8,128)(2,1)S(1)} %get-tuple-element.51), channel_id=1, source_target_pairs={{0,16},{1,17},{2,18},{3,19},{4,20},{5,21},{6,22},{7,23},{8,24},{9,... | collective-permute-start | bytes 196616 | tf_op jit(solution)/shard_map/ppermute | solution.py:124
